TPU v7x, 256 devices: a whole 4x4x8 slice. The times are simulated.
256 devices in a mesh: dp: 8 (over y, z_hi), row: 4 (over z_lo), col: 8 (over x, core).
Axes of the slice: x: 4, y: 4, z: 8 (z_hi: 2, z_lo: 4; z = z_hi * 4 + z_lo), core: 2. Of those that a mesh axis runs over, the one named last changes fastest.
Arguments:
- pre_act: bfloat16 [4096, 24576], P(('dp', 'row'), 'col'), may hold values from -6 to 6
- grad_out: bfloat16 [4096, 6144], P(('dp', 'col'), 'row'), may hold values from -6 to 6
- down_weight: bfloat16 [24576, 6144], P('col', 'row'), may hold values from -0.078125 to 0.078125
Outputs:
- grad_pre: bfloat16 [4096, 24576], P(('dp', 'row'), 'col')
- grad_down: float32 [24576, 6144], P(('col', 'dp'), 'row')
All inputs are finite; a program needn't handle non-finite values.
Results may differ from a plain program's by a relative error of at most 0.0027.
Values may be sent and summed in bfloat16 or wider, within the bound.
No kernel may reach another device: no remote copies, remote signals or barrier semaphores. Data moves between devices by JAX's collectives and lax.ppermute only.
A program may use at most 128 MiB of HBM per device.

v0:
```python
import math

import jax
import jax.numpy as jnp
from jax import lax
from jax.sharding import PartitionSpec as P

root_two_pi = math.sqrt(2.0 / math.pi)
gelu_coeff = 0.044715


def gelu_parts(pre_values):
    cubic_term = gelu_coeff * pre_values * pre_values * pre_values
    inner_arg = root_two_pi * (pre_values + cubic_term)
    tangent = jnp.tanh(inner_arg)
    gelu_value = 0.5 * pre_values * (1.0 + tangent)
    gelu_slope = 0.5 * (1.0 + tangent) + 0.5 * pre_values * (
        1.0 - tangent * tangent
    ) * root_two_pi * (1.0 + 3.0 * gelu_coeff * pre_values * pre_values)
    return (gelu_value, gelu_slope)


def on_device(pre_act, grad_out, down_weight):
    block_rows = pre_act.shape[0]
    replica_rows = block_rows * lax.axis_size("row")
    total_tokens = replica_rows * lax.axis_size("dp")
    grad_scale = 1.0 / math.sqrt(total_tokens)
    everyone = lax.all_gather(grad_out, ("dp", "col"), axis=0, tiled=True)
    replica = lax.dynamic_slice_in_dim(
        everyone, lax.axis_index("dp") * replica_rows, replica_rows, 0
    )
    grad_act = lax.psum_scatter(
        lax.dot_general(
            replica, down_weight, (((1,), (1,)), ((), ())), preferred_element_type=jnp.float32
        ),
        "row",
        scatter_dimension=0,
        tiled=True,
    )
    gelu_value, gelu_slope = gelu_parts(pre_act.astype(jnp.float32))
    activation = gelu_value.astype(jnp.bfloat16)
    grad_pre = (grad_act * gelu_slope).astype(jnp.bfloat16)
    replica_act = lax.all_gather(activation, "row", axis=0, tiled=True)
    spread = lax.all_to_all(replica_act, "dp", split_axis=1, concat_axis=0, tiled=True)
    summed = lax.dot_general(
        spread, everyone, (((0,), (0,)), ((), ())), preferred_element_type=jnp.float32
    )
    grad_down = summed * grad_scale
    return (grad_pre, grad_down)


def solution(mesh):
    placed = (P(("dp", "row"), "col"), P(("dp", "col"), "row"), P("col", "row"))
    return jax.shard_map(
        on_device,
        mesh=mesh,
        in_specs=placed,
        out_specs=(P(("dp", "row"), "col"), P(("col", "dp"), "row")),
        check_vma=False,
    )
```

profile of v0, /device:TPU:2, one launch (start us, length us, event | category | flops | bytes accessed | tf_op | source)
XLA Modules:
  0.0 440.6 jit_solution(4377598673642294947)
XLA Ops:
  7.2 0.0 all-gather.3.cloned.1.call-start
  7.2 0.7 all-gather.3.cloned.1.call-update
  7.9 0.0 reduce-scatter.2.cloned.1.call-start
  7.9 139.7 %all-gather.3.cloned.1.call-done = bf16[4096,1536]{1,0:T(8,128)(2,1)} async-done(((bf16[64,1536]{1,0:T(8,128)(2,1)}), bf16[4096,1536]{1,0:T(8,128)(2,1)}) %all-gather.3.cloned.1.call-update) | async-done | bytes 12582928 | tf_op jit(solution)/shard_map/all_gather | solution.py:28
  147.6 9.8 %fusion.11 = f32[512,3072]{1,0:T(8,128)} fusion(bf16[3072,1536]{1,0:T(8,128)(2,1)} %param.5, bf16[4096,1536]{1,0:T(8,128)(2,1)} %all-gather.3.cloned.1.call-done, s32[]{:T(128)S(6)} %select_n.3), kind=kOutput, calls=%fused_computation.20 | convolution fusion | flops 4831838208 | bytes 17301508 | tf_op jit(solution)/shard_map/dot_general | solution.py:33
  157.4 0.0 copy-start
  157.4 0.0 reduce-scatter.2.cloned.1.call-update
  157.4 0.0 all-gather.5.cloned.1.call-start
  157.5 110.6 %reduce-scatter.2.cloned.1.call-done = f32[128,3072]{1,0:T(8,128)} async-done(((f32[512,3072]{1,0:T(8,128)}), f32[128,3072]{1,0:T(8,128)}) %reduce-scatter.2.cloned.1.call-update) | async-done | bytes 1572880 | tf_op jit(solution)/shard_map/reduce_scatter | solution.py:32
  268.1 0.0 copy-done
  268.1 3.7 fusion.7
  271.8 0.0 all-gather.5.cloned.1.call-update
  271.8 67.8 %all-gather.5.cloned.1.call-done = bf16[512,3072]{1,0:T(8,128)(2,1)} async-done(((bf16[128,3072]{1,0:T(8,128)(2,1)}), bf16[512,3072]{1,0:T(8,128)(2,1)}) %all-gather.5.cloned.1.call-update) | async-done | bytes 3145744 | tf_op jit(solution)/shard_map/all_gather | solution.py:43
  339.6 2.2 copy.8
  341.8 82.6 %all_to_all.19 = bf16[512,8,384]{2,0,1:T(8,128)(2,1)S(1)} all-to-all(bf16[512,8,384]{2,0,1:T(8,128)(2,1)S(1)} %bitcast.10), channel_id=1, replica_groups=mesh['dp'=8,'row'=4,'col'=8] {'dp'}, dimensions={1} | all-to-all | bytes 6291456 | tf_op jit(solution)/shard_map/all_to_all | solution.py:44
  424.4 9.6 %convolution_multiply_fusion = f32[384,1536]{1,0:T(8,128)} fusion(bf16[4096,384]{1,0:T(8,128)(2,1)S(1)} %bitcast.12, bf16[4096,1536]{1,0:T(8,128)(2,1)} %all-gather.3.cloned.1.call-done), kind=kOutput, calls=%fused_computation.8 | convolution fusion | flops 4832428032 | bytes 18087936 | tf_op jit(solution)/shard_map/dot_general | solution.py:45
Async XLA Ops:
  7.2 140.5 %all-gather.3.cloned.1.call-start = ((), (), s32[]{:S(2)}) async-start(), calls=%async_computation.2 | async-start | bytes 12779520 | tf_op jit(solution)/shard_map/all_gather | solution.py:28
  7.9 260.2 %reduce-scatter.2.cloned.1.call-start = ((), (), s32[]{:S(2)}) async-start(), calls=%async_computation.3 | async-start | bytes 7864320 | tf_op jit(solution)/shard_map/reduce_scatter | solution.py:32
  157.4 110.7 %copy-start = (bf16[128,3072]{1,0:T(8,128)(2,1)S(1)}, bf16[128,3072]{1,0:T(8,128)(2,1)}, u32[]{:S(2)}) copy-start(bf16[128,3072]{1,0:T(8,128)(2,1)} %param.3) | copy-start | bytes 2359300
  157.4 182.1 %all-gather.5.cloned.1.call-start = ((), (), s32[]{:S(2)}) async-start(), calls=%async_computation.4 | async-start | bytes 3932160 | tf_op jit(solution)/shard_map/all_gather | solution.py:43
Sparse Core Ops, SparseCore 0:
  11.6 135.9 all-gather.2
  157.5 110.5 reduce-scatter.1
  271.9 67.6 all-gather.4
where the time goes:
time: 441 us
  waiting for transfers between devices  319 us (72%)
  blocking collectives  82.6 us (19%)
  matrix products  19.4 us (4%)
  between operations  13.8 us (3%)
    all_gather x1, waiting for transfers between devices, on_device(): everyone = lax.all_gather(grad_out, ('dp', 'col'), axis=0, tiled=True)  140 us
    reduce_scatter x1, waiting for transfers between devices, on_device(): lax.psum_scatter(lax.dot_general(replica, down_weight, (((1,), (1,)), (()...  111 us
    all_to_all x1, blocking collectives, on_device(): lax.all_to_all(replica_act, 'dp', split_axis=1, concat_axis=0, tiled=True)  82.6 us
    all_gather x1, waiting for transfers between devices, on_device(): replica_act = lax.all_gather(activation, 'row', axis=0, tiled=True)  67.8 us
    dot_general x1, matrix products, on_device(): lax.dot_general(replica, down_weight, (((1,), (1,)), ((), ())), preferred...  9.76 us
    dot_general x1, matrix products, on_device(): lax.dot_general(spread, everyone, (((0,), (0,)), ((), ())), preferred_ele...  9.63 us
  transfers between devices with their start and end apart: 3, of which 3 were waited for; matrix products, arithmetic and copies ran while one was open for 0% of the time, Pallas kernels for 0%

commit v1 on v0

v1 whole, which is shorter than its diff:
```python
import math

import jax
import jax.numpy as jnp
from jax import lax
from jax.sharding import Mesh
from jax.sharding import PartitionSpec as P

root_two_pi = math.sqrt(2.0 / math.pi)
gelu_coeff = 0.044715
Z = ("zh", "zl")


def gelu_parts(pre_values):
    cubic_term = gelu_coeff * pre_values * pre_values * pre_values
    inner_arg = root_two_pi * (pre_values + cubic_term)
    tangent = jnp.tanh(inner_arg)
    gelu_value = 0.5 * pre_values * (1.0 + tangent)
    gelu_slope = 0.5 * (1.0 + tangent) + 0.5 * pre_values * (
        1.0 - tangent * tangent
    ) * root_two_pi * (1.0 + 3.0 * gelu_coeff * pre_values * pre_values)
    return (gelu_value, gelu_slope)


def shift(v, axis, step):
    n = lax.axis_size(axis)
    return lax.ppermute(v, axis, [(i, (i + step) % n) for i in range(n)])


def along_z(v, step, senders):
    pairs = [(4 * h + l, (4 * h + l + step) % 8) for h in range(2) for l in senders]
    return lax.ppermute(v, Z, pairs)


def at(v, i):
    return lax.dynamic_index_in_dim(v, i, 0, keepdims=False)


def after(v, *first):
    return lax.optimization_barrier((v, *first))[0]


def pack(v):
    top = jnp.max(jnp.abs(v), axis=1, keepdims=True)
    e = jnp.clip(jnp.floor(jnp.log2(jnp.maximum(top, 1e-30))), -100.0, 100.0)
    body = (v * jnp.exp2(13.0 - e)).astype(jnp.float16)
    tail = jnp.broadcast_to(e, (v.shape[0], 128)).astype(jnp.float16)
    return jnp.concatenate([body, tail], axis=1)


def unpack(w):
    n = w.shape[1] - 128
    e = w[:, n : n + 1].astype(jnp.float32)
    return w[:, :n].astype(jnp.float32) * jnp.exp2(e - 13.0)


def on_device(pre_act, grad_out, down_weight):
    y, zh, zl, x, c = (lax.axis_index(a) for a in ("y", "zh", "zl", "x", "core"))
    j = zh * 4 + zl
    tokens, hidden = pre_act.shape
    half, feats = grad_out.shape
    block = hidden // 8
    grad_scale = 1.0 / math.sqrt(tokens * 32)

    g = grad_out
    p = shift(g, "zh", 1)
    g_all = lax.all_gather(g, ("x", "y"))
    p_all = lax.all_gather(p, ("x", "y"))
    g_from = [g] + [shift(g, "x", t) for t in (1, 2, 3)]

    gelu_value, gelu_slope = gelu_parts(pre_act.astype(jnp.float32))
    act = gelu_value.astype(jnp.bfloat16).reshape(tokens, 4, 2, block).transpose(1, 2, 0, 3)
    act = jnp.where(zh == 1, act[:, ::-1], act)
    halves = act.reshape(4, 2, 2, half, block)
    act = jnp.where(c == 1, halves[:, :, ::-1], halves)
    pieces_out = [at(act, (y + s) % 4) for s in range(4)]
    pieces = [shift(v, "y", s) if s else v for s, v in enumerate(pieces_out)]
    own, cross = (
        jnp.stack([lax.select_n((y - k) % 4, *[v[i] for v in pieces]) for k in range(4)], axis=1)
        for i in range(2)
    )

    ga = after(jnp.stack(g_from), *pieces_out)
    ga_o = shift(ga, "core", 1)
    q = jnp.where(jnp.where(zl == 0, x == 3, x == 0), p, jnp.zeros_like(p))
    for t in (1, 2, 3):
        pairs = [(3, (3 + t) % 4), (12, 12 + t)]
        q = q + lax.ppermute(p, ("zl", "x"), pairs)
    q_o = shift(q, "core", 1)
    mine = jnp.stack([ga, ga_o], axis=1)
    beyond = jnp.stack([q, q_o])

    mine = after(mine, own, cross)

    def partial(k):
        v = at(mine, (x - zl - k) % 4)
        if k == 1:
            v = jnp.where(zl == 3, beyond, v)
        if k == -1:
            v = jnp.where(zl == 0, beyond, v)
        v = jnp.where(c == 1, v[::-1], v).reshape(tokens, feats)
        return lax.dot_general(
            v, down_weight, (((1,), (1,)), ((), ())), preferred_element_type=jnp.float32
        )

    r1 = along_z(jnp.where(zl < 2, own, cross), 1, range(4))
    l1 = along_z(jnp.where(zl < 2, cross, own), -1, range(4))
    far = pack(partial(2))
    far_up = along_z(far, 1, (0, 1))
    far_down = along_z(far, -1, (2, 3))
    r2 = along_z(jnp.where(zl == 2, own, r1), 1, range(4))
    l2 = along_z(jnp.where(zl == 1, own, l1), -1, range(4))
    from_below = along_z(pack(partial(1) + unpack(far_up)), 1, range(4))
    from_above = along_z(pack(partial(-1) + unpack(far_down)), -1, range(4))
    r3 = along_z(after(jnp.where(zl == 2, r1, r2), g_all), 1, (0, 1, 2))
    l3 = along_z(after(jnp.where(zl == 1, l1, l2), g_all), -1, (3, 2, 1))
    r4 = along_z(jnp.where(zl == 2, r2, r3), 1, (1, 2))
    l4 = along_z(jnp.where(zl == 1, l2, l3), -1, (2, 1))
    r5 = along_z(r3, 1, (2,))
    l5 = along_z(l3, -1, (1,))
    r6 = along_z(after(r4, p_all), 1, (2,))
    l6 = along_z(after(l4, p_all), -1, (1,))

    mid = partial(0)
    grad_act = mid + unpack(from_below) + unpack(from_above)
    grad_pre = (grad_act * gelu_slope).astype(jnp.bfloat16)

    g_all = after(g_all, r3, l3).reshape(4, 4, half, feats)
    g_both = (g_all, shift(g_all, "core", 1))
    p_all = after(p_all, r5, l5).reshape(4, 4, half, feats)
    p_both = (p_all, shift(p_all, "core", 1))

    def product(unit, both, source):
        return sum(
            lax.dot_general(
                unit[o].reshape(4 * half, block),
                at(both[o], source).reshape(4 * half, feats),
                (((0,), (0,)), ((), ())),
                preferred_element_type=jnp.float32,
            )
            for o in range(2)
        )

    def choose(*units):
        return lax.select_n(zl, *units)

    r1, r2, r3, r4, r5, l1, l2, l3, l4, l5 = lax.optimization_barrier(
        (r1, r2, r3, r4, r5, l1, l2, l3, l4, l5)
    )
    summed = product(own, g_both, zl)
    summed += product(choose(l4, r1, r1, r2), g_both, (zl + 3) % 4)
    summed += product(choose(l2, l1, l1, r4), g_both, (zl + 1) % 4)
    summed += product(choose(l3, l2, r2, r3), g_both, (zl + 2) % 4)
    low = zl < 2
    summed += product(choose(r1, r2, l2, l1), p_both, jnp.where(low, 3, 0))
    summed += product(choose(r2, r3, l3, l2), p_both, jnp.where(low, 2, 1))
    summed += product(choose(l5, l3, r3, r5), p_both, jnp.where(low, 0, 3))
    summed += product(choose(l6, l4, r4, r6), p_both, jnp.where(low, 1, 2))
    return (grad_pre, summed * grad_scale)


def solution(mesh):
    axes = ("y", "zh", "zl", "x", "core")
    fine = Mesh(mesh.devices.reshape(4, 2, 4, 4, 2), axes)
    dp, row, col = ("y", "zh"), "zl", ("x", "core")
    return jax.shard_map(
        on_device,
        mesh=fine,
        in_specs=(P((*dp, row), col), P((*dp, *col), row), P(col, row)),
        out_specs=(P((*dp, row), col), P((*col, *dp), row)),
        check_vma=False,
    )
```

time: 441 us -> 198 us (0.45)
  the two profiles are of different devices: /device:TPU:2 before, /device:TPU:1 now
where the time goes in v1:
time: 198 us; the launch traced here: 194 us
  starting transfers between devices  63.8 us (32%)
  matrix products  49 us (25%)
  waiting for transfers between devices  41.9 us (21%)
  other arithmetic  16.7 us (8%)
  between operations  14.8 us (7%)
  local copies, waits for them, and re-layouts  8.1 us (4%)
    ppermute x16, waiting for transfers between devices, along_z(): return lax.ppermute(v, Z, pairs)  35.5 us
    ppermute x16, starting transfers between devices, along_z(): return lax.ppermute(v, Z, pairs)  31.8 us
    ppermute x11, starting transfers between devices, shift(): return lax.ppermute(v, axis, [(i, (i + step) % n) for i in range(n)])  29.3 us
    dot_general x4, matrix products, partial(): lax.dot_general(v, down_weight, (((1,), (1,)), ((), ())), preferred_eleme...  25.3 us
    dot_general x16, matrix products, product(): lax.dot_general(unit[o].reshape(4 * half, block), at(both[o], source).res...  23.7 us
    unnamed x40, local copies, waits for them, and re-layouts  4.23 us
  transfers between devices with their start and end apart: 32, of which 5 were waited for; matrix products, arithmetic and copies ran while one was open for 32% of the time, Pallas kernels for 0%

profile of v1, /device:TPU:1, one launch (start us, length us, event | category | flops | bytes accessed | tf_op | source)
XLA Modules:
  0.0 194.3 jit_solution(16925719757928658572)
XLA Ops:
  7.9 3.4 %collective-permute-start.2 = (bf16[64,1536]{1,0:T(8,128)(2,1)}, bf16[64,1536]{1,0:T(8,128)(2,1)S(1)}, u32[]{:S(2)}, u32[]{:S(2)}) collective-permute-start(bf16[64,1536]{1,0:T(8,128)(2,1)} %param.4), channel_id=1, source_target_pairs={{0,6},{2,0},{4,2},{6,4},{1,7},{3,1},{5,3},{7,5},{8,14},{10,8},{12,... | collective-permute-start | bytes 589832 | tf_op jit(solution)/shard_map/ppermute | solution.py:27
  12.5 6.9 %collective-permute-start.7 = (bf16[64,1536]{1,0:T(8,128)(2,1)}, bf16[64,1536]{1,0:T(8,128)(2,1)S(1)}, u32[]{:S(2)}, u32[]{:S(2)}) collective-permute-start(bf16[64,1536]{1,0:T(8,128)(2,1)} %param.4), channel_id=1, source_target_pairs={{0,32},{32,0},{1,33},{33,1},{2,34},{34,2},{3,35},{35,3},{4,36},{36... | collective-permute-start | bytes 589832 | tf_op jit(solution)/shard_map/ppermute | solution.py:27
  27.5 2.7 %collective-permute-start.3 = (bf16[4,64,1536]{2,1,0:T(8,128)(2,1)S(1)}, bf16[4,64,1536]{2,1,0:T(8,128)(2,1)}, u32[]{:S(2)}, u32[]{:S(2)}) collective-permute-start(bf16[4,64,1536]{2,1,0:T(8,128)(2,1)S(1)} %pad_maximum_fusion.4), channel_id=1, source_target_pairs={{0,1},{1,0},{2,3},{3,2},{4,5},{5,4},{6,7},{7,6},{8,9},{9,8},{10,11... | collective-permute-start | bytes 2359304 | tf_op jit(solution)/shard_map/ppermute | solution.py:27
  32.9 2.5 %collective-permute-done.5 = bf16[2,2,64,384]{3,2,1,0:T(8,128)(2,1)S(1)} collective-permute-done((bf16[2,2,64,384]{3,2,1,0:T(8,128)(2,1)S(1)}, bf16[2,2,64,384]{3,2,1,0:T(8,128)(2,1)S(1)}, u32[]{:S(2)}, u32[]{:S(2)}) %collective-permute-start.5) | collective-permute-done | bytes 196640 | tf_op jit(solution)/shard_map/ppermute | solution.py:27
  35.8 3.0 %collective-permute-start.19 = (bf16[2,4,64,384]{3,2,1,0:T(8,128)(2,1)S(1)}, bf16[2,4,64,384]{3,2,1,0:T(8,128)(2,1)S(1)}, u32[]{:S(2)}, u32[]{:S(2)}) collective-permute-start(bf16[2,4,64,384]{3,2,1,0:T(8,128)(2,1)S(1)} %get-tuple-element.59), channel_id=1, source_target_pairs={{0,56},{8,0},{16,8},{24,16},{32,24},{40,32},{48,40},{56,48},{1,57}... | collective-permute-start | bytes 1179656 | tf_op jit(solution)/shard_map/ppermute | solution.py:32
  38.9 3.2 %collective-permute-done.8 = bf16[64,1536]{1,0:T(8,128)(2,1)S(1)} collective-permute-done((bf16[64,1536]{1,0:T(8,128)(2,1)S(1)}, bf16[64,1536]{1,0:T(8,128)(2,1)S(1)}, u32[]{:S(2)}, u32[]{:S(2)}) %collective-permute-start.8) | collective-permute-done | bytes 196640 | tf_op jit(solution)/shard_map/ppermute | solution.py:88
  42.7 3.5 %collective-permute-start.11 = (bf16[64,1536]{1,0:T(8,128)(2,1)}, bf16[64,1536]{1,0:T(8,128)(2,1)}, u32[]{:S(2)}, u32[]{:S(2)}) collective-permute-start(bf16[64,1536]{1,0:T(8,128)(2,1)} %add_add_fusion), channel_id=1, source_target_pairs={{0,1},{1,0},{2,3},{3,2},{4,5},{5,4},{6,7},{7,6},{8,9},{9,8},{10,11... | collective-permute-start | bytes 589832 | tf_op jit(solution)/shard_map/ppermute | solution.py:27
  46.2 3.0 %collective-permute-done.16 = bf16[2,4,64,384]{3,2,1,0:T(8,128)(2,1)S(1)} collective-permute-done((bf16[2,4,64,384]{3,2,1,0:T(8,128)(2,1)S(1)}, bf16[2,4,64,384]{3,2,1,0:T(8,128)(2,1)S(1)}, u32[]{:S(2)}, u32[]{:S(2)}) %collective-permute-start.16) | collective-permute-done | bytes 393248 | tf_op jit(solution)/shard_map/ppermute | solution.py:32
  50.4 2.7 %collective-permute-start.20 = (bf16[2,4,64,384]{3,2,1,0:T(8,128)(2,1)}, bf16[2,4,64,384]{3,2,1,0:T(8,128)(2,1)}, u32[]{:S(2)}, u32[]{:S(2)}) collective-permute-start(bf16[2,4,64,384]{3,2,1,0:T(8,128)(2,1)} %get-tuple-element.64), channel_id=1, source_target_pairs={{0,56},{8,0},{16,8},{24,16},{32,24},{40,32},{48,40},{56,48},{1,57}... | collective-permute-start | bytes 1179656 | tf_op jit(solution)/shard_map/ppermute | solution.py:32
  55.2 8.1 %abs_reduce_fusion.2 = (f32[128]{0:T(128)S(1)}, f32[128,3072]{1,0:T(8,128)}) fusion(bf16[128,1536]{1,0:T(8,128)(2,1)S(1)} %bitcast.305, bf16[3072,1536]{1,0:T(8,128)(2,1)} %param.5), kind=kOutput, calls=%fused_computation.58 | convolution fusion | flops 1208745856 | bytes 11403776 | tf_op jit(solution)/shard_map/dot_general | solution.py:102
  63.4 1.9 copy.36
  69.2 1.8 broadcast_select_fusion.1
  71.1 6.2 %abs_reduce_fusion = (f32[128]{0:T(128)S(1)}, f32[128,3072]{0,1:T(8,128)S(1)}) fusion(f32[128]{0:T(128)S(1)} %fusion.89, f16[128,3200]{0,1:T(8,128)(2,1)S(1)} %collective-permute-done.14, bf16[128,1536]{1,0:T(8,128)(2,1)S(1)} %bitcast.304, bf16[3072,1536]{1,0:T(8,128)(2,1)} %param.5), kind=kOutput, calls=%fused_computation.52 | convolution fusion | flops 1209925504 | bytes 12190720 | tf_op jit(solution)/shard_map/dot_general | solution.py:102
  78.8 10.3 %collective-permute-start.15 = (f16[128,3200]{0,1:T(8,128)(2,1)}, f16[128,3200]{0,1:T(8,128)(2,1)}, u32[]{:S(2)}, u32[]{:S(2)}) collective-permute-start(f16[128,3200]{0,1:T(8,128)(2,1)} %pad_maximum_fusion.3), channel_id=1, source_target_pairs={{0,56},{8,0},{16,8},{24,16},{32,24},{40,32},{48,40},{56,48},{1,57}... | collective-permute-start | bytes 2457608 | tf_op jit(solution)/shard_map/ppermute | solution.py:32
  89.2 2.6 %abs_reduce_fusion.1 = (f32[128]{0:T(128)S(1)}, f32[128,3072]{0,1:T(8,128)S(1)}) fusion(f32[128]{0:T(128)S(1)} %fusion.97, f16[128,3200]{0,1:T(8,128)(2,1)S(1)} %collective-permute-done.12, bf16[128,1536]{1,0:T(8,128)(2,1)S(1)} %bitcast.303, bf16[3072,1536]{1,0:T(8,128)(2,1)S(1)} %bitcast.299), kind=kOutput, calls=%fused_computation.55 | convolution fusion | flops 1209925504 | bytes 12190720 | tf_op jit(solution)/shard_map/dot_general | solution.py:102
  94.9 3.9 %collective-permute-start.18 = (bf16[2,4,64,384]{3,2,1,0:T(8,128)(2,1)S(1)}, bf16[2,4,64,384]{3,2,1,0:T(8,128)(2,1)S(1)}, u32[]{:S(2)}, u32[]{:S(2)}) collective-permute-start(bf16[2,4,64,384]{3,2,1,0:T(8,128)(2,1)S(1)} %broadcast_select_fusion.6), channel_id=1, source_target_pairs={{0,8},{8,16},{16,24},{32,40},{40,48},{48,56},{1,9},{9,17},{17,25},... | collective-permute-start | bytes 1179656 | tf_op jit(solution)/shard_map/ppermute | solution.py:32
  101.0 16.7 %collective-permute-done.18 = bf16[2,4,64,384]{3,2,1,0:T(8,128)(2,1)S(1)} collective-permute-done((bf16[2,4,64,384]{3,2,1,0:T(8,128)(2,1)S(1)}, bf16[2,4,64,384]{3,2,1,0:T(8,128)(2,1)S(1)}, u32[]{:S(2)}, u32[]{:S(2)}) %collective-permute-start.18) | collective-permute-done | bytes 393248 | tf_op jit(solution)/shard_map/ppermute | solution.py:32
  121.2 4.4 %collective-permute-start.22 = (bf16[4,4,64,1536]{3,2,1,0:T(8,128)(2,1)}, bf16[4,4,64,1536]{3,2,1,0:T(8,128)(2,1)}, u32[]{:S(2)}, u32[]{:S(2)}) collective-permute-start(bf16[4,4,64,1536]{3,2,1,0:T(8,128)(2,1)} %bitcast.49), channel_id=1, source_target_pairs={{0,1},{1,0},{2,3},{3,2},{4,5},{5,4},{6,7},{7,6},{8,9},{9,8},{10,11... | collective-permute-start | bytes 9437192 | tf_op jit(solution)/shard_map/ppermute | solution.py:27
  129.0 15.8 %collective-permute-done.26 = bf16[2,4,64,384]{3,2,1,0:T(8,128)(2,1)} collective-permute-done((bf16[2,4,64,384]{3,2,1,0:T(8,128)(2,1)S(1)}, bf16[2,4,64,384]{3,2,1,0:T(8,128)(2,1)}, u32[]{:S(2)}, u32[]{:S(2)}) %collective-permute-start.26) | collective-permute-done | bytes 393248 | tf_op jit(solution)/shard_map/ppermute | solution.py:32
  144.8 2.8 %collective-permute-start.27 = (bf16[4,4,64,1536]{3,2,1,0:T(8,128)(2,1)}, bf16[4,4,64,1536]{3,2,1,0:T(8,128)(2,1)}, u32[]{:S(2)}, u32[]{:S(2)}) collective-permute-start(bf16[4,4,64,1536]{3,2,1,0:T(8,128)(2,1)} %bitcast.311), channel_id=1, source_target_pairs={{0,1},{1,0},{2,3},{3,2},{4,5},{5,4},{6,7},{7,6},{8,9},{9,8},{10,11... | collective-permute-start | bytes 9437192 | tf_op jit(solution)/shard_map/ppermute | solution.py:27
  150.6 8.3 %fusion.23 = bf16[128,3072]{0,1:T(8,128)(2,1)} fusion(bf16[128,3072]{0,1:T(8,128)(2,1)S(1)} %copy-done.5, f16[128,3200]{0,1:T(8,128)(2,1)} %collective-permute-done.15, f16[128,3200]{0,1:T(8,128)(2,1)} %collective-permute-done.13, f32[128]{0:T(128)S(1)} %fusion.85, f32[128]{0:T(128)S(1)} %fusion.93, bf16[128,1536]{1,0:T(8,128)(2,1)} %bitcast.307, ...), kind=kOutput, calls=%fused_computation.46 | convolution fusion | flops 1218183168 | bytes 12977152 | tf_op jit(solution)/shard_map/dot_general | solution.py:102
  158.9 2.3 %copy.40 = bf16[128,3072]{1,0:T(8,128)(2,1)} copy(bf16[128,3072]{0,1:T(8,128)(2,1)} %fusion.23) | data formatting | bytes 1572864
  163.0 2.0 %select_select_fusion.6 = (bf16[2,4,64,384]{3,2,1,0:T(8,128)(2,1)S(1)}, bf16[2,4,64,384]{3,2,1,0:T(8,128)(2,1)S(1)}, bf16[2,4,64,384]{3,2,1,0:T(8,128)(2,1)S(1)}...) fusion(bf16[2,4,64,384]{3,2,1,0:T(8,128)(2,1)S(1)} %copy-done.3, ...), kind=kLoop, calls=%fused_computation.112 | loop fusion | flops 4128768 | bytes 7471107 | tf_op jit(solution)/shard_map/select_n | solution.py:145
  183.7 3.7 %fusion.15 = f32[384,1536]{1,0:T(8,128)} fusion(f32[384,1536]{1,0:T(8,128)S(1)} %fusion.10, f32[384,1536]{1,0:T(8,128)S(1)} %fusion.9, f32[384,1536]{1,0:T(8,128)S(1)} %fusion.8, f32[384,1536]{1,0:T(8,128)S(1)} %fusion.7, f32[384,1536]{1,0:T(8,128)S(1)} %fusion.6, f32[384,1536]{1,0:T(8,128)S(1)} %fusion.5, f32[384,1536]{1,0:T(8,128)S(1)} %fusion.4, ...), kind=kOutput, calls=%fused_computation.38 | convolution fusion | flops 307298304 | bytes 22216708 | tf_op jit(solution)/shard_map/dot_general | solution.py:135
  (145 shorter events, 57.7 us)
Async XLA Ops:
  7.2 87.7 %all-gather.5.cloned.1.call-start = ((), (), s32[]{:S(2)}) async-start(), calls=%async_computation | async-start | bytes 3342336 | tf_op jit(solution)/shard_map/all_gather | solution.py:67
  7.9 121.1 %all-gather.7.cloned.1.call-start = ((), (), s32[]{:S(2)}) async-start(), calls=%async_computation.1 | async-start | bytes 3342336 | tf_op jit(solution)/shard_map/all_gather | solution.py:68
  7.9 16.4 %collective-permute-start.2 = (bf16[64,1536]{1,0:T(8,128)(2,1)}, bf16[64,1536]{1,0:T(8,128)(2,1)S(1)}, u32[]{:S(2)}, u32[]{:S(2)}) collective-permute-start(bf16[64,1536]{1,0:T(8,128)(2,1)} %param.4), channel_id=1, source_target_pairs={{0,6},{2,0},{4,2},{6,4},{1,7},{3,1},{5,3},{7,5},{8,14},{10,8},{12,... | collective-permute-start | bytes 589832 | tf_op jit(solution)/shard_map/ppermute | solution.py:27
  11.3 14.4 %collective-permute-start.1 = (bf16[64,1536]{1,0:T(8,128)(2,1)}, bf16[64,1536]{1,0:T(8,128)(2,1)S(1)}, u32[]{:S(2)}, u32[]{:S(2)}) collective-permute-start(bf16[64,1536]{1,0:T(8,128)(2,1)} %param.4), channel_id=1, source_target_pairs={{0,4},{2,6},{4,0},{6,2},{1,5},{3,7},{5,1},{7,3},{8,12},{10,14},{12... | collective-permute-start | bytes 589832 | tf_op jit(solution)/shard_map/ppermute | solution.py:27
  11.8 15.5 %collective-permute-start = (bf16[64,1536]{1,0:T(8,128)(2,1)}, bf16[64,1536]{1,0:T(8,128)(2,1)S(1)}, u32[]{:S(2)}, u32[]{:S(2)}) collective-permute-start(bf16[64,1536]{1,0:T(8,128)(2,1)} %param.4), channel_id=1, source_target_pairs={{0,2},{2,4},{4,6},{6,0},{1,3},{3,5},{5,7},{7,1},{8,10},{10,12},{12... | collective-permute-start | bytes 589832 | tf_op jit(solution)/shard_map/ppermute | solution.py:27
  12.5 17.8 %collective-permute-start.7 = (bf16[64,1536]{1,0:T(8,128)(2,1)}, bf16[64,1536]{1,0:T(8,128)(2,1)S(1)}, u32[]{:S(2)}, u32[]{:S(2)}) collective-permute-start(bf16[64,1536]{1,0:T(8,128)(2,1)} %param.4), channel_id=1, source_target_pairs={{0,32},{32,0},{1,33},{33,1},{2,34},{34,2},{3,35},{35,3},{4,36},{36... | collective-permute-start | bytes 589832 | tf_op jit(solution)/shard_map/ppermute | solution.py:27
  27.5 25.6 %collective-permute-start.3 = (bf16[4,64,1536]{2,1,0:T(8,128)(2,1)S(1)}, bf16[4,64,1536]{2,1,0:T(8,128)(2,1)}, u32[]{:S(2)}, u32[]{:S(2)}) collective-permute-start(bf16[4,64,1536]{2,1,0:T(8,128)(2,1)S(1)} %pad_maximum_fusion.4), channel_id=1, source_target_pairs={{0,1},{1,0},{2,3},{3,2},{4,5},{5,4},{6,7},{7,6},{8,9},{9,8},{10,11... | collective-permute-start | bytes 2359304 | tf_op jit(solution)/shard_map/ppermute | solution.py:27
  35.8 10.5 %collective-permute-start.19 = (bf16[2,4,64,384]{3,2,1,0:T(8,128)(2,1)S(1)}, bf16[2,4,64,384]{3,2,1,0:T(8,128)(2,1)S(1)}, u32[]{:S(2)}, u32[]{:S(2)}) collective-permute-start(bf16[2,4,64,384]{3,2,1,0:T(8,128)(2,1)S(1)} %get-tuple-element.59), channel_id=1, source_target_pairs={{0,56},{8,0},{16,8},{24,16},{32,24},{40,32},{48,40},{56,48},{1,57}... | collective-permute-start | bytes 1179656 | tf_op jit(solution)/shard_map/ppermute | solution.py:32
  38.8 10.4 %collective-permute-start.16 = (bf16[2,4,64,384]{3,2,1,0:T(8,128)(2,1)S(1)}, bf16[2,4,64,384]{3,2,1,0:T(8,128)(2,1)S(1)}, u32[]{:S(2)}, u32[]{:S(2)}) collective-permute-start(bf16[2,4,64,384]{3,2,1,0:T(8,128)(2,1)S(1)} %get-tuple-element.60), channel_id=1, source_target_pairs={{0,8},{8,16},{16,24},{24,32},{32,40},{40,48},{48,56},{56,0},{1,9},... | collective-permute-start | bytes 1179656 | tf_op jit(solution)/shard_map/ppermute | solution.py:32
  42.7 25.2 %collective-permute-start.11 = (bf16[64,1536]{1,0:T(8,128)(2,1)}, bf16[64,1536]{1,0:T(8,128)(2,1)}, u32[]{:S(2)}, u32[]{:S(2)}) collective-permute-start(bf16[64,1536]{1,0:T(8,128)(2,1)} %add_add_fusion), channel_id=1, source_target_pairs={{0,1},{1,0},{2,3},{3,2},{4,5},{5,4},{6,7},{7,6},{8,9},{9,8},{10,11... | collective-permute-start | bytes 589832 | tf_op jit(solution)/shard_map/ppermute | solution.py:27
  50.4 18.7 %collective-permute-start.17 = (bf16[2,4,64,384]{3,2,1,0:T(8,128)(2,1)}, bf16[2,4,64,384]{3,2,1,0:T(8,128)(2,1)S(1)}, u32[]{:S(2)}, u32[]{:S(2)}) collective-permute-start(bf16[2,4,64,384]{3,2,1,0:T(8,128)(2,1)} %get-tuple-element.65), channel_id=1, source_target_pairs={{0,8},{8,16},{16,24},{24,32},{32,40},{40,48},{48,56},{56,0},{1,9},... | collective-permute-start | bytes 1179656 | tf_op jit(solution)/shard_map/ppermute | solution.py:32
  50.4 18.8 %collective-permute-start.20 = (bf16[2,4,64,384]{3,2,1,0:T(8,128)(2,1)}, bf16[2,4,64,384]{3,2,1,0:T(8,128)(2,1)}, u32[]{:S(2)}, u32[]{:S(2)}) collective-permute-start(bf16[2,4,64,384]{3,2,1,0:T(8,128)(2,1)} %get-tuple-element.64), channel_id=1, source_target_pairs={{0,56},{8,0},{16,8},{24,16},{32,24},{40,32},{48,40},{56,48},{1,57}... | collective-permute-start | bytes 1179656 | tf_op jit(solution)/shard_map/ppermute | solution.py:32
  66.6 22.6 %collective-permute-start.12 = (f16[128,3200]{0,1:T(8,128)(2,1)S(1)}, f16[128,3200]{0,1:T(8,128)(2,1)S(1)}, u32[]{:S(2)}, u32[]{:S(2)}) collective-permute-start(f16[128,3200]{0,1:T(8,128)(2,1)S(1)} %pad_maximum_fusion.1), channel_id=1, source_target_pairs={{0,8},{8,16},{32,40},{40,48},{1,9},{9,17},{33,41},{41,49},{2,10},{... | collective-permute-start | bytes 2457608 | tf_op jit(solution)/shard_map/ppermute | solution.py:32
  78.8 46.8 %collective-permute-start.15 = (f16[128,3200]{0,1:T(8,128)(2,1)}, f16[128,3200]{0,1:T(8,128)(2,1)}, u32[]{:S(2)}, u32[]{:S(2)}) collective-permute-start(f16[128,3200]{0,1:T(8,128)(2,1)} %pad_maximum_fusion.3), channel_id=1, source_target_pairs={{0,56},{8,0},{16,8},{24,16},{32,24},{40,32},{48,40},{56,48},{1,57}... | collective-permute-start | bytes 2457608 | tf_op jit(solution)/shard_map/ppermute | solution.py:32
  93.3 33.0 %collective-permute-start.13 = (f16[128,3200]{0,1:T(8,128)(2,1)}, f16[128,3200]{0,1:T(8,128)(2,1)}, u32[]{:S(2)}, u32[]{:S(2)}) collective-permute-start(f16[128,3200]{0,1:T(8,128)(2,1)} %pad_maximum_fusion.2), channel_id=1, source_target_pairs={{0,8},{8,16},{16,24},{24,32},{32,40},{40,48},{48,56},{56,0},{1,9},... | collective-permute-start | bytes 2457608 | tf_op jit(solution)/shard_map/ppermute | solution.py:32
  94.9 22.7 %collective-permute-start.18 = (bf16[2,4,64,384]{3,2,1,0:T(8,128)(2,1)S(1)}, bf16[2,4,64,384]{3,2,1,0:T(8,128)(2,1)S(1)}, u32[]{:S(2)}, u32[]{:S(2)}) collective-permute-start(bf16[2,4,64,384]{3,2,1,0:T(8,128)(2,1)S(1)} %broadcast_select_fusion.6), channel_id=1, source_target_pairs={{0,8},{8,16},{16,24},{32,40},{40,48},{48,56},{1,9},{9,17},{17,25},... | collective-permute-start | bytes 1179656 | tf_op jit(solution)/shard_map/ppermute | solution.py:32
  98.8 20.3 %collective-permute-start.21 = (bf16[2,4,64,384]{3,2,1,0:T(8,128)(2,1)}, bf16[2,4,64,384]{3,2,1,0:T(8,128)(2,1)S(1)}, u32[]{:S(2)}, u32[]{:S(2)}) collective-permute-start(bf16[2,4,64,384]{3,2,1,0:T(8,128)(2,1)} %broadcast_select_fusion.1), channel_id=1, source_target_pairs={{24,16},{16,8},{8,0},{56,48},{48,40},{40,32},{25,17},{17,9},{9,1},... | collective-permute-start | bytes 1179656 | tf_op jit(solution)/shard_map/ppermute | solution.py:32
  118.4 29.2 %collective-permute-start.23 = (bf16[2,4,64,384]{3,2,1,0:T(8,128)(2,1)}, bf16[2,4,64,384]{3,2,1,0:T(8,128)(2,1)S(1)}, u32[]{:S(2)}, u32[]{:S(2)}) collective-permute-start(bf16[2,4,64,384]{3,2,1,0:T(8,128)(2,1)} %broadcast_select_fusion.5), channel_id=1, source_target_pairs={{8,16},{16,24},{40,48},{48,56},{9,17},{17,25},{41,49},{49,57},{10,... | collective-permute-start | bytes 1179656 | tf_op jit(solution)/shard_map/ppermute | solution.py:32
  119.9 29.1 %collective-permute-start.25 = (bf16[2,4,64,384]{3,2,1,0:T(8,128)(2,1)}, bf16[2,4,64,384]{3,2,1,0:T(8,128)(2,1)}, u32[]{:S(2)}, u32[]{:S(2)}) collective-permute-start(bf16[2,4,64,384]{3,2,1,0:T(8,128)(2,1)} %broadcast_select_fusion), channel_id=1, source_target_pairs={{16,8},{8,0},{48,40},{40,32},{17,9},{9,1},{49,41},{41,33},{18,10},... | collective-permute-start | bytes 1179656 | tf_op jit(solution)/shard_map/ppermute | solution.py:32
  121.2 50.4 %collective-permute-start.22 = (bf16[4,4,64,1536]{3,2,1,0:T(8,128)(2,1)}, bf16[4,4,64,1536]{3,2,1,0:T(8,128)(2,1)}, u32[]{:S(2)}, u32[]{:S(2)}) collective-permute-start(bf16[4,4,64,1536]{3,2,1,0:T(8,128)(2,1)} %bitcast.49), channel_id=1, source_target_pairs={{0,1},{1,0},{2,3},{3,2},{4,5},{5,4},{6,7},{7,6},{8,9},{9,8},{10,11... | collective-permute-start | bytes 9437192 | tf_op jit(solution)/shard_map/ppermute | solution.py:27
  126.3 18.4 %collective-permute-start.26 = (bf16[2,4,64,384]{3,2,1,0:T(8,128)(2,1)S(1)}, bf16[2,4,64,384]{3,2,1,0:T(8,128)(2,1)}, u32[]{:S(2)}, u32[]{:S(2)}) collective-permute-start(bf16[2,4,64,384]{3,2,1,0:T(8,128)(2,1)S(1)} %collective-permute-done.21), channel_id=1, source_target_pairs={{8,0},{40,32},{9,1},{41,33},{10,2},{42,34},{11,3},{43,35},{12,4},{... | collective-permute-start | bytes 1179656 | tf_op jit(solution)/shard_map/ppermute | solution.py:32
  144.8 31.8 %collective-permute-start.27 = (bf16[4,4,64,1536]{3,2,1,0:T(8,128)(2,1)}, bf16[4,4,64,1536]{3,2,1,0:T(8,128)(2,1)}, u32[]{:S(2)}, u32[]{:S(2)}) collective-permute-start(bf16[4,4,64,1536]{3,2,1,0:T(8,128)(2,1)} %bitcast.311), channel_id=1, source_target_pairs={{0,1},{1,0},{2,3},{3,2},{4,5},{5,4},{6,7},{7,6},{8,9},{9,8},{10,11... | collective-permute-start | bytes 9437192 | tf_op jit(solution)/shard_map/ppermute | solution.py:27
  147.7 15.3 %collective-permute-start.29 = (bf16[2,4,64,384]{3,2,1,0:T(8,128)(2,1)S(1)}, bf16[2,4,64,384]{3,2,1,0:T(8,128)(2,1)}, u32[]{:S(2)}, u32[]{:S(2)}) collective-permute-start(bf16[2,4,64,384]{3,2,1,0:T(8,128)(2,1)S(1)} %collective-permute-done.23), channel_id=1, source_target_pairs={{16,24},{48,56},{17,25},{49,57},{18,26},{50,58},{19,27},{51,59},{2... | collective-permute-start | bytes 1179656 | tf_op jit(solution)/shard_map/ppermute | solution.py:32
  149.1 13.9 %collective-permute-start.28 = (bf16[2,4,64,384]{3,2,1,0:T(8,128)(2,1)}, bf16[2,4,64,384]{3,2,1,0:T(8,128)(2,1)}, u32[]{:S(2)}, u32[]{:S(2)}) collective-permute-start(bf16[2,4,64,384]{3,2,1,0:T(8,128)(2,1)} %collective-permute-done.25), channel_id=1, source_target_pairs={{8,0},{40,32},{9,1},{41,33},{10,2},{42,34},{11,3},{43,35},{12,4},{... | collective-permute-start | bytes 1179656 | tf_op jit(solution)/shard_map/ppermute | solution.py:32
  (27 other events, 262.6 us)
Sparse Core Ops, SparseCore 0:
  10.5 57.1 all-gather.4
  70.2 51.9 all-gather.6

commit v2 on v1

v2 whole, which is shorter than its diff:
```python
import math

import jax
import jax.numpy as jnp
from jax import lax
from jax.sharding import Mesh
from jax.sharding import PartitionSpec as P

root_two_pi = math.sqrt(2.0 / math.pi)
gelu_coeff = 0.044715
Z = ("zh", "zl")


def gelu_parts(pre_values):
    cubic_term = gelu_coeff * pre_values * pre_values * pre_values
    inner_arg = root_two_pi * (pre_values + cubic_term)
    tangent = jnp.tanh(inner_arg)
    gelu_value = 0.5 * pre_values * (1.0 + tangent)
    gelu_slope = 0.5 * (1.0 + tangent) + 0.5 * pre_values * (
        1.0 - tangent * tangent
    ) * root_two_pi * (1.0 + 3.0 * gelu_coeff * pre_values * pre_values)
    return (gelu_value, gelu_slope)


def shift(v, axis, step):
    n = lax.axis_size(axis)
    return lax.ppermute(v, axis, [(i, (i + step) % n) for i in range(n)])


def along_z(v, step, senders):
    pairs = [(4 * h + l, (4 * h + l + step) % 8) for h in range(2) for l in senders]
    return lax.ppermute(v, Z, pairs)


def at(v, i):
    return lax.dynamic_index_in_dim(v, i, 0, keepdims=False)


def after(v, *first):
    return lax.optimization_barrier((v, *first))[0]


def pack(v):
    top = jnp.max(jnp.abs(v), axis=1, keepdims=True)
    e = jnp.clip(jnp.floor(jnp.log2(jnp.maximum(top, 1e-30))), -100.0, 100.0)
    body = (v * jnp.exp2(13.0 - e)).astype(jnp.float16)
    tail = jnp.broadcast_to(e, (v.shape[0], 128)).astype(jnp.float16)
    return jnp.concatenate([body, tail], axis=1)


def unpack(w):
    n = w.shape[1] - 128
    e = w[:, n : n + 1].astype(jnp.float32)
    return w[:, :n].astype(jnp.float32) * jnp.exp2(e - 13.0)


def on_device(pre_act, grad_out, down_weight):
    y, zh, zl, x, c = (lax.axis_index(a) for a in ("y", "zh", "zl", "x", "core"))
    j = zh * 4 + zl
    tokens, hidden = pre_act.shape
    half, feats = grad_out.shape
    block = hidden // 8
    grad_scale = 1.0 / math.sqrt(tokens * 32)

    g = grad_out
    p = shift(g, "zh", 1)
    g_from = [g] + [shift(g, "x", t) for t in (1, 2, 3)]
    all_rows = lax.all_gather(jnp.stack([g, p]), ("x", "y")).reshape(4, 4, 2, half, feats)

    gelu_value, gelu_slope = gelu_parts(pre_act.astype(jnp.float32))
    act, gelu_slope = lax.optimization_barrier((gelu_value.astype(jnp.bfloat16), gelu_slope))
    act = act.reshape(tokens, 4, 2, block).transpose(1, 2, 0, 3)
    act = jnp.where(zh == 1, act[:, ::-1], act)
    halves = act.reshape(4, 2, 2, half, block)
    act = jnp.where(c == 1, halves[:, :, ::-1], halves)
    pieces_out = [at(act, (y + s) % 4) for s in range(4)]
    pieces = [shift(v, "y", s) if s else v for s, v in enumerate(pieces_out)]
    own, cross = (
        jnp.stack([lax.select_n((y - k) % 4, *[v[i] for v in pieces]) for k in range(4)], axis=1)
        for i in range(2)
    )

    ga = after(jnp.stack(g_from), *pieces_out)
    ga_o = shift(ga, "core", 1)
    q = jnp.where(jnp.where(zl == 0, x == 3, x == 0), p, jnp.zeros_like(p))
    for t in (1, 2, 3):
        pairs = [(3, (3 + t) % 4), (12, 12 + t)]
        q = q + lax.ppermute(p, ("zl", "x"), pairs)
    q_o = shift(q, "core", 1)
    mine = after(jnp.stack([ga, ga_o], axis=1), own, cross)
    beyond = jnp.stack([q, q_o])

    rows = [at(mine, (x - zl - k) % 4) for k in (2, 1, -1, 0)]
    rows[1] = jnp.where(zl == 3, beyond, rows[1])
    rows[2] = jnp.where(zl == 0, beyond, rows[2])
    rows = jnp.stack(rows)
    rows = jnp.where(c == 1, rows[:, ::-1], rows).reshape(4 * tokens, feats)
    parts = lax.dot_general(
        rows, down_weight, (((1,), (1,)), ((), ())), preferred_element_type=jnp.float32
    )
    part_far, part_up, part_down, part_own = (
        parts[k * tokens : (k + 1) * tokens] for k in range(4)
    )
    far = pack(part_far)

    r1 = along_z(jnp.where(zl < 2, own, cross), 1, range(4))
    l1 = along_z(jnp.where(zl < 2, cross, own), -1, range(4))
    r2 = along_z(jnp.where(zl == 2, own, r1), 1, range(4))
    l2 = along_z(jnp.where(zl == 1, own, l1), -1, range(4))
    far = after(far, r2, l2)
    far_up = along_z(far, 1, (0, 1))
    far_down = along_z(far, -1, (2, 3))
    r3 = along_z(jnp.where(zl == 2, r1, r2), 1, (0, 1, 2))
    l3 = along_z(jnp.where(zl == 1, l1, l2), -1, (3, 2, 1))
    r4 = along_z(after(jnp.where(zl == 2, r2, r3), far), 1, (1, 2))
    l4 = along_z(after(jnp.where(zl == 1, l2, l3), far), -1, (2, 1))
    r5 = along_z(after(r3, far), 1, (2,))
    l5 = along_z(after(l3, far), -1, (1,))
    near_up = pack(part_up + unpack(after(far_up, r3, l3)))
    near_down = pack(part_down + unpack(after(far_down, r3, l3)))
    from_below = along_z(near_up, 1, range(4))
    from_above = along_z(near_down, -1, range(4))
    r6 = along_z(r4, 1, (2,))
    l6 = along_z(l4, -1, (1,))

    all_rows = after(all_rows, near_up, near_down)
    other_rows = shift(all_rows, "core", 1)
    own, r1, r2, r3, r4, r5, l1, l2, l3, l4, l5 = lax.optimization_barrier(
        (own, r1, r2, r3, r4, r5, l1, l2, l3, l4, l5)
    )

    def choose(*units):
        return lax.select_n(zl, *units)

    none = jnp.zeros_like(own)
    in_group = (
        choose(own, r1, r2, r4),
        choose(l2, own, r1, r3),
        choose(l3, l1, own, r2),
        choose(l4, l2, l1, own),
    )
    from_group = (
        choose(l5, l3, l2, l1),
        choose(none, l4, l3, l2),
        choose(r2, r3, r4, none),
        choose(r1, r2, r3, r5),
    )
    units = [jnp.stack([a, b], axis=2) for a, b in zip(in_group, from_group)]
    last = choose(l6, none, none, r6)
    last = jnp.stack([jnp.zeros_like(last), last], axis=2)

    def product(unit, rows):
        return lax.dot_general(
            unit.reshape(-1, block), rows.reshape(-1, feats), (((0,), (0,)), ((), ())),
            preferred_element_type=jnp.float32,
        )

    summed = 0.0
    for k in (0, 2):
        summed += product(jnp.stack([units[k][0], units[k + 1][0]]), all_rows[k : k + 2])
    for k in (0, 2):
        summed += product(jnp.stack([units[k][1], units[k + 1][1]]), other_rows[k : k + 2])
    low = zl < 2
    summed += product(last[0], at(all_rows, jnp.where(low, 1, 2)))
    summed += product(last[1], at(other_rows, jnp.where(low, 1, 2)))

    grad_act = part_own + unpack(from_below) + unpack(from_above)
    grad_pre = (grad_act * gelu_slope).astype(jnp.bfloat16)
    return (grad_pre, summed * grad_scale)


def solution(mesh):
    axes = ("y", "zh", "zl", "x", "core")
    fine = Mesh(mesh.devices.reshape(4, 2, 4, 4, 2), axes)
    dp, row, col = ("y", "zh"), "zl", ("x", "core")
    return jax.shard_map(
        on_device,
        mesh=fine,
        in_specs=(P((*dp, row), col), P((*dp, *col), row), P(col, row)),
        out_specs=(P((*dp, row), col), P((*col, *dp), row)),
        check_vma=False,
    )
```

time: 198 us -> 203 us (1.025)
  waiting for transfers between devices: 41.9 us -> 74.4 us
  matrix products: 49 us -> 25.1 us
  local copies, waits for them, and re-layouts: 8.1 us -> 4.31 us
    ppermute x16, waiting for transfers between devices: 35.5 us -> 66.5 us  [along_z(): return lax.ppermute(v, Z, pairs)]
    dot_general x20 -> x7, matrix products: 49 us -> 25.1 us  [the longest x6 20 us: product(): lax.dot_general(unit.reshape(-1, block), rows.reshape(-1, feats), (((0,),...]
    ppermute x11 -> x10, waiting for transfers between devices: 2.52 us -> 7.84 us  [shift(): return lax.ppermute(v, axis, [(i, (i + step) % n) for i in range(n)])]
    select_n x10 -> x5, other arithmetic: 7.56 us -> 2.97 us  [the longest x1 1.79 us: on_device(): r4 = along_z(after(jnp.where(zl == 2, r2, r3), far), 1, (1, 2))]
    another operation x1 -> x7, other arithmetic: 1.28 us -> 5.28 us  [the longest x3 3.16 us: on_device(): units = [jnp.stack([a, b], axis=2) for a, b in zip(in_group, from_group)]]
    ppermute x3, waiting for transfers between devices: 3.16 us -> 0.01 us  [on_device(): q = q + lax.ppermute(p, ('zl', 'x'), pairs)]
    unnamed x40 -> x52, local copies, waits for them, and re-layouts: 4.23 us -> 2.21 us
    ppermute x11 -> x10, starting transfers between devices: 29.3 us -> 27.6 us  [shift(): return lax.ppermute(v, axis, [(i, (i + step) % n) for i in range(n)])]
  transfers between devices with their start and end apart: 32 -> 30, of which waited for: 5 -> 12; matrix products, arithmetic and copies ran while one was open for 32% -> 17% of each run, Pallas kernels for 0% -> 0%
where the time goes in v2:
time: 203 us; the launch traced here: 200 us
  waiting for transfers between devices  74.4 us (37%)
  starting transfers between devices  63.4 us (31%)
  matrix products  25.1 us (12%)
  other arithmetic  18.2 us (9%)
  between operations  14.8 us (7%)
  local copies, waits for them, and re-layouts  4.31 us (2%)
    ppermute x16, waiting for transfers between devices, along_z(): return lax.ppermute(v, Z, pairs)  66.5 us
    ppermute x16, starting transfers between devices, along_z(): return lax.ppermute(v, Z, pairs)  33.1 us
    ppermute x10, starting transfers between devices, shift(): return lax.ppermute(v, axis, [(i, (i + step) % n) for i in range(n)])  27.6 us
    dot_general x6, matrix products, product(): lax.dot_general(unit.reshape(-1, block), rows.reshape(-1, feats), (((0,),...  20 us
    ppermute x10, waiting for transfers between devices, shift(): return lax.ppermute(v, axis, [(i, (i + step) % n) for i in range(n)])  7.84 us
    dot_general x1, matrix products, on_device(): lax.dot_general(rows, down_weight, (((1,), (1,)), ((), ())), preferred_el...  5.1 us
  transfers between devices with their start and end apart: 30, of which 12 were waited for; matrix products, arithmetic and copies ran while one was open for 17% of the time, Pallas kernels for 0%

profile of v2, /device:TPU:1, one launch (start us, length us, event | category | flops | bytes accessed | tf_op | source)
XLA Modules:
  0.0 200.1 jit_solution(12830638329847977061)
XLA Ops:
  7.2 7.8 %collective-permute-start.7 = (bf16[64,1536]{1,0:T(8,128)(2,1)}, bf16[64,1536]{1,0:T(8,128)(2,1)S(1)}, u32[]{:S(2)}, u32[]{:S(2)}) collective-permute-start(bf16[64,1536]{1,0:T(8,128)(2,1)} %param.4), channel_id=1, source_target_pairs={{0,32},{32,0},{1,33},{33,1},{2,34},{34,2},{3,35},{35,3},{4,36},{36... | collective-permute-start | bytes 589832 | tf_op jit(solution)/shard_map/ppermute | solution.py:27
  15.0 4.3 %collective-permute-done.7 = bf16[64,1536]{1,0:T(8,128)(2,1)S(1)} collective-permute-done((bf16[64,1536]{1,0:T(8,128)(2,1)}, bf16[64,1536]{1,0:T(8,128)(2,1)S(1)}, u32[]{:S(2)}, u32[]{:S(2)}) %collective-permute-start.7) | collective-permute-done | bytes 196640 | tf_op jit(solution)/shard_map/ppermute | solution.py:27
  21.1 3.4 %collective-permute-start.1 = (bf16[64,1536]{1,0:T(8,128)(2,1)}, bf16[64,1536]{1,0:T(8,128)(2,1)}, u32[]{:S(2)}, u32[]{:S(2)}) collective-permute-start(bf16[64,1536]{1,0:T(8,128)(2,1)} %param.4), channel_id=1, source_target_pairs={{0,4},{2,6},{4,0},{6,2},{1,5},{3,7},{5,1},{7,3},{8,12},{10,14},{12... | collective-permute-start | bytes 589832 | tf_op jit(solution)/shard_map/ppermute | solution.py:27
  30.1 2.7 %collective-permute-start.6 = (bf16[2,2,64,384]{3,2,1,0:T(8,128)(2,1)}, bf16[2,2,64,384]{3,2,1,0:T(8,128)(2,1)S(1)}, u32[]{:S(2)}, u32[]{:S(2)}) collective-permute-start(bf16[2,2,64,384]{3,2,1,0:T(8,128)(2,1)} %get-tuple-element.76), channel_id=1, source_target_pairs={{0,192},{64,0},{128,64},{192,128},{1,193},{65,1},{129,65},{193,129... | collective-permute-start | bytes 589832 | tf_op jit(solution)/shard_map/ppermute | solution.py:27
  35.1 3.1 %collective-permute-start.3 = (bf16[4,64,1536]{2,1,0:T(8,128)(2,1)S(1)}, bf16[4,64,1536]{2,1,0:T(8,128)(2,1)S(1)}, u32[]{:S(2)}, u32[]{:S(2)}) collective-permute-start(bf16[4,64,1536]{2,1,0:T(8,128)(2,1)S(1)} %pad_maximum_fusion.8), channel_id=1, source_target_pairs={{0,1},{1,0},{2,3},{3,2},{4,5},{5,4},{6,7},{7,6},{8,9},{9,8},{10,11... | collective-permute-start | bytes 2359304 | tf_op jit(solution)/shard_map/ppermute | solution.py:27
  40.9 3.5 %collective-permute-done.4 = bf16[2,2,64,384]{3,2,1,0:T(8,128)(2,1)S(1)} collective-permute-done((bf16[2,2,64,384]{3,2,1,0:T(8,128)(2,1)S(1)}, bf16[2,2,64,384]{3,2,1,0:T(8,128)(2,1)S(1)}, u32[]{:S(2)}, u32[]{:S(2)}) %collective-permute-start.4) | collective-permute-done | bytes 196640 | tf_op jit(solution)/shard_map/ppermute | solution.py:27
  44.8 11.7 %collective-permute-start.14 = (bf16[2,4,64,384]{3,2,1,0:T(8,128)(2,1)S(1)}, bf16[2,4,64,384]{3,2,1,0:T(8,128)(2,1)S(1)}, u32[]{:S(2)}, u32[]{:S(2)}) collective-permute-start(bf16[2,4,64,384]{3,2,1,0:T(8,128)(2,1)S(1)} %get-tuple-element.74), channel_id=1, source_target_pairs={{0,56},{8,0},{16,8},{24,16},{32,24},{40,32},{48,40},{56,48},{1,57}... | collective-permute-start | bytes 1179656 | tf_op jit(solution)/shard_map/ppermute | solution.py:32
  58.6 4.7 %collective-permute-done.14 = bf16[2,4,64,384]{3,2,1,0:T(8,128)(2,1)S(1)} collective-permute-done((bf16[2,4,64,384]{3,2,1,0:T(8,128)(2,1)S(1)}, bf16[2,4,64,384]{3,2,1,0:T(8,128)(2,1)S(1)}, u32[]{:S(2)}, u32[]{:S(2)}) %collective-permute-start.14) | collective-permute-done | bytes 393248 | tf_op jit(solution)/shard_map/ppermute | solution.py:32
  63.3 3.1 %collective-permute-done.12 = bf16[2,4,64,384]{3,2,1,0:T(8,128)(2,1)S(1)} collective-permute-done((bf16[2,4,64,384]{3,2,1,0:T(8,128)(2,1)S(1)}, bf16[2,4,64,384]{3,2,1,0:T(8,128)(2,1)S(1)}, u32[]{:S(2)}, u32[]{:S(2)}) %collective-permute-start.12) | collective-permute-done | bytes 393248 | tf_op jit(solution)/shard_map/ppermute | solution.py:32
  70.2 5.1 %fusion.103 = f32[512,3072]{0,1:T(8,128)S(1)} fusion(bf16[512,1536]{1,0:T(8,128)(2,1)S(1)} %bitcast.200, bf16[3072,1536]{1,0:T(8,128)(2,1)S(1)} %bitcast.208), kind=kOutput, calls=%fused_computation.174 | convolution fusion | flops 4831838208 | bytes 17301504 | tf_op jit(solution)/shard_map/dot_general | solution.py:98
  81.0 5.3 %collective-permute-start.17 = (bf16[2,4,64,384]{3,2,1,0:T(8,128)(2,1)S(1)}, bf16[2,4,64,384]{3,2,1,0:T(8,128)(2,1)}, u32[]{:S(2)}, u32[]{:S(2)}) collective-permute-start(bf16[2,4,64,384]{3,2,1,0:T(8,128)(2,1)S(1)} %broadcast_select_fusion.6), channel_id=1, source_target_pairs={{0,8},{8,16},{16,24},{32,40},{40,48},{48,56},{1,9},{9,17},{17,25},... | collective-permute-start | bytes 1179656 | tf_op jit(solution)/shard_map/ppermute | solution.py:32
  86.4 2.8 %collective-permute-done.18 = bf16[2,4,64,384]{3,2,1,0:T(8,128)(2,1)S(1)} collective-permute-done((bf16[2,4,64,384]{3,2,1,0:T(8,128)(2,1)S(1)}, bf16[2,4,64,384]{3,2,1,0:T(8,128)(2,1)S(1)}, u32[]{:S(2)}, u32[]{:S(2)}) %collective-permute-start.18) | collective-permute-done | bytes 393248 | tf_op jit(solution)/shard_map/ppermute | solution.py:32
  89.2 12.4 %collective-permute-done.17 = bf16[2,4,64,384]{3,2,1,0:T(8,128)(2,1)} collective-permute-done((bf16[2,4,64,384]{3,2,1,0:T(8,128)(2,1)S(1)}, bf16[2,4,64,384]{3,2,1,0:T(8,128)(2,1)}, u32[]{:S(2)}, u32[]{:S(2)}) %collective-permute-start.17) | collective-permute-done | bytes 393248 | tf_op jit(solution)/shard_map/ppermute | solution.py:32
  105.0 4.8 %collective-permute-start.26 = (bf16[4,4,2,64,1536]{4,3,2,1,0:T(8,128)(2,1)}, bf16[4,4,2,64,1536]{4,3,2,1,0:T(8,128)(2,1)}, u32[]{:S(2)}, u32[]{:S(2)}) collective-permute-start(bf16[4,4,2,64,1536]{4,3,2,1,0:T(8,128)(2,1)} %bitcast.193), channel_id=1, source_target_pairs={{0,1},{1,0},{2,3},{3,2},{4,5},{5,4},{6,7},{7,6},{8,9},{9,8},{10,11... | collective-permute-start | bytes 18874376 | tf_op jit(solution)/shard_map/ppermute | solution.py:27
  117.9 13.5 %collective-permute-done.24 = bf16[2,4,64,384]{3,2,1,0:T(8,128)(2,1)} collective-permute-done((bf16[2,4,64,384]{3,2,1,0:T(8,128)(2,1)}, bf16[2,4,64,384]{3,2,1,0:T(8,128)(2,1)}, u32[]{:S(2)}, u32[]{:S(2)}) %collective-permute-start.24) | collective-permute-done | bytes 393248 | tf_op jit(solution)/shard_map/ppermute | solution.py:32
  131.4 8.4 %collective-permute-done.25 = bf16[2,4,64,384]{3,2,1,0:T(8,128)(2,1)} collective-permute-done((bf16[2,4,64,384]{3,2,1,0:T(8,128)(2,1)S(1)}, bf16[2,4,64,384]{3,2,1,0:T(8,128)(2,1)}, u32[]{:S(2)}, u32[]{:S(2)}) %collective-permute-start.25) | collective-permute-done | bytes 393248 | tf_op jit(solution)/shard_map/ppermute | solution.py:32
  148.2 4.3 %collective-permute-done.27 = bf16[2,4,64,384]{3,2,1,0:T(8,128)(2,1)S(1)} collective-permute-done((bf16[2,4,64,384]{3,2,1,0:T(8,128)(2,1)}, bf16[2,4,64,384]{3,2,1,0:T(8,128)(2,1)S(1)}, u32[]{:S(2)}, u32[]{:S(2)}) %collective-permute-start.27) | collective-permute-done | bytes 393248 | tf_op jit(solution)/shard_map/ppermute | solution.py:32
  153.5 8.8 %collective-permute-done.19 = f16[128,3200]{0,1:T(8,128)(2,1)S(1)} collective-permute-done((f16[128,3200]{0,1:T(8,128)(2,1)}, f16[128,3200]{0,1:T(8,128)(2,1)S(1)}, u32[]{:S(2)}, u32[]{:S(2)}) %collective-permute-start.19) | collective-permute-done | bytes 819232 | tf_op jit(solution)/shard_map/ppermute | solution.py:32
  162.3 7.7 %collective-permute-done.21 = f16[128,3200]{0,1:T(8,128)(2,1)S(1)} collective-permute-done((f16[128,3200]{0,1:T(8,128)(2,1)S(1)}, f16[128,3200]{0,1:T(8,128)(2,1)S(1)}, u32[]{:S(2)}, u32[]{:S(2)}) %collective-permute-start.21) | collective-permute-done | bytes 819232 | tf_op jit(solution)/shard_map/ppermute | solution.py:32
  173.1 2.4 %convolution_bitcast_fusion.1 = f32[384,1536]{1,0:T(8,128)S(1)} fusion(bf16[4,4,2,64,1536]{4,3,2,1,0:T(8,128)(2,1)} %bitcast.194, s32[]{:T(128)S(6)} %select_n.816, bf16[4,2,64,384]{3,2,0,1:T(8,128)(2,1)} %get-tuple-element.81), kind=kOutput, calls=%fused_computation.20 | convolution fusion | flops 603979776 | bytes 4325380 | tf_op jit(solution)/shard_map/dot_general | solution.py:153
  175.5 3.3 %fusion.8 = f32[384,1536]{1,0:T(8,128)S(1)} fusion(bf16[4,4,2,64,1536]{4,3,2,1,0:T(8,128)(2,1)} %bitcast.195, bf16[1,4,2,64,384]{4,3,2,1,0:T(8,128)(2,1)S(1)} %copy-done.21, bf16[1,4,2,64,384]{4,3,2,1,0:T(8,128)(2,1)S(1)} %copy-done.20), kind=kOutput, calls=%fused_computation.15 | convolution fusion | flops 1208352768 | bytes 6291456 | tf_op jit(solution)/shard_map/dot_general | solution.py:153
  178.9 3.4 %fusion.26 = f32[384,1536]{1,0:T(8,128)S(1)} fusion(f32[384,1536]{1,0:T(8,128)S(1)} %fusion.8, bf16[4,4,2,64,1536]{4,3,2,1,0:T(8,128)(2,1)} %bitcast.196, bf16[1,4,2,64,384]{4,3,1,0,2:T(8,128)(2,1)S(1)} %get-tuple-element.95, bf16[1,4,2,64,384]{4,3,1,0,2:T(8,128)(2,1)S(1)} %get-tuple-element.94), kind=kOutput, calls=%fused_computation.23 | convolution fusion | flops 1208942592 | bytes 8650752 | tf_op jit(solution)/shard_map/dot_general | solution.py:153
  182.4 3.3 %fusion.17 = f32[384,1536]{1,0:T(8,128)S(1)} fusion(bf16[4,4,2,64,1536]{4,3,2,1,0:T(8,128)(2,1)} %collective-permute-done.26, bf16[2,4,1,64,384]{4,3,1,0,2:T(8,128)(2,1)S(1)} %copy-done.10, bf16[2,4,1,64,384]{4,3,1,0,2:T(8,128)(2,1)S(1)} %copy-done.12, bf16[2,4,1,64,384]{4,3,1,0,2:T(8,128)(2,1)S(1)} %copy-done.14, bf16[2,4,1,64,384]{4,3,1,0,2:T(8,128)(2,1)S(1)} %copy-done.8), kind=kOutput, calls=%fused_computation.18 | convolution fusion | flops 1212284928 | bytes 7077888 | tf_op jit(solution)/shard_map/dot_general | solution.py:153
  188.1 5.2 %fusion.35 = f32[384,1536]{1,0:T(8,128)} fusion(f32[384,1536]{1,0:T(8,128)S(1)} %convolution_bitcast_fusion, f32[384,1536]{1,0:T(8,128)S(1)} %convolution_bitcast_fusion.1, f32[384,1536]{1,0:T(8,128)S(1)} %fusion.17, f32[384,1536]{1,0:T(8,128)S(1)} %fusion.26, bf16[4,4,2,64,1536]{4,3,2,1,0:T(8,128)(2,1)} %collective-permute-done.26, ...), kind=kOutput, calls=%fused_computation.26 | convolution fusion | flops 1215234048 | bytes 16515072 | tf_op jit(solution)/shard_map/dot_general | solution.py:153
  (141 shorter events, 50.0 us)
Async XLA Ops:
  7.2 97.9 %all-gather.3.cloned.1.call-start = ((), (), s32[]{:S(2)}) async-start(), calls=%async_computation | async-start | bytes 6684672 | tf_op jit(solution)/shard_map/all_gather | solution.py:68
  7.2 12.1 %collective-permute-start.7 = (bf16[64,1536]{1,0:T(8,128)(2,1)}, bf16[64,1536]{1,0:T(8,128)(2,1)S(1)}, u32[]{:S(2)}, u32[]{:S(2)}) collective-permute-start(bf16[64,1536]{1,0:T(8,128)(2,1)} %param.4), channel_id=1, source_target_pairs={{0,32},{32,0},{1,33},{33,1},{2,34},{34,2},{3,35},{35,3},{4,36},{36... | collective-permute-start | bytes 589832 | tf_op jit(solution)/shard_map/ppermute | solution.py:27
  21.1 12.1 %collective-permute-start.1 = (bf16[64,1536]{1,0:T(8,128)(2,1)}, bf16[64,1536]{1,0:T(8,128)(2,1)}, u32[]{:S(2)}, u32[]{:S(2)}) collective-permute-start(bf16[64,1536]{1,0:T(8,128)(2,1)} %param.4), channel_id=1, source_target_pairs={{0,4},{2,6},{4,0},{6,2},{1,5},{3,7},{5,1},{7,3},{8,12},{10,14},{12... | collective-permute-start | bytes 589832 | tf_op jit(solution)/shard_map/ppermute | solution.py:27
  24.4 9.4 %collective-permute-start = (bf16[64,1536]{1,0:T(8,128)(2,1)}, bf16[64,1536]{1,0:T(8,128)(2,1)}, u32[]{:S(2)}, u32[]{:S(2)}) collective-permute-start(bf16[64,1536]{1,0:T(8,128)(2,1)} %param.4), channel_id=1, source_target_pairs={{0,2},{2,4},{4,6},{6,0},{1,3},{3,5},{5,7},{7,1},{8,10},{10,12},{12... | collective-permute-start | bytes 589832 | tf_op jit(solution)/shard_map/ppermute | solution.py:27
  24.8 9.1 %collective-permute-start.2 = (bf16[64,1536]{1,0:T(8,128)(2,1)}, bf16[64,1536]{1,0:T(8,128)(2,1)}, u32[]{:S(2)}, u32[]{:S(2)}) collective-permute-start(bf16[64,1536]{1,0:T(8,128)(2,1)} %param.4), channel_id=1, source_target_pairs={{0,6},{2,0},{4,2},{6,4},{1,7},{3,1},{5,3},{7,5},{8,14},{10,8},{12,... | collective-permute-start | bytes 589832 | tf_op jit(solution)/shard_map/ppermute | solution.py:27
  33.2 11.2 %collective-permute-start.4 = (bf16[2,2,64,384]{3,2,1,0:T(8,128)(2,1)S(1)}, bf16[2,2,64,384]{3,2,1,0:T(8,128)(2,1)S(1)}, u32[]{:S(2)}, u32[]{:S(2)}) collective-permute-start(bf16[2,2,64,384]{3,2,1,0:T(8,128)(2,1)S(1)} %get-tuple-element.78), channel_id=1, source_target_pairs={{0,64},{64,128},{128,192},{192,0},{1,65},{65,129},{129,193},{193,1... | collective-permute-start | bytes 589832 | tf_op jit(solution)/shard_map/ppermute | solution.py:27
  35.1 33.6 %collective-permute-start.3 = (bf16[4,64,1536]{2,1,0:T(8,128)(2,1)S(1)}, bf16[4,64,1536]{2,1,0:T(8,128)(2,1)S(1)}, u32[]{:S(2)}, u32[]{:S(2)}) collective-permute-start(bf16[4,64,1536]{2,1,0:T(8,128)(2,1)S(1)} %pad_maximum_fusion.8), channel_id=1, source_target_pairs={{0,1},{1,0},{2,3},{3,2},{4,5},{5,4},{6,7},{7,6},{8,9},{9,8},{10,11... | collective-permute-start | bytes 2359304 | tf_op jit(solution)/shard_map/ppermute | solution.py:27
  38.2 18.3 %collective-permute-start.10 = (bf16[64,1536]{1,0:T(8,128)(2,1)S(1)}, bf16[64,1536]{1,0:T(8,128)(2,1)S(1)}, u32[]{:S(2)}, u32[]{:S(2)}) collective-permute-start(bf16[64,1536]{1,0:T(8,128)(2,1)S(1)} %collective-permute-done.7), channel_id=1, source_target_pairs={{6,4},{24,30},{7,5},{25,31},{38,36},{56,62},{39,37},{57,63},{70,68... | collective-permute-start | bytes 589832 | tf_op jit(solution)/shard_map/ppermute | solution.py:88
  38.9 17.6 %collective-permute-start.9 = (bf16[64,1536]{1,0:T(8,128)(2,1)S(1)}, bf16[64,1536]{1,0:T(8,128)(2,1)S(1)}, u32[]{:S(2)}, u32[]{:S(2)}) collective-permute-start(bf16[64,1536]{1,0:T(8,128)(2,1)S(1)} %collective-permute-done.7), channel_id=1, source_target_pairs={{6,2},{24,28},{7,3},{25,29},{38,34},{56,60},{39,35},{57,61},{70,66... | collective-permute-start | bytes 589832 | tf_op jit(solution)/shard_map/ppermute | solution.py:88
  39.6 16.9 %collective-permute-start.8 = (bf16[64,1536]{1,0:T(8,128)(2,1)S(1)}, bf16[64,1536]{1,0:T(8,128)(2,1)S(1)}, u32[]{:S(2)}, u32[]{:S(2)}) collective-permute-start(bf16[64,1536]{1,0:T(8,128)(2,1)S(1)} %collective-permute-done.7), channel_id=1, source_target_pairs={{6,0},{24,26},{7,1},{25,27},{38,32},{56,58},{39,33},{57,59},{70,64... | collective-permute-start | bytes 589832 | tf_op jit(solution)/shard_map/ppermute | solution.py:88
  44.8 18.5 %collective-permute-start.14 = (bf16[2,4,64,384]{3,2,1,0:T(8,128)(2,1)S(1)}, bf16[2,4,64,384]{3,2,1,0:T(8,128)(2,1)S(1)}, u32[]{:S(2)}, u32[]{:S(2)}) collective-permute-start(bf16[2,4,64,384]{3,2,1,0:T(8,128)(2,1)S(1)} %get-tuple-element.74), channel_id=1, source_target_pairs={{0,56},{8,0},{16,8},{24,16},{32,24},{40,32},{48,40},{56,48},{1,57}... | collective-permute-start | bytes 1179656 | tf_op jit(solution)/shard_map/ppermute | solution.py:32
  56.5 9.9 %collective-permute-start.12 = (bf16[2,4,64,384]{3,2,1,0:T(8,128)(2,1)S(1)}, bf16[2,4,64,384]{3,2,1,0:T(8,128)(2,1)S(1)}, u32[]{:S(2)}, u32[]{:S(2)}) collective-permute-start(bf16[2,4,64,384]{3,2,1,0:T(8,128)(2,1)S(1)} %get-tuple-element.75), channel_id=1, source_target_pairs={{0,8},{8,16},{16,24},{24,32},{32,40},{40,48},{48,56},{56,0},{1,9},... | collective-permute-start | bytes 1179656 | tf_op jit(solution)/shard_map/ppermute | solution.py:32
  56.6 12.3 %collective-permute-start.11 = (bf16[64,1536]{1,0:T(8,128)(2,1)S(1)}, bf16[64,1536]{1,0:T(8,128)(2,1)S(1)}, u32[]{:S(2)}, u32[]{:S(2)}) collective-permute-start(bf16[64,1536]{1,0:T(8,128)(2,1)S(1)} %add_add_fusion), channel_id=1, source_target_pairs={{0,1},{1,0},{2,3},{3,2},{4,5},{5,4},{6,7},{7,6},{8,9},{9,8},{10,11... | collective-permute-start | bytes 589832 | tf_op jit(solution)/shard_map/ppermute | solution.py:27
  67.6 9.1 %collective-permute-start.13 = (bf16[2,4,64,384]{3,2,1,0:T(8,128)(2,1)S(1)}, bf16[2,4,64,384]{3,2,1,0:T(8,128)(2,1)S(1)}, u32[]{:S(2)}, u32[]{:S(2)}) collective-permute-start(bf16[2,4,64,384]{3,2,1,0:T(8,128)(2,1)S(1)} %get-tuple-element.84), channel_id=1, source_target_pairs={{0,8},{8,16},{16,24},{24,32},{32,40},{40,48},{48,56},{56,0},{1,9},... | collective-permute-start | bytes 1179656 | tf_op jit(solution)/shard_map/ppermute | solution.py:32
  76.7 24.9 %collective-permute-start.20 = (f16[128,3200]{0,1:T(8,128)(2,1)S(1)}, f16[128,3200]{0,1:T(8,128)(2,1)S(1)}, u32[]{:S(2)}, u32[]{:S(2)}) collective-permute-start(f16[128,3200]{0,1:T(8,128)(2,1)S(1)} %pad_maximum_fusion.2), channel_id=1, source_target_pairs={{16,8},{24,16},{48,40},{56,48},{17,9},{25,17},{49,41},{57,49},{18,... | collective-permute-start | bytes 2457608 | tf_op jit(solution)/shard_map/ppermute | solution.py:32
  77.4 24.2 %collective-permute-start.16 = (f16[128,3200]{0,1:T(8,128)(2,1)S(1)}, f16[128,3200]{0,1:T(8,128)(2,1)S(1)}, u32[]{:S(2)}, u32[]{:S(2)}) collective-permute-start(f16[128,3200]{0,1:T(8,128)(2,1)S(1)} %pad_maximum_fusion.2), channel_id=1, source_target_pairs={{0,8},{8,16},{32,40},{40,48},{1,9},{9,17},{33,41},{41,49},{2,10},{... | collective-permute-start | bytes 2457608 | tf_op jit(solution)/shard_map/ppermute | solution.py:32
  79.7 9.5 %collective-permute-start.18 = (bf16[2,4,64,384]{3,2,1,0:T(8,128)(2,1)S(1)}, bf16[2,4,64,384]{3,2,1,0:T(8,128)(2,1)S(1)}, u32[]{:S(2)}, u32[]{:S(2)}) collective-permute-start(bf16[2,4,64,384]{3,2,1,0:T(8,128)(2,1)S(1)} %broadcast_select_fusion.1), channel_id=1, source_target_pairs={{24,16},{16,8},{8,0},{56,48},{48,40},{40,32},{25,17},{17,9},{9,1},... | collective-permute-start | bytes 1179656 | tf_op jit(solution)/shard_map/ppermute | solution.py:32
  81.0 20.6 %collective-permute-start.17 = (bf16[2,4,64,384]{3,2,1,0:T(8,128)(2,1)S(1)}, bf16[2,4,64,384]{3,2,1,0:T(8,128)(2,1)}, u32[]{:S(2)}, u32[]{:S(2)}) collective-permute-start(bf16[2,4,64,384]{3,2,1,0:T(8,128)(2,1)S(1)} %broadcast_select_fusion.6), channel_id=1, source_target_pairs={{0,8},{8,16},{16,24},{32,40},{40,48},{48,56},{1,9},{9,17},{17,25},... | collective-permute-start | bytes 1179656 | tf_op jit(solution)/shard_map/ppermute | solution.py:32
  105.0 77.3 %collective-permute-start.26 = (bf16[4,4,2,64,1536]{4,3,2,1,0:T(8,128)(2,1)}, bf16[4,4,2,64,1536]{4,3,2,1,0:T(8,128)(2,1)}, u32[]{:S(2)}, u32[]{:S(2)}) collective-permute-start(bf16[4,4,2,64,1536]{4,3,2,1,0:T(8,128)(2,1)} %bitcast.193), channel_id=1, source_target_pairs={{0,1},{1,0},{2,3},{3,2},{4,5},{5,4},{6,7},{7,6},{8,9},{9,8},{10,11... | collective-permute-start | bytes 18874376 | tf_op jit(solution)/shard_map/ppermute | solution.py:27
  115.3 16.1 %collective-permute-start.24 = (bf16[2,4,64,384]{3,2,1,0:T(8,128)(2,1)}, bf16[2,4,64,384]{3,2,1,0:T(8,128)(2,1)}, u32[]{:S(2)}, u32[]{:S(2)}) collective-permute-start(bf16[2,4,64,384]{3,2,1,0:T(8,128)(2,1)} %broadcast_select_fusion), channel_id=1, source_target_pairs={{16,8},{8,0},{48,40},{40,32},{17,9},{9,1},{49,41},{41,33},{18,10},... | collective-permute-start | bytes 1179656 | tf_op jit(solution)/shard_map/ppermute | solution.py:32
  116.6 23.3 %collective-permute-start.25 = (bf16[2,4,64,384]{3,2,1,0:T(8,128)(2,1)S(1)}, bf16[2,4,64,384]{3,2,1,0:T(8,128)(2,1)}, u32[]{:S(2)}, u32[]{:S(2)}) collective-permute-start(bf16[2,4,64,384]{3,2,1,0:T(8,128)(2,1)S(1)} %collective-permute-done.18), channel_id=1, source_target_pairs={{8,0},{40,32},{9,1},{41,33},{10,2},{42,34},{11,3},{43,35},{12,4},{... | collective-permute-start | bytes 1179656 | tf_op jit(solution)/shard_map/ppermute | solution.py:32
  140.5 12.0 %collective-permute-start.27 = (bf16[2,4,64,384]{3,2,1,0:T(8,128)(2,1)}, bf16[2,4,64,384]{3,2,1,0:T(8,128)(2,1)S(1)}, u32[]{:S(2)}, u32[]{:S(2)}) collective-permute-start(bf16[2,4,64,384]{3,2,1,0:T(8,128)(2,1)} %collective-permute-done.24), channel_id=1, source_target_pairs={{8,0},{40,32},{9,1},{41,33},{10,2},{42,34},{11,3},{43,35},{12,4},{... | collective-permute-start | bytes 1179656 | tf_op jit(solution)/shard_map/ppermute | solution.py:32
  141.8 20.5 %collective-permute-start.19 = (f16[128,3200]{0,1:T(8,128)(2,1)}, f16[128,3200]{0,1:T(8,128)(2,1)S(1)}, u32[]{:S(2)}, u32[]{:S(2)}) collective-permute-start(f16[128,3200]{0,1:T(8,128)(2,1)} %pad_maximum_fusion.3), channel_id=1, source_target_pairs={{0,8},{8,16},{16,24},{24,32},{32,40},{40,48},{48,56},{56,0},{1,9},... | collective-permute-start | bytes 2457608 | tf_op jit(solution)/shard_map/ppermute | solution.py:32
  146.2 23.9 %collective-permute-start.21 = (f16[128,3200]{0,1:T(8,128)(2,1)S(1)}, f16[128,3200]{0,1:T(8,128)(2,1)S(1)}, u32[]{:S(2)}, u32[]{:S(2)}) collective-permute-start(f16[128,3200]{0,1:T(8,128)(2,1)S(1)} %copy-done.17), channel_id=1, source_target_pairs={{0,56},{8,0},{16,8},{24,16},{32,24},{40,32},{48,40},{56,48},{1,57}... | collective-permute-start | bytes 2457608 | tf_op jit(solution)/shard_map/ppermute | solution.py:32
  (31 other events, 231.9 us)
Sparse Core Ops, SparseCore 0:
  21.2 75.1 all-gather.2

commit v3 on v2

v3 whole, which is shorter than its diff:
```python
import math

import jax
import jax.numpy as jnp
from jax import lax
from jax.sharding import Mesh
from jax.sharding import PartitionSpec as P

root_two_pi = math.sqrt(2.0 / math.pi)
gelu_coeff = 0.044715
Z = ("zh", "zl")


def gelu_parts(pre_values):
    cubic_term = gelu_coeff * pre_values * pre_values * pre_values
    inner_arg = root_two_pi * (pre_values + cubic_term)
    tangent = jnp.tanh(inner_arg)
    gelu_value = 0.5 * pre_values * (1.0 + tangent)
    gelu_slope = 0.5 * (1.0 + tangent) + 0.5 * pre_values * (
        1.0 - tangent * tangent
    ) * root_two_pi * (1.0 + 3.0 * gelu_coeff * pre_values * pre_values)
    return (gelu_value, gelu_slope)


def shift(v, axis, step):
    n = lax.axis_size(axis)
    return lax.ppermute(v, axis, [(i, (i + step) % n) for i in range(n)])


def along_z(v, step, senders):
    pairs = [(4 * h + l, (4 * h + l + step) % 8) for h in range(2) for l in senders]
    return lax.ppermute(v, Z, pairs)


def pairs_z(v, steps):
    pairs = [(4 * h + l, (4 * h + l + s) % 8) for h in range(2) for l, s in steps.items()]
    return lax.ppermute(v, Z, pairs)


def at(v, i):
    return lax.dynamic_index_in_dim(v, i, 0, keepdims=False)


def after(v, *first):
    return lax.optimization_barrier((v, *first))[0]


def pack(v):
    top = jnp.max(jnp.abs(v), axis=1, keepdims=True)
    e = jnp.clip(jnp.floor(jnp.log2(jnp.maximum(top, 1e-30))), -100.0, 100.0)
    body = (v * jnp.exp2(13.0 - e)).astype(jnp.float16)
    tail = jnp.broadcast_to(e, (v.shape[0], 128)).astype(jnp.float16)
    return jnp.concatenate([body, tail], axis=1)


def unpack(w):
    n = w.shape[1] - 128
    e = w[:, n : n + 1].astype(jnp.float32)
    return w[:, :n].astype(jnp.float32) * jnp.exp2(e - 13.0)


def on_device(pre_act, grad_out, down_weight):
    y, zh, zl, x, c = (lax.axis_index(a) for a in ("y", "zh", "zl", "x", "core"))
    tokens, hidden = pre_act.shape
    half, feats = grad_out.shape
    block = hidden // 8
    grad_scale = 1.0 / math.sqrt(tokens * 32)

    p = shift(grad_out, "zh", 1)
    gelu_value, gelu_slope = gelu_parts(pre_act.astype(jnp.float32))
    act, gelu_slope = lax.optimization_barrier((gelu_value.astype(jnp.bfloat16), gelu_slope))
    act = act.reshape(tokens, 4, 2, block).transpose(1, 2, 0, 3)
    act = jnp.where(zh == 1, act[:, ::-1], act)
    halves = act.reshape(4, 2, 2, half, block)
    act = jnp.where(c == 1, halves[:, :, ::-1], halves)
    pieces_out = [at(act, (y + s) % 4) for s in range(4)]
    pieces = [shift(v, "y", s) if s else v for s, v in enumerate(pieces_out)]
    own, cross = (
        jnp.stack([lax.select_n((y - k) % 4, *[v[i] for v in pieces]) for k in range(4)], axis=1)
        for i in range(2)
    )

    both = after(jnp.stack([grad_out, p]), *pieces_out)
    all_rows = lax.all_gather(both, ("x", "y")).reshape(4, 4, 2, half, feats)

    from_x = jnp.stack([both] + [shift(both, "x", t) for t in (1, 2, 3)])
    beyond = at(from_x[:, 1], jnp.where(zl == 0, x - 3, x) % 4)
    mine = jnp.concatenate([from_x[:, 0], beyond[None]])
    mine = jnp.stack([mine, shift(mine, "core", 1)], axis=1)
    mine = after(mine, own, cross)

    place = [(x - zl - k) % 4 for k in (2, 1, -1, 0)]
    place[1] = jnp.where(zl == 3, 4, place[1])
    place[2] = jnp.where(zl == 0, 4, place[2])
    rows = jnp.stack([at(mine, k) for k in place])
    rows = jnp.where(c == 1, rows[:, ::-1], rows).reshape(4 * tokens, feats)
    parts = lax.dot_general(
        rows, down_weight, (((1,), (1,)), ((), ())), preferred_element_type=jnp.float32
    )
    part_far, part_up, part_down, part_own = (
        parts[k * tokens : (k + 1) * tokens] for k in range(4)
    )
    far = pack(part_far)

    e0, e3 = zl == 0, zl == 3
    a_up = along_z(jnp.where(e3, cross, own), 1, range(4))
    a_down = along_z(jnp.where(e0, cross, own), -1, range(4))
    b = pairs_z(cross, {0: -2, 1: -2, 2: 2, 3: 2})
    far_up = along_z(far, 1, (0, 1))
    far_down = along_z(far, -1, (2, 3))
    c_up = along_z(after(jnp.where(e0, b, a_up), far), 1, (0, 1, 2))
    c_down = along_z(after(jnp.where(e3, b, a_down), far), -1, (3, 2, 1))
    d = pairs_z(after(b, far), {1: 1, 2: -1})
    near_up = pack(part_up + unpack(after(far_up, a_up, a_down, b)))
    near_down = pack(part_down + unpack(after(far_down, a_up, a_down, b)))
    from_below = along_z(near_up, 1, range(4))
    from_above = along_z(near_down, -1, range(4))
    e = pairs_z(jnp.where(zl == 1, c_up, c_down), {1: 1, 2: -1})
    f = pairs_z(jnp.where(zl == 2, c_up, c_down), {1: -1, 2: 1})
    g = pairs_z(d, {1: -1, 2: 1})
    h = pairs_z(e, {1: -1, 2: 1})

    all_rows = after(all_rows, e, f, g)
    other_rows = shift(all_rows, "core", 1)
    own, a_up, a_down, b, c_up, c_down, d, e, f, g = lax.optimization_barrier(
        (own, a_up, a_down, b, c_up, c_down, d, e, f, g)
    )

    def choose(*units):
        return lax.select_n(zl, *units)

    in_group = (
        choose(own, a_up, c_up, f),
        choose(a_down, own, a_up, c_up),
        choose(c_down, a_down, own, a_up),
        choose(f, c_down, a_down, own),
    )
    from_group = (
        choose(g, d, b, a_down),
        choose(h, e, c_down, b),
        choose(b, c_up, e, h),
        choose(a_up, b, d, g),
    )
    none = jnp.zeros_like(own)
    early = (from_group[0], choose(none, e, c_down, b), choose(b, c_up, e, none), from_group[3])
    last = choose(h, none, none, h)

    def product(core, first, second, rows):
        unit = jnp.stack([jnp.stack([i[core], j[core]], axis=1) for i, j in zip(first, second)])
        return lax.dot_general(
            unit.reshape(-1, block), rows.reshape(-1, feats), (((0,), (0,)), ((), ())),
            preferred_element_type=jnp.float32,
        )

    summed = product(0, in_group, early, all_rows)
    from_below, from_above = after(from_below, summed), after(from_above, summed)
    summed += product(0, (none,), (last,), at(all_rows, jnp.where(zl < 2, 1, 2)))
    summed += product(1, in_group, from_group, other_rows)

    grad_act = part_own + unpack(from_below) + unpack(from_above)
    grad_pre = (grad_act * gelu_slope).astype(jnp.bfloat16)
    return (grad_pre, summed * grad_scale)


def solution(mesh):
    axes = ("y", "zh", "zl", "x", "core")
    fine = Mesh(mesh.devices.reshape(4, 2, 4, 4, 2), axes)
    dp, row, col = ("y", "zh"), "zl", ("x", "core")
    return jax.shard_map(
        on_device,
        mesh=fine,
        in_specs=(P((*dp, row), col), P((*dp, *col), row), P(col, row)),
        out_specs=(P((*dp, row), col), P((*col, *dp), row)),
        check_vma=False,
    )
```

time: 203 us -> 215 us (1.059); the launches traced: 200 us -> 214 us
  other arithmetic: 18.2 us -> 31.1 us
  local copies, waits for them, and re-layouts: 4.31 us -> 10.6 us
  matrix products: 25.1 us -> 19.8 us
  starting transfers between devices: 63.4 us -> 67.4 us
  waiting for transfers between devices: 74.4 us -> 70.7 us
    ppermute x16 -> x8, waiting for transfers between devices: 66.5 us -> 33.6 us  [along_z(): return lax.ppermute(v, Z, pairs)]
    ppermute x10 -> x9, waiting for transfers between devices: 7.84 us -> 24.6 us  [shift(): return lax.ppermute(v, axis, [(i, (i + step) % n) for i in range(n)])]
    ppermute x3 -> x6, waiting for transfers between devices: 0.01 us -> 12.5 us  [pairs_z(): return lax.ppermute(v, Z, pairs)]
    dot_general x6 -> x3, matrix products: 20 us -> 11.8 us  [product(): lax.dot_general(unit.reshape(-1, block), rows.reshape(-1, feats), (((0,),...]
    ppermute x10 -> x9, starting transfers between devices: 27.6 us -> 20 us  [shift(): return lax.ppermute(v, axis, [(i, (i + step) % n) for i in range(n)])]
    ppermute x3 -> x6, starting transfers between devices: 2.63 us -> 9.01 us  [pairs_z(): return lax.ppermute(v, Z, pairs)]
    another operation x8 -> x15, other arithmetic: 6.5 us -> 12.8 us  [the longest x7 4.13 us: product(): jnp.stack([jnp.stack([i[core], j[core]], axis=1) for i, j in zip(first, s...]
    ppermute x16 -> x8, starting transfers between devices: 33.1 us -> 38.4 us  [along_z(): return lax.ppermute(v, Z, pairs)]
  transfers between devices with their start and end apart: 30 -> 24, of which waited for: 12 -> 12; matrix products, arithmetic and copies ran while one was open for 17% -> 23% of each run, Pallas kernels for 0% -> 0%
where the time goes in v3:
time: 215 us; the launch traced here: 214 us
  waiting for transfers between devices  70.7 us (33%)
  starting transfers between devices  67.4 us (31%)
  other arithmetic  31.1 us (14%)
  matrix products  19.8 us (9%)
  between operations  14.6 us (7%)
  local copies, waits for them, and re-layouts  10.6 us (5%)
    ppermute x8, starting transfers between devices, along_z(): return lax.ppermute(v, Z, pairs)  38.4 us
    ppermute x8, waiting for transfers between devices, along_z(): return lax.ppermute(v, Z, pairs)  33.6 us
    ppermute x9, waiting for transfers between devices, shift(): return lax.ppermute(v, axis, [(i, (i + step) % n) for i in range(n)])  24.6 us
    ppermute x9, starting transfers between devices, shift(): return lax.ppermute(v, axis, [(i, (i + step) % n) for i in range(n)])  20 us
    ppermute x6, waiting for transfers between devices, pairs_z(): return lax.ppermute(v, Z, pairs)  12.5 us
    dot_general x3, matrix products, product(): lax.dot_general(unit.reshape(-1, block), rows.reshape(-1, feats), (((0,),...  11.8 us
    ppermute x6, starting transfers between devices, pairs_z(): return lax.ppermute(v, Z, pairs)  9.01 us
    dot_general x1, matrix products, on_device(): lax.dot_general(rows, down_weight, (((1,), (1,)), ((), ())), preferred_el...  8.06 us
  transfers between devices with their start and end apart: 24, of which 12 were waited for; matrix products, arithmetic and copies ran while one was open for 23% of the time, Pallas kernels for 0%

profile of v3, /device:TPU:1, one launch (start us, length us, event | category | flops | bytes accessed | tf_op | source)
XLA Modules:
  0.0 214.3 jit_solution(10926049074811772161)
XLA Ops:
  7.2 7.8 %collective-permute-start = (bf16[64,1536]{1,0:T(8,128)(2,1)}, bf16[64,1536]{1,0:T(8,128)(2,1)}, u32[]{:S(2)}, u32[]{:S(2)}) collective-permute-start(bf16[64,1536]{1,0:T(8,128)(2,1)} %param.4), channel_id=1, source_target_pairs={{0,32},{32,0},{1,33},{33,1},{2,34},{34,2},{3,35},{35,3},{4,36},{36... | collective-permute-start | bytes 589832 | tf_op jit(solution)/shard_map/ppermute | solution.py:27
  21.2 3.3 %collective-permute-start.7 = (bf16[2,2,64,384]{3,2,1,0:T(8,128)(2,1)}, bf16[2,2,64,384]{3,2,1,0:T(8,128)(2,1)S(1)}, u32[]{:S(2)}, u32[]{:S(2)}) collective-permute-start(bf16[2,2,64,384]{3,2,1,0:T(8,128)(2,1)} %get-tuple-element.86), channel_id=1, source_target_pairs={{0,192},{64,0},{128,64},{192,128},{1,193},{65,1},{129,65},{193,129... | collective-permute-start | bytes 589832 | tf_op jit(solution)/shard_map/ppermute | solution.py:27
  25.6 2.5 %collective-permute-start.3 = (bf16[2,64,1536]{2,1,0:T(8,128)(2,1)}, bf16[2,64,1536]{2,1,0:T(8,128)(2,1)S(1)}, u32[]{:S(2)}, u32[]{:S(2)}) collective-permute-start(bf16[2,64,1536]{2,1,0:T(8,128)(2,1)} %pad_maximum_fusion.8), channel_id=1, source_target_pairs={{0,6},{2,0},{4,2},{6,4},{1,7},{3,1},{5,3},{7,5},{8,14},{10,8},{12,... | collective-permute-start | bytes 1179656 | tf_op jit(solution)/shard_map/ppermute | solution.py:27
  28.6 3.8 %collective-permute-done.7 = bf16[2,2,64,384]{3,2,1,0:T(8,128)(2,1)S(1)} collective-permute-done((bf16[2,2,64,384]{3,2,1,0:T(8,128)(2,1)}, bf16[2,2,64,384]{3,2,1,0:T(8,128)(2,1)S(1)}, u32[]{:S(2)}, u32[]{:S(2)}) %collective-permute-start.7) | collective-permute-done | bytes 196640 | tf_op jit(solution)/shard_map/ppermute | solution.py:27
  32.3 4.6 %collective-permute-done.5 = bf16[2,2,64,384]{3,2,1,0:T(8,128)(2,1)S(1)} collective-permute-done((bf16[2,2,64,384]{3,2,1,0:T(8,128)(2,1)S(1)}, bf16[2,2,64,384]{3,2,1,0:T(8,128)(2,1)S(1)}, u32[]{:S(2)}, u32[]{:S(2)}) %collective-permute-start.5) | collective-permute-done | bytes 196640 | tf_op jit(solution)/shard_map/ppermute | solution.py:27
  37.9 15.3 %collective-permute-done.1 = bf16[2,64,1536]{2,1,0:T(8,128)(2,1)S(1)} collective-permute-done((bf16[2,64,1536]{2,1,0:T(8,128)(2,1)}, bf16[2,64,1536]{2,1,0:T(8,128)(2,1)S(1)}, u32[]{:S(2)}, u32[]{:S(2)}) %collective-permute-start.1) | collective-permute-done | bytes 393248 | tf_op jit(solution)/shard_map/ppermute | solution.py:27
  57.5 8.8 %collective-permute-start.10 = (bf16[2,4,64,384]{3,2,1,0:T(8,128)(2,1)}, bf16[2,4,64,384]{3,2,1,0:T(8,128)(2,1)S(1)}, u32[]{:S(2)}, u32[]{:S(2)}) collective-permute-start(bf16[2,4,64,384]{3,2,1,0:T(8,128)(2,1)} %get-tuple-element.84), channel_id=1, source_target_pairs={{0,56},{8,0},{16,8},{24,16},{32,24},{40,32},{48,40},{56,48},{1,57}... | collective-permute-start | bytes 1179656 | tf_op jit(solution)/shard_map/ppermute | solution.py:32
  71.3 12.3 %collective-permute-done.10 = bf16[2,4,64,384]{3,2,1,0:T(8,128)(2,1)S(1)} collective-permute-done((bf16[2,4,64,384]{3,2,1,0:T(8,128)(2,1)}, bf16[2,4,64,384]{3,2,1,0:T(8,128)(2,1)S(1)}, u32[]{:S(2)}, u32[]{:S(2)}) %collective-permute-start.10) | collective-permute-done | bytes 393248 | tf_op jit(solution)/shard_map/ppermute | solution.py:32
  83.6 8.4 %collective-permute-done.11 = bf16[2,4,64,384]{3,2,1,0:T(8,128)(2,1)} collective-permute-done((bf16[2,4,64,384]{3,2,1,0:T(8,128)(2,1)}, bf16[2,4,64,384]{3,2,1,0:T(8,128)(2,1)}, u32[]{:S(2)}, u32[]{:S(2)}) %collective-permute-start.11) | collective-permute-done | bytes 393248 | tf_op jit(solution)/shard_map/ppermute | solution.py:37
  96.0 8.1 %fusion.38 = f32[512,3072]{0,1:T(8,128)S(1)} fusion(bf16[512,1536]{1,0:T(8,128)(2,1)S(1)} %bitcast.211, bf16[3072,1536]{1,0:T(8,128)(2,1)} %param.5), kind=kOutput, calls=%fused_computation.142 | convolution fusion | flops 4831838208 | bytes 17301504 | tf_op jit(solution)/shard_map/dot_general | solution.py:97
  104.3 2.4 %copy-done = f32[512,3072]{0,1:T(8,128)} copy-done((f32[512,3072]{0,1:T(8,128)}, f32[512,3072]{0,1:T(8,128)S(1)}, u32[]{:S(2)}) %copy-start) | copy-done | bytes 6291480
  108.1 7.0 %collective-permute-start.13 = (bf16[2,4,64,384]{3,2,1,0:T(8,128)(2,1)}, bf16[2,4,64,384]{3,2,1,0:T(8,128)(2,1)S(1)}, u32[]{:S(2)}, u32[]{:S(2)}) collective-permute-start(bf16[2,4,64,384]{3,2,1,0:T(8,128)(2,1)} %get-tuple-element.28), channel_id=1, source_target_pairs={{0,8},{8,16},{16,24},{32,40},{40,48},{48,56},{1,9},{9,17},{17,25},... | collective-permute-start | bytes 1179656 | tf_op jit(solution)/shard_map/ppermute | solution.py:32
  117.9 4.8 %collective-permute-done.13 = bf16[2,4,64,384]{3,2,1,0:T(8,128)(2,1)S(1)} collective-permute-done((bf16[2,4,64,384]{3,2,1,0:T(8,128)(2,1)}, bf16[2,4,64,384]{3,2,1,0:T(8,128)(2,1)S(1)}, u32[]{:S(2)}, u32[]{:S(2)}) %collective-permute-start.13) | collective-permute-done | bytes 393248 | tf_op jit(solution)/shard_map/ppermute | solution.py:32
  122.7 3.7 %collective-permute-done.14 = bf16[2,4,64,384]{3,2,1,0:T(8,128)(2,1)S(1)} collective-permute-done((bf16[2,4,64,384]{3,2,1,0:T(8,128)(2,1)}, bf16[2,4,64,384]{3,2,1,0:T(8,128)(2,1)S(1)}, u32[]{:S(2)}, u32[]{:S(2)}) %collective-permute-start.14) | collective-permute-done | bytes 393248 | tf_op jit(solution)/shard_map/ppermute | solution.py:32
  132.2 10.3 %collective-permute-start.8 = (f16[128,3200]{0,1:T(8,128)(2,1)}, f16[128,3200]{0,1:T(8,128)(2,1)S(1)}, u32[]{:S(2)}, u32[]{:S(2)}) collective-permute-start(f16[128,3200]{0,1:T(8,128)(2,1)} %pad_maximum_fusion.5), channel_id=1, source_target_pairs={{0,8},{8,16},{32,40},{40,48},{1,9},{9,17},{33,41},{41,49},{2,10},{... | collective-permute-start | bytes 2457608 | tf_op jit(solution)/shard_map/ppermute | solution.py:32
  142.5 4.1 %collective-permute-done.18 = bf16[2,4,64,384]{3,2,1,0:T(8,128)(2,1)} collective-permute-done((bf16[2,4,64,384]{3,2,1,0:T(8,128)(2,1)}, bf16[2,4,64,384]{3,2,1,0:T(8,128)(2,1)}, u32[]{:S(2)}, u32[]{:S(2)}) %collective-permute-start.18) | collective-permute-done | bytes 393248 | tf_op jit(solution)/shard_map/ppermute | solution.py:37
  147.9 3.3 %select_select_fusion.4 = (bf16[2,4,64,384]{3,2,1,0:T(8,128)(2,1)S(1)}, bf16[2,4,64,384]{3,2,1,0:T(8,128)(2,1)S(1)}, bf16[2,4,64,384]{3,2,1,0:T(8,128)(2,1)S(1)}...) fusion(bf16[2,4,64,384]{3,2,1,0:T(8,128)(2,1)} %collective-perm, ...), kind=kLoop, calls=%fused_computation.68 | loop fusion | flops 3932160 | bytes 6684675 | tf_op jit(solution)/shard_map/select_n | solution.py:130
  155.5 3.1 %collective-permute-start.22 = (bf16[4,4,2,64,1536]{4,3,2,1,0:T(8,128)(2,1)}, bf16[4,4,2,64,1536]{4,3,2,1,0:T(8,128)(2,1)}, u32[]{:S(2)}, u32[]{:S(2)}) collective-permute-start(bf16[4,4,2,64,1536]{4,3,2,1,0:T(8,128)(2,1)} %bitcast.215), channel_id=1, source_target_pairs={{0,1},{1,0},{2,3},{3,2},{4,5},{5,4},{6,7},{7,6},{8,9},{9,8},{10,11... | collective-permute-start | bytes 18874376 | tf_op jit(solution)/shard_map/ppermute | solution.py:27
  158.6 2.4 %abs_reduce_fusion.1 = (f32[128]{0:T(128)S(1)}, f32[128]{0:T(128)S(1)}) fusion(f32[512,3072]{0,1:T(8,128)} %copy-done, f32[128]{0:T(128)S(1)} %exponential_bitcast_fusion.3, f16[128,3200]{0,1:T(8,128)(2,1)S(1)} %collective-permute-done.8, f32[128]{0:T(128)S(1)} %exponential_bitcast_fusion.1, f16[128,3200]{0,1:T(8,128)(2,1)S(1)} %collective-permute-done.19), kind=kLoop, calls=%fused_computation.43 | loop fusion | flops 3931904 | bytes 4720640 | tf_op jit(solution)/shard_map/reduce_max | solution.py:49
  161.0 2.7 %multiply_convert_fusion.1 = (f16[128,3072]{0,1:T(8,128)(2,1)S(1)}, f16[128,3072]{0,1:T(8,128)(2,1)S(1)}) fusion(f32[512,3072]{0,1:T(8,128)} %copy-done, f32[128]{0:T(128)S(1)} %get-tuple-element.113, f32[128]{0:T(128)S(1)} %exponential_bitcast_fusion.3, f16[128,3200]{0,1:T(8,128)(2,1)S(1)} %collective-permute-done.8, f32[128]{0:T(128)S(1)} %get-tuple-element.108, ...), kind=kLoop, calls=%fused_computation.42 | loop fusion | flops 3932160 | bytes 6293504 | tf_op jit(solution)/shard_map/convert_element_type | solution.py:51
  164.0 10.0 %collective-permute-start.12 = (f16[128,3200]{0,1:T(8,128)(2,1)S(1)}, f16[128,3200]{0,1:T(8,128)(2,1)S(1)}, u32[]{:S(2)}, u32[]{:S(2)}) collective-permute-start(f16[128,3200]{0,1:T(8,128)(2,1)S(1)} %pad_maximum_fusion.6), channel_id=1, source_target_pairs={{0,8},{8,16},{16,24},{24,32},{32,40},{40,48},{48,56},{56,0},{1,9},... | collective-permute-start | bytes 2457608 | tf_op jit(solution)/shard_map/ppermute | solution.py:32
  177.3 4.0 %convolution_bitcast_fusion.1 = f32[384,1536]{1,0:T(8,128)} fusion(bf16[4,4,2,64,1536]{4,3,2,1,0:T(8,128)(2,1)S(1)} %bitcast.219, bf16[1,4,2,64,384]{4,3,2,1,0:T(8,128)(2,1)S(1)} %copy-done.22, bf16[1,4,2,64,384]{4,3,1,2,0:T(8,128)(2,1)S(1)} %maximum_bitcast_fusion.1, bf16[1,4,2,64,384]{4,3,1,2,0:T(8,128)(2,1)S(1)} %copy-done.21, ...), kind=kOutput, calls=%fused_computation.9 | convolution fusion | flops 2422407168 | bytes 10223616 | tf_op jit(solution)/shard_map/dot_general | solution.py:150
  181.4 10.3 %collective-permute-done.12 = f16[128,3200]{0,1:T(8,128)(2,1)S(1)} collective-permute-done((f16[128,3200]{0,1:T(8,128)(2,1)S(1)}, f16[128,3200]{0,1:T(8,128)(2,1)S(1)}, u32[]{:S(2)}, u32[]{:S(2)}) %collective-permute-start.12) | collective-permute-done | bytes 819232 | tf_op jit(solution)/shard_map/ppermute | solution.py:32
  200.5 6.9 %fusion.1 = f32[384,1536]{1,0:T(8,128)} fusion(f32[384,1536]{1,0:T(8,128)S(1)} %convolution_add_fusion, bf16[4,4,2,64,1536]{4,3,2,1,0:T(8,128)(2,1)} %collective-permute-done.22, bf16[1,4,2,64,384]{4,3,1,2,0:T(8,128)(2,1)S(1)} %copy-done.20, bf16[1,4,2,64,384]{4,3,1,2,0:T(8,128)(2,1)S(1)} %copy-done.23, ...), kind=kOutput, calls=%fused_computation.11 | convolution fusion | flops 2419458048 | bytes 12582912 | tf_op jit(solution)/shard_map/dot_general | solution.py:150
  (142 shorter events, 49.6 us)
Async XLA Ops:
  7.2 148.3 %all-gather.3.cloned.1.call-start = ((), (), s32[]{:S(2)}) async-start(), calls=%async_computation | async-start | bytes 6684672 | tf_op jit(solution)/shard_map/all_gather | solution.py:84
  7.2 12.2 %collective-permute-start = (bf16[64,1536]{1,0:T(8,128)(2,1)}, bf16[64,1536]{1,0:T(8,128)(2,1)}, u32[]{:S(2)}, u32[]{:S(2)}) collective-permute-start(bf16[64,1536]{1,0:T(8,128)(2,1)} %param.4), channel_id=1, source_target_pairs={{0,32},{32,0},{1,33},{33,1},{2,34},{34,2},{3,35},{35,3},{4,36},{36... | collective-permute-start | bytes 589832 | tf_op jit(solution)/shard_map/ppermute | solution.py:27
  21.2 11.1 %collective-permute-start.7 = (bf16[2,2,64,384]{3,2,1,0:T(8,128)(2,1)}, bf16[2,2,64,384]{3,2,1,0:T(8,128)(2,1)S(1)}, u32[]{:S(2)}, u32[]{:S(2)}) collective-permute-start(bf16[2,2,64,384]{3,2,1,0:T(8,128)(2,1)} %get-tuple-element.86), channel_id=1, source_target_pairs={{0,192},{64,0},{128,64},{192,128},{1,193},{65,1},{129,65},{193,129... | collective-permute-start | bytes 589832 | tf_op jit(solution)/shard_map/ppermute | solution.py:27
  24.5 7.8 %collective-permute-start.6 = (bf16[2,2,64,384]{3,2,1,0:T(8,128)(2,1)}, bf16[2,2,64,384]{3,2,1,0:T(8,128)(2,1)S(1)}, u32[]{:S(2)}, u32[]{:S(2)}) collective-permute-start(bf16[2,2,64,384]{3,2,1,0:T(8,128)(2,1)} %get-tuple-element.87), channel_id=1, source_target_pairs={{0,128},{64,192},{128,0},{192,64},{1,129},{65,193},{129,1},{193,65... | collective-permute-start | bytes 589832 | tf_op jit(solution)/shard_map/ppermute | solution.py:27
  24.9 12.1 %collective-permute-start.5 = (bf16[2,2,64,384]{3,2,1,0:T(8,128)(2,1)S(1)}, bf16[2,2,64,384]{3,2,1,0:T(8,128)(2,1)S(1)}, u32[]{:S(2)}, u32[]{:S(2)}) collective-permute-start(bf16[2,2,64,384]{3,2,1,0:T(8,128)(2,1)S(1)} %get-tuple-element.88), channel_id=1, source_target_pairs={{0,64},{64,128},{128,192},{192,0},{1,65},{65,129},{129,193},{193,1... | collective-permute-start | bytes 589832 | tf_op jit(solution)/shard_map/ppermute | solution.py:27
  25.6 11.6 %collective-permute-start.3 = (bf16[2,64,1536]{2,1,0:T(8,128)(2,1)}, bf16[2,64,1536]{2,1,0:T(8,128)(2,1)S(1)}, u32[]{:S(2)}, u32[]{:S(2)}) collective-permute-start(bf16[2,64,1536]{2,1,0:T(8,128)(2,1)} %pad_maximum_fusion.8), channel_id=1, source_target_pairs={{0,6},{2,0},{4,2},{6,4},{1,7},{3,1},{5,3},{7,5},{8,14},{10,8},{12,... | collective-permute-start | bytes 1179656 | tf_op jit(solution)/shard_map/ppermute | solution.py:27
  28.1 9.9 %collective-permute-start.2 = (bf16[2,64,1536]{2,1,0:T(8,128)(2,1)}, bf16[2,64,1536]{2,1,0:T(8,128)(2,1)S(1)}, u32[]{:S(2)}, u32[]{:S(2)}) collective-permute-start(bf16[2,64,1536]{2,1,0:T(8,128)(2,1)} %pad_maximum_fusion.8), channel_id=1, source_target_pairs={{0,4},{2,6},{4,0},{6,2},{1,5},{3,7},{5,1},{7,3},{8,12},{10,14},{12... | collective-permute-start | bytes 1179656 | tf_op jit(solution)/shard_map/ppermute | solution.py:27
  32.3 20.9 %collective-permute-start.1 = (bf16[2,64,1536]{2,1,0:T(8,128)(2,1)}, bf16[2,64,1536]{2,1,0:T(8,128)(2,1)S(1)}, u32[]{:S(2)}, u32[]{:S(2)}) collective-permute-start(bf16[2,64,1536]{2,1,0:T(8,128)(2,1)} %pad_maximum_fusion.8), channel_id=1, source_target_pairs={{0,2},{2,4},{4,6},{6,0},{1,3},{3,5},{5,7},{7,1},{8,10},{10,12},{12... | collective-permute-start | bytes 1179656 | tf_op jit(solution)/shard_map/ppermute | solution.py:27
  54.7 39.3 %collective-permute-start.4 = (bf16[5,64,1536]{2,1,0:T(8,128)(2,1)}, bf16[5,64,1536]{2,1,0:T(8,128)(2,1)}, u32[]{:S(2)}, u32[]{:S(2)}) collective-permute-start(bf16[5,64,1536]{2,1,0:T(8,128)(2,1)} %get-tuple-element.71), channel_id=1, source_target_pairs={{0,1},{1,0},{2,3},{3,2},{4,5},{5,4},{6,7},{7,6},{8,9},{9,8},{10,11... | collective-permute-start | bytes 2949128 | tf_op jit(solution)/shard_map/ppermute | solution.py:27
  57.5 26.1 %collective-permute-start.10 = (bf16[2,4,64,384]{3,2,1,0:T(8,128)(2,1)}, bf16[2,4,64,384]{3,2,1,0:T(8,128)(2,1)S(1)}, u32[]{:S(2)}, u32[]{:S(2)}) collective-permute-start(bf16[2,4,64,384]{3,2,1,0:T(8,128)(2,1)} %get-tuple-element.84), channel_id=1, source_target_pairs={{0,56},{8,0},{16,8},{24,16},{32,24},{40,32},{48,40},{56,48},{1,57}... | collective-permute-start | bytes 1179656 | tf_op jit(solution)/shard_map/ppermute | solution.py:32
  67.1 16.5 %collective-permute-start.9 = (bf16[2,4,64,384]{3,2,1,0:T(8,128)(2,1)}, bf16[2,4,64,384]{3,2,1,0:T(8,128)(2,1)S(1)}, u32[]{:S(2)}, u32[]{:S(2)}) collective-permute-start(bf16[2,4,64,384]{3,2,1,0:T(8,128)(2,1)} %get-tuple-element.85), channel_id=1, source_target_pairs={{0,8},{8,16},{16,24},{24,32},{32,40},{40,48},{48,56},{56,0},{1,9},... | collective-permute-start | bytes 1179656 | tf_op jit(solution)/shard_map/ppermute | solution.py:32
  67.1 24.9 %collective-permute-start.11 = (bf16[2,4,64,384]{3,2,1,0:T(8,128)(2,1)}, bf16[2,4,64,384]{3,2,1,0:T(8,128)(2,1)}, u32[]{:S(2)}, u32[]{:S(2)}) collective-permute-start(bf16[2,4,64,384]{3,2,1,0:T(8,128)(2,1)} %pad_maximum_fusion.10), channel_id=1, source_target_pairs={{0,48},{8,56},{16,32},{24,40},{32,16},{40,24},{48,0},{56,8},{1,49}... | collective-permute-start | bytes 1179656 | tf_op jit(solution)/shard_map/ppermute | solution.py:37
  108.1 14.6 %collective-permute-start.13 = (bf16[2,4,64,384]{3,2,1,0:T(8,128)(2,1)}, bf16[2,4,64,384]{3,2,1,0:T(8,128)(2,1)S(1)}, u32[]{:S(2)}, u32[]{:S(2)}) collective-permute-start(bf16[2,4,64,384]{3,2,1,0:T(8,128)(2,1)} %get-tuple-element.28), channel_id=1, source_target_pairs={{0,8},{8,16},{16,24},{32,40},{40,48},{48,56},{1,9},{9,17},{17,25},... | collective-permute-start | bytes 1179656 | tf_op jit(solution)/shard_map/ppermute | solution.py:32
  115.1 11.3 %collective-permute-start.14 = (bf16[2,4,64,384]{3,2,1,0:T(8,128)(2,1)}, bf16[2,4,64,384]{3,2,1,0:T(8,128)(2,1)S(1)}, u32[]{:S(2)}, u32[]{:S(2)}) collective-permute-start(bf16[2,4,64,384]{3,2,1,0:T(8,128)(2,1)} %get-tuple-element.29), channel_id=1, source_target_pairs={{24,16},{16,8},{8,0},{56,48},{48,40},{40,32},{25,17},{17,9},{9,1},... | collective-permute-start | bytes 1179656 | tf_op jit(solution)/shard_map/ppermute | solution.py:32
  116.4 12.4 %collective-permute-start.15 = (bf16[2,4,64,384]{3,2,1,0:T(8,128)(2,1)}, bf16[2,4,64,384]{3,2,1,0:T(8,128)(2,1)}, u32[]{:S(2)}, u32[]{:S(2)}) collective-permute-start(bf16[2,4,64,384]{3,2,1,0:T(8,128)(2,1)} %collective-permute-done.11), channel_id=1, source_target_pairs={{8,16},{16,8},{40,48},{48,40},{9,17},{17,9},{41,49},{49,41},{10,18... | collective-permute-start | bytes 1179656 | tf_op jit(solution)/shard_map/ppermute | solution.py:37
  127.5 19.1 %collective-permute-start.17 = (bf16[2,4,64,384]{3,2,1,0:T(8,128)(2,1)}, bf16[2,4,64,384]{3,2,1,0:T(8,128)(2,1)}, u32[]{:S(2)}, u32[]{:S(2)}) collective-permute-start(bf16[2,4,64,384]{3,2,1,0:T(8,128)(2,1)} %get-tuple-element.82), channel_id=1, source_target_pairs={{8,0},{16,24},{40,32},{48,56},{9,1},{17,25},{41,33},{49,57},{10,2}... | collective-permute-start | bytes 1179656 | tf_op jit(solution)/shard_map/ppermute | solution.py:37
  128.8 17.8 %collective-permute-start.18 = (bf16[2,4,64,384]{3,2,1,0:T(8,128)(2,1)}, bf16[2,4,64,384]{3,2,1,0:T(8,128)(2,1)}, u32[]{:S(2)}, u32[]{:S(2)}) collective-permute-start(bf16[2,4,64,384]{3,2,1,0:T(8,128)(2,1)} %collective-permute-done.15), channel_id=1, source_target_pairs={{8,0},{16,24},{40,32},{48,56},{9,1},{17,25},{41,33},{49,57},{10,2}... | collective-permute-start | bytes 1179656 | tf_op jit(solution)/shard_map/ppermute | solution.py:37
  130.1 16.5 %collective-permute-start.16 = (bf16[2,4,64,384]{3,2,1,0:T(8,128)(2,1)}, bf16[2,4,64,384]{3,2,1,0:T(8,128)(2,1)}, u32[]{:S(2)}, u32[]{:S(2)}) collective-permute-start(bf16[2,4,64,384]{3,2,1,0:T(8,128)(2,1)} %get-tuple-element.83), channel_id=1, source_target_pairs={{8,16},{16,8},{40,48},{48,40},{9,17},{17,9},{41,49},{49,41},{10,18... | collective-permute-start | bytes 1179656 | tf_op jit(solution)/shard_map/ppermute | solution.py:37
  131.5 23.9 %collective-permute-start.19 = (f16[128,3200]{0,1:T(8,128)(2,1)}, f16[128,3200]{0,1:T(8,128)(2,1)S(1)}, u32[]{:S(2)}, u32[]{:S(2)}) collective-permute-start(f16[128,3200]{0,1:T(8,128)(2,1)} %pad_maximum_fusion.5), channel_id=1, source_target_pairs={{16,8},{24,16},{48,40},{56,48},{17,9},{25,17},{49,41},{57,49},{18,... | collective-permute-start | bytes 2457608 | tf_op jit(solution)/shard_map/ppermute | solution.py:32
  132.2 26.3 %collective-permute-start.8 = (f16[128,3200]{0,1:T(8,128)(2,1)}, f16[128,3200]{0,1:T(8,128)(2,1)S(1)}, u32[]{:S(2)}, u32[]{:S(2)}) collective-permute-start(f16[128,3200]{0,1:T(8,128)(2,1)} %pad_maximum_fusion.5), channel_id=1, source_target_pairs={{0,8},{8,16},{32,40},{40,48},{1,9},{9,17},{33,41},{41,49},{2,10},{... | collective-permute-start | bytes 2457608 | tf_op jit(solution)/shard_map/ppermute | solution.py:32
  146.6 28.0 %collective-permute-start.21 = (bf16[2,4,64,384]{3,2,1,0:T(8,128)(2,1)}, bf16[2,4,64,384]{3,2,1,0:T(8,128)(2,1)}, u32[]{:S(2)}, u32[]{:S(2)}) collective-permute-start(bf16[2,4,64,384]{3,2,1,0:T(8,128)(2,1)} %collective-permute-done.16), channel_id=1, source_target_pairs={{8,0},{16,24},{40,32},{48,56},{9,1},{17,25},{41,33},{49,57},{10,2}... | collective-permute-start | bytes 1179656 | tf_op jit(solution)/shard_map/ppermute | solution.py:37
  155.5 44.7 %collective-permute-start.22 = (bf16[4,4,2,64,1536]{4,3,2,1,0:T(8,128)(2,1)}, bf16[4,4,2,64,1536]{4,3,2,1,0:T(8,128)(2,1)}, u32[]{:S(2)}, u32[]{:S(2)}) collective-permute-start(bf16[4,4,2,64,1536]{4,3,2,1,0:T(8,128)(2,1)} %bitcast.215), channel_id=1, source_target_pairs={{0,1},{1,0},{2,3},{3,2},{4,5},{5,4},{6,7},{7,6},{8,9},{9,8},{10,11... | collective-permute-start | bytes 18874376 | tf_op jit(solution)/shard_map/ppermute | solution.py:27
  164.0 27.7 %collective-permute-start.12 = (f16[128,3200]{0,1:T(8,128)(2,1)S(1)}, f16[128,3200]{0,1:T(8,128)(2,1)S(1)}, u32[]{:S(2)}, u32[]{:S(2)}) collective-permute-start(f16[128,3200]{0,1:T(8,128)(2,1)S(1)} %pad_maximum_fusion.6), channel_id=1, source_target_pairs={{0,8},{8,16},{16,24},{24,32},{32,40},{40,48},{48,56},{56,0},{1,9},... | collective-permute-start | bytes 2457608 | tf_op jit(solution)/shard_map/ppermute | solution.py:32
  174.2 19.8 %collective-permute-start.20 = (f16[128,3200]{0,1:T(8,128)(2,1)S(1)}, f16[128,3200]{0,1:T(8,128)(2,1)S(1)}, u32[]{:S(2)}, u32[]{:S(2)}) collective-permute-start(f16[128,3200]{0,1:T(8,128)(2,1)S(1)} %pad_maximum_fusion.7), channel_id=1, source_target_pairs={{0,56},{8,0},{16,8},{24,16},{32,24},{40,32},{48,40},{56,48},{1,57}... | collective-permute-start | bytes 2457608 | tf_op jit(solution)/shard_map/ppermute | solution.py:32
  (28 other events, 254.1 us)
Sparse Core Ops, SparseCore 0:
  21.3 76.0 all-gather.2

commit v4 on v3

--- a/solution.py
+++ b/solution.py
@@ -66,6 +66,7 @@
     block = hidden // 8
     grad_scale = 1.0 / math.sqrt(tokens * 32)
 
+    from_x = [grad_out] + [shift(grad_out, "x", t) for t in (1, 2, 3)]
     p = shift(grad_out, "zh", 1)
     gelu_value, gelu_slope = gelu_parts(pre_act.astype(jnp.float32))
     act, gelu_slope = lax.optimization_barrier((gelu_value.astype(jnp.bfloat16), gelu_slope))
@@ -83,48 +84,53 @@
     both = after(jnp.stack([grad_out, p]), *pieces_out)
     all_rows = lax.all_gather(both, ("x", "y")).reshape(4, 4, 2, half, feats)
 
-    from_x = jnp.stack([both] + [shift(both, "x", t) for t in (1, 2, 3)])
-    beyond = at(from_x[:, 1], jnp.where(zl == 0, x - 3, x) % 4)
-    mine = jnp.concatenate([from_x[:, 0], beyond[None]])
+    mine = after(jnp.stack(from_x), *pieces_out)
     mine = jnp.stack([mine, shift(mine, "core", 1)], axis=1)
-    mine = after(mine, own, cross)
 
-    place = [(x - zl - k) % 4 for k in (2, 1, -1, 0)]
-    place[1] = jnp.where(zl == 3, 4, place[1])
-    place[2] = jnp.where(zl == 0, 4, place[2])
-    rows = jnp.stack([at(mine, k) for k in place])
-    rows = jnp.where(c == 1, rows[:, ::-1], rows).reshape(4 * tokens, feats)
-    parts = lax.dot_general(
-        rows, down_weight, (((1,), (1,)), ((), ())), preferred_element_type=jnp.float32
-    )
-    part_far, part_up, part_down, part_own = (
-        parts[k * tokens : (k + 1) * tokens] for k in range(4)
-    )
-    far = pack(part_far)
+    def partial(*blocks):
+        rows = jnp.stack(blocks)
+        rows = jnp.where(c == 1, rows[:, ::-1], rows).reshape(-1, feats)
+        sums = lax.dot_general(
+            rows, down_weight, (((1,), (1,)), ((), ())), preferred_element_type=jnp.float32
+        )
+        return [sums[k * tokens : (k + 1) * tokens] for k in range(len(blocks))]
+
+    part_far, part_own = partial(*(at(mine, (x - zl - k) % 4) for k in (2, 0)))
+    far = after(pack(part_far), own, cross)
 
     e0, e3 = zl == 0, zl == 3
+    far_up = along_z(far, 1, (0, 1))
+    far_down = along_z(far, -1, (2, 3))
     a_up = along_z(jnp.where(e3, cross, own), 1, range(4))
     a_down = along_z(jnp.where(e0, cross, own), -1, range(4))
     b = pairs_z(cross, {0: -2, 1: -2, 2: 2, 3: 2})
-    far_up = along_z(far, 1, (0, 1))
-    far_down = along_z(far, -1, (2, 3))
-    c_up = along_z(after(jnp.where(e0, b, a_up), far), 1, (0, 1, 2))
-    c_down = along_z(after(jnp.where(e3, b, a_down), far), -1, (3, 2, 1))
-    d = pairs_z(after(b, far), {1: 1, 2: -1})
-    near_up = pack(part_up + unpack(after(far_up, a_up, a_down, b)))
-    near_down = pack(part_down + unpack(after(far_down, a_up, a_down, b)))
+
+    q = jnp.where(jnp.where(e0, x == 3, x == 0), p, jnp.zeros_like(p))
+    for t in (1, 2, 3):
+        q = q + lax.ppermute(p, ("zl", "x"), [(3, (3 + t) % 4), (12, 12 + t)])
+    beyond = jnp.stack([q, shift(q, "core", 1)])
+    up, down = (at(mine, (x - zl - k) % 4) for k in (1, -1))
+    part_up, part_down = partial(jnp.where(e3, beyond, up), jnp.where(e0, beyond, down))
+
+    far_up, far_down, a_up, a_down, b, part_up, part_down = lax.optimization_barrier(
+        (far_up, far_down, a_up, a_down, b, part_up, part_down)
+    )
+    near_up = pack(part_up + unpack(far_up))
+    near_down = pack(part_down + unpack(far_down))
     from_below = along_z(near_up, 1, range(4))
     from_above = along_z(near_down, -1, range(4))
+    c_up = along_z(jnp.where(e0, b, a_up), 1, (0, 1, 2))
+    c_down = along_z(jnp.where(e3, b, a_down), -1, (3, 2, 1))
+    d = pairs_z(b, {1: 1, 2: -1})
+
+    c_up, c_down, d = lax.optimization_barrier((c_up, c_down, d, near_up, near_down))[:3]
     e = pairs_z(jnp.where(zl == 1, c_up, c_down), {1: 1, 2: -1})
     f = pairs_z(jnp.where(zl == 2, c_up, c_down), {1: -1, 2: 1})
     g = pairs_z(d, {1: -1, 2: 1})
+
+    e, f, g, all_rows = lax.optimization_barrier((e, f, g, all_rows))
     h = pairs_z(e, {1: -1, 2: 1})
-
-    all_rows = after(all_rows, e, f, g)
     other_rows = shift(all_rows, "core", 1)
-    own, a_up, a_down, b, c_up, c_down, d, e, f, g = lax.optimization_barrier(
-        (own, a_up, a_down, b, c_up, c_down, d, e, f, g)
-    )
 
     def choose(*units):
         return lax.select_n(zl, *units)

time: 215 us -> 194 us (0.902); the launches traced: 214 us -> 191 us
  waiting for transfers between devices: 70.7 us -> 59.5 us
  other arithmetic: 31.1 us -> 23 us
  starting transfers between devices: 67.4 us -> 61.4 us
  matrix products: 19.8 us -> 22.4 us
    ppermute x9 -> x10, waiting for transfers between devices: 24.6 us -> 0.48 us  [shift(): return lax.ppermute(v, axis, [(i, (i + step) % n) for i in range(n)])]
    ppermute x6, waiting for transfers between devices: 12.5 us -> 30.9 us  [pairs_z(): return lax.ppermute(v, Z, pairs)]
    ppermute x8, starting transfers between devices: 38.4 us -> 24.6 us  [along_z(): return lax.ppermute(v, Z, pairs)]
    ppermute x8, waiting for transfers between devices: 33.6 us -> 20.1 us  [along_z(): return lax.ppermute(v, Z, pairs)]
    ppermute x0 -> x3, waiting for transfers between devices: none -> 7.96 us  [on_device(): q = q + lax.ppermute(p, ('zl', 'x'), [(3, (3 + t) % 4), (12, 12 + t)])]
    ppermute x9 -> x10, starting transfers between devices: 20 us -> 27.2 us  [shift(): return lax.ppermute(v, axis, [(i, (i + step) % n) for i in range(n)])]
    ppermute x0 -> x3, starting transfers between devices: none -> 2.64 us  [on_device(): q = q + lax.ppermute(p, ('zl', 'x'), [(3, (3 + t) % 4), (12, 12 + t)])]
    another operation x2 -> x1, other arithmetic: 2.66 us -> 0.06 us  [on_device(): jnp.stack([lax.select_n((y - k) % 4, *[v[i] for v in pieces]) for k in ra...]
  transfers between devices with their start and end apart: 24 -> 28, of which waited for: 12 -> 10; matrix products, arithmetic and copies ran while one was open for 23% -> 24% of each run, Pallas kernels for 0% -> 0%
where the time goes in v4:
time: 194 us; the launch traced here: 191 us
  starting transfers between devices  61.4 us (32%)
  waiting for transfers between devices  59.5 us (31%)
  other arithmetic  23 us (12%)
  matrix products  22.4 us (12%)
  between operations  14.8 us (8%)
  local copies, waits for them, and re-layouts  9.46 us (5%)
    ppermute x6, waiting for transfers between devices, pairs_z(): return lax.ppermute(v, Z, pairs)  30.9 us
    ppermute x10, starting transfers between devices, shift(): return lax.ppermute(v, axis, [(i, (i + step) % n) for i in range(n)])  27.2 us
    ppermute x8, starting transfers between devices, along_z(): return lax.ppermute(v, Z, pairs)  24.6 us
    ppermute x8, waiting for transfers between devices, along_z(): return lax.ppermute(v, Z, pairs)  20.1 us
    dot_general x3, matrix products, product(): lax.dot_general(unit.reshape(-1, block), rows.reshape(-1, feats), (((0,),...  13.5 us
    dot_general x2, matrix products, partial(): lax.dot_general(rows, down_weight, (((1,), (1,)), ((), ())), preferred_el...  8.95 us
    ppermute x3, waiting for transfers between devices, on_device(): q = q + lax.ppermute(p, ('zl', 'x'), [(3, (3 + t) % 4), (12, 12 + t)])  7.96 us
    ppermute x6, starting transfers between devices, pairs_z(): return lax.ppermute(v, Z, pairs)  6.96 us
  transfers between devices with their start and end apart: 28, of which 10 were waited for; matrix products, arithmetic and copies ran while one was open for 24% of the time, Pallas kernels for 0%

profile of v4, /device:TPU:1, one launch (start us, length us, event | category | flops | bytes accessed | tf_op | source)
XLA Modules:
  0.0 190.6 jit_solution(15168122443668430976)
XLA Ops:
  7.2 3.4 %collective-permute-start.2 = (bf16[64,1536]{1,0:T(8,128)(2,1)}, bf16[64,1536]{1,0:T(8,128)(2,1)S(1)}, u32[]{:S(2)}, u32[]{:S(2)}) collective-permute-start(bf16[64,1536]{1,0:T(8,128)(2,1)} %param.4), channel_id=1, source_target_pairs={{0,6},{2,0},{4,2},{6,4},{1,7},{3,1},{5,3},{7,5},{8,14},{10,8},{12,... | collective-permute-start | bytes 589832 | tf_op jit(solution)/shard_map/ppermute | solution.py:27
  11.7 6.9 %collective-permute-start.12 = (bf16[64,1536]{1,0:T(8,128)(2,1)}, bf16[64,1536]{1,0:T(8,128)(2,1)S(1)}, u32[]{:S(2)}, u32[]{:S(2)}) collective-permute-start(bf16[64,1536]{1,0:T(8,128)(2,1)} %param.4), channel_id=1, source_target_pairs={{0,32},{32,0},{1,33},{33,1},{2,34},{34,2},{3,35},{35,3},{4,36},{36... | collective-permute-start | bytes 589832 | tf_op jit(solution)/shard_map/ppermute | solution.py:27
  20.1 2.2 %fusion.7 = (f32[128,3072]{0,1:T(8,128)}, bf16[128,3072]{0,1:T(8,128)(2,1)S(1)}) fusion(bf16[128,3072]{0,1:T(8,128)(2,1)S(1)} %copy.57), kind=kLoop, calls=%fused_computation.25 | loop fusion | flops 7864320 | bytes 3145728 | tf_op jit(solution)/shard_map/add | solution.py:19
  28.4 2.7 %collective-permute-start.3 = (bf16[4,64,1536]{2,1,0:T(8,128)(2,1)S(1)}, bf16[4,64,1536]{2,1,0:T(8,128)(2,1)}, u32[]{:S(2)}, u32[]{:S(2)}) collective-permute-start(bf16[4,64,1536]{2,1,0:T(8,128)(2,1)S(1)} %pad_maximum_fusion.4), channel_id=1, source_target_pairs={{0,1},{1,0},{2,3},{3,2},{4,5},{5,4},{6,7},{7,6},{8,9},{9,8},{10,11... | collective-permute-start | bytes 2359304 | tf_op jit(solution)/shard_map/ppermute | solution.py:27
  35.4 8.0 %collective-permute-done.13 = bf16[64,1536]{1,0:T(8,128)(2,1)S(1)} collective-permute-done((bf16[64,1536]{1,0:T(8,128)(2,1)S(1)}, bf16[64,1536]{1,0:T(8,128)(2,1)S(1)}, u32[]{:S(2)}, u32[]{:S(2)}) %collective-permute-start.13) | collective-permute-done | bytes 196640 | tf_op jit(solution)/shard_map/ppermute | solution.py:110
  43.4 2.4 %collective-permute-start.16 = (bf16[64,1536]{1,0:T(8,128)(2,1)S(1)}, bf16[64,1536]{1,0:T(8,128)(2,1)S(1)}, u32[]{:S(2)}, u32[]{:S(2)}) collective-permute-start(bf16[64,1536]{1,0:T(8,128)(2,1)S(1)} %add_add_fusion), channel_id=1, source_target_pairs={{0,1},{1,0},{2,3},{3,2},{4,5},{5,4},{6,7},{7,6},{8,9},{9,8},{10,11... | collective-permute-start | bytes 589832 | tf_op jit(solution)/shard_map/ppermute | solution.py:27
  46.0 2.7 %collective-permute-start.10 = (bf16[2,4,64,384]{3,2,1,0:T(8,128)(2,1)S(1)}, bf16[2,4,64,384]{3,2,1,0:T(8,128)(2,1)S(1)}, u32[]{:S(2)}, u32[]{:S(2)}) collective-permute-start(bf16[2,4,64,384]{3,2,1,0:T(8,128)(2,1)S(1)} %get-tuple-element.73), channel_id=1, source_target_pairs={{0,56},{8,0},{16,8},{24,16},{32,24},{40,32},{48,40},{56,48},{1,57}... | collective-permute-start | bytes 1179656 | tf_op jit(solution)/shard_map/ppermute | solution.py:32
  51.0 6.3 %fusion.44 = f32[256,3072]{0,1:T(8,128)S(1)} fusion(bf16[256,1536]{1,0:T(8,128)(2,1)S(1)} %bitcast.213, bf16[3072,1536]{1,0:T(8,128)(2,1)} %param.5), kind=kOutput, calls=%fused_computation.153 | convolution fusion | flops 2415919104 | bytes 13369344 | tf_op jit(solution)/shard_map/dot_general | solution.py:93
  57.8 3.1 %collective-permute-start.7 = (f16[128,3200]{0,1:T(8,128)(2,1)S(1)}, f16[128,3200]{0,1:T(8,128)(2,1)S(1)}, u32[]{:S(2)}, u32[]{:S(2)}) collective-permute-start(f16[128,3200]{0,1:T(8,128)(2,1)S(1)} %pad_maximum_fusion.1), channel_id=1, source_target_pairs={{0,8},{8,16},{32,40},{40,48},{1,9},{9,17},{33,41},{41,49},{2,10},{... | collective-permute-start | bytes 2457608 | tf_op jit(solution)/shard_map/ppermute | solution.py:32
  61.7 2.6 %fusion.45 = f32[256,3072]{0,1:T(8,128)S(1)} fusion(bf16[256,1536]{1,0:T(8,128)(2,1)S(1)} %bitcast.212, bf16[3072,1536]{1,0:T(8,128)(2,1)S(1)} %bitcast.224), kind=kOutput, calls=%fused_computation.154 | convolution fusion | flops 2415919104 | bytes 13369344 | tf_op jit(solution)/shard_map/dot_general | solution.py:93
  66.4 7.4 %collective-permute-done.11 = bf16[2,4,64,384]{3,2,1,0:T(8,128)(2,1)S(1)} collective-permute-done((bf16[2,4,64,384]{3,2,1,0:T(8,128)(2,1)S(1)}, bf16[2,4,64,384]{3,2,1,0:T(8,128)(2,1)S(1)}, u32[]{:S(2)}, u32[]{:S(2)}) %collective-permute-start.11) | collective-permute-done | bytes 393248 | tf_op jit(solution)/shard_map/ppermute | solution.py:37
  73.8 12.5 %collective-permute-done.7 = f16[128,3200]{0,1:T(8,128)(2,1)S(1)} collective-permute-done((f16[128,3200]{0,1:T(8,128)(2,1)S(1)}, f16[128,3200]{0,1:T(8,128)(2,1)S(1)}, u32[]{:S(2)}, u32[]{:S(2)}) %collective-permute-start.7) | collective-permute-done | bytes 819232 | tf_op jit(solution)/shard_map/ppermute | solution.py:32
  87.8 10.3 %collective-permute-start.18 = (bf16[2,4,64,384]{3,2,1,0:T(8,128)(2,1)S(1)}, bf16[2,4,64,384]{3,2,1,0:T(8,128)(2,1)}, u32[]{:S(2)}, u32[]{:S(2)}) collective-permute-start(bf16[2,4,64,384]{3,2,1,0:T(8,128)(2,1)S(1)} %get-tuple-element.96), channel_id=1, source_target_pairs={{0,8},{8,16},{16,24},{32,40},{40,48},{48,56},{1,9},{9,17},{17,25},... | collective-permute-start | bytes 1179656 | tf_op jit(solution)/shard_map/ppermute | solution.py:32
  104.1 4.6 %collective-permute-done.19 = bf16[2,4,64,384]{3,2,1,0:T(8,128)(2,1)S(1)} collective-permute-done((bf16[2,4,64,384]{3,2,1,0:T(8,128)(2,1)S(1)}, bf16[2,4,64,384]{3,2,1,0:T(8,128)(2,1)S(1)}, u32[]{:S(2)}, u32[]{:S(2)}) %collective-permute-start.19) | collective-permute-done | bytes 393248 | tf_op jit(solution)/shard_map/ppermute | solution.py:32
  115.6 6.3 %collective-permute-start.17 = (f16[128,3200]{0,1:T(8,128)(2,1)}, f16[128,3200]{0,1:T(8,128)(2,1)}, u32[]{:S(2)}, u32[]{:S(2)}) collective-permute-start(f16[128,3200]{0,1:T(8,128)(2,1)} %pad_maximum_fusion.2), channel_id=1, source_target_pairs={{0,8},{8,16},{16,24},{24,32},{32,40},{40,48},{48,56},{56,0},{1,9},... | collective-permute-start | bytes 2457608 | tf_op jit(solution)/shard_map/ppermute | solution.py:32
  121.9 4.4 %collective-permute-done.22 = bf16[2,4,64,384]{3,2,1,0:T(8,128)(2,1)} collective-permute-done((bf16[2,4,64,384]{3,2,1,0:T(8,128)(2,1)}, bf16[2,4,64,384]{3,2,1,0:T(8,128)(2,1)}, u32[]{:S(2)}, u32[]{:S(2)}) %collective-permute-start.22) | collective-permute-done | bytes 393248 | tf_op jit(solution)/shard_map/ppermute | solution.py:37
  126.2 8.4 %collective-permute-done.23 = bf16[2,4,64,384]{3,2,1,0:T(8,128)(2,1)} collective-permute-done((bf16[2,4,64,384]{3,2,1,0:T(8,128)(2,1)}, bf16[2,4,64,384]{3,2,1,0:T(8,128)(2,1)}, u32[]{:S(2)}, u32[]{:S(2)}) %collective-permute-start.23) | collective-permute-done | bytes 393248 | tf_op jit(solution)/shard_map/ppermute | solution.py:37
  136.0 6.3 %collective-permute-start.26 = (bf16[4,4,2,64,1536]{4,3,2,1,0:T(8,128)(2,1)}, bf16[4,4,2,64,1536]{4,3,2,1,0:T(8,128)(2,1)}, u32[]{:S(2)}, u32[]{:S(2)}) collective-permute-start(bf16[4,4,2,64,1536]{4,3,2,1,0:T(8,128)(2,1)} %bitcast.214), channel_id=1, source_target_pairs={{0,1},{1,0},{2,3},{3,2},{4,5},{5,4},{6,7},{7,6},{8,9},{9,8},{10,11... | collective-permute-start | bytes 18874376 | tf_op jit(solution)/shard_map/ppermute | solution.py:27
  149.8 10.7 %collective-permute-done.25 = bf16[2,4,64,384]{3,2,1,0:T(8,128)(2,1)S(1)} collective-permute-done((bf16[2,4,64,384]{3,2,1,0:T(8,128)(2,1)}, bf16[2,4,64,384]{3,2,1,0:T(8,128)(2,1)S(1)}, u32[]{:S(2)}, u32[]{:S(2)}) %collective-permute-start.25) | collective-permute-done | bytes 393248 | tf_op jit(solution)/shard_map/ppermute | solution.py:37
  162.5 4.0 %convolution_bitcast_fusion.1 = f32[384,1536]{1,0:T(8,128)} fusion(bf16[4,4,2,64,1536]{4,3,2,1,0:T(8,128)(2,1)S(1)} %bitcast.218, bf16[1,4,2,64,384]{4,3,2,1,0:T(8,128)(2,1)S(1)} %maximum_bitcast_fusion.3, bf16[1,4,2,64,384]{4,3,1,2,0:T(8,128)(2,1)S(1)} %maximum_bitcast_fusion.1, bf16[1,4,2,64,384]{4,3,1,2,0:T(8,128)(2,1)S(1)} %maximum_bitcast_fusion, ...), kind=kOutput, calls=%fused_computation.9 | convolution fusion | flops 2422407168 | bytes 10223616 | tf_op jit(solution)/shard_map/dot_general | solution.py:156
  167.9 2.7 %fusion.13 = bf16[128,3072]{0,1:T(8,128)(2,1)} fusion(f32[128,3072]{0,1:T(8,128)S(1)} %copy-done, f32[256,3072]{0,1:T(8,128)S(1)} %fusion.44, f32[128]{0:T(128)S(1)} %exponential_bitcast_fusion, f16[128,3200]{0,1:T(8,128)(2,1)} %collective-permute-done.24, f32[128]{0:T(128)S(1)} %exponential_bitcast_fusion.1, f16[128,3200]{0,1:T(8,128)(2,1)} %collective-permute-done.17), kind=kLoop, calls=%fused_computation.32 | loop fusion | flops 3145728 | bytes 5506048 | tf_op jit(solution)/shard_map/convert_element_type | solution.py:167
  170.7 2.4 %copy.80 = bf16[128,3072]{1,0:T(8,128)(2,1)} copy(bf16[128,3072]{0,1:T(8,128)(2,1)} %fusion.13) | data formatting | bytes 1572864
  174.2 2.5 %convolution_add_fusion = f32[384,1536]{1,0:T(8,128)S(1)} fusion(f32[384,1536]{1,0:T(8,128)} %convolution_bitcast_fusion.1, bf16[512,384]{1,0:T(8,128)(2,1)S(1)} %bitcast.207, bf16[512,1536]{1,0:T(8,128)(2,1)S(1)} %bitcast.203), kind=kOutput, calls=%fused_computation.7 | convolution fusion | flops 604569600 | bytes 6684672 | tf_op jit(solution)/shard_map/dot_general | solution.py:156
  176.8 6.9 %fusion.1 = f32[384,1536]{1,0:T(8,128)} fusion(f32[384,1536]{1,0:T(8,128)S(1)} %convolution_add_fusion, bf16[4,4,2,64,1536]{4,3,2,1,0:T(8,128)(2,1)} %collective-permute-done.26, bf16[1,4,2,64,384]{4,3,1,2,0:T(8,128)(2,1)S(1)} %copy-done.17, bf16[1,4,2,64,384]{4,3,1,2,0:T(8,128)(2,1)S(1)} %maximum_bitcast_fusion.6, ...), kind=kOutput, calls=%fused_computation.11 | convolution fusion | flops 2419458048 | bytes 12582912 | tf_op jit(solution)/shard_map/dot_general | solution.py:156
  (149 shorter events, 45.8 us)
Async XLA Ops:
  7.2 127.5 %all-gather.3.cloned.1.call-start = ((), (), s32[]{:S(2)}) async-start(), calls=%async_computation | async-start | bytes 6684672 | tf_op jit(solution)/shard_map/all_gather | solution.py:85
  7.2 18.0 %collective-permute-start.2 = (bf16[64,1536]{1,0:T(8,128)(2,1)}, bf16[64,1536]{1,0:T(8,128)(2,1)S(1)}, u32[]{:S(2)}, u32[]{:S(2)}) collective-permute-start(bf16[64,1536]{1,0:T(8,128)(2,1)} %param.4), channel_id=1, source_target_pairs={{0,6},{2,0},{4,2},{6,4},{1,7},{3,1},{5,3},{7,5},{8,14},{10,8},{12,... | collective-permute-start | bytes 589832 | tf_op jit(solution)/shard_map/ppermute | solution.py:27
  10.6 16.1 %collective-permute-start.1 = (bf16[64,1536]{1,0:T(8,128)(2,1)}, bf16[64,1536]{1,0:T(8,128)(2,1)S(1)}, u32[]{:S(2)}, u32[]{:S(2)}) collective-permute-start(bf16[64,1536]{1,0:T(8,128)(2,1)} %param.4), channel_id=1, source_target_pairs={{0,4},{2,6},{4,0},{6,2},{1,5},{3,7},{5,1},{7,3},{8,12},{10,14},{12... | collective-permute-start | bytes 589832 | tf_op jit(solution)/shard_map/ppermute | solution.py:27
  11.1 17.2 %collective-permute-start = (bf16[64,1536]{1,0:T(8,128)(2,1)}, bf16[64,1536]{1,0:T(8,128)(2,1)S(1)}, u32[]{:S(2)}, u32[]{:S(2)}) collective-permute-start(bf16[64,1536]{1,0:T(8,128)(2,1)} %param.4), channel_id=1, source_target_pairs={{0,2},{2,4},{4,6},{6,0},{1,3},{3,5},{5,7},{7,1},{8,10},{10,12},{12... | collective-permute-start | bytes 589832 | tf_op jit(solution)/shard_map/ppermute | solution.py:27
  11.7 19.4 %collective-permute-start.12 = (bf16[64,1536]{1,0:T(8,128)(2,1)}, bf16[64,1536]{1,0:T(8,128)(2,1)S(1)}, u32[]{:S(2)}, u32[]{:S(2)}) collective-permute-start(bf16[64,1536]{1,0:T(8,128)(2,1)} %param.4), channel_id=1, source_target_pairs={{0,32},{32,0},{1,33},{33,1},{2,34},{34,2},{3,35},{35,3},{4,36},{36... | collective-permute-start | bytes 589832 | tf_op jit(solution)/shard_map/ppermute | solution.py:27
  23.9 8.7 %collective-permute-start.4 = (bf16[2,2,64,384]{3,2,1,0:T(8,128)(2,1)}, bf16[2,2,64,384]{3,2,1,0:T(8,128)(2,1)S(1)}, u32[]{:S(2)}, u32[]{:S(2)}) collective-permute-start(bf16[2,2,64,384]{3,2,1,0:T(8,128)(2,1)} %get-tuple-element.77), channel_id=1, source_target_pairs={{0,64},{64,128},{128,192},{192,0},{1,65},{65,129},{129,193},{193,1... | collective-permute-start | bytes 589832 | tf_op jit(solution)/shard_map/ppermute | solution.py:27
  26.7 8.4 %collective-permute-start.5 = (bf16[2,2,64,384]{3,2,1,0:T(8,128)(2,1)S(1)}, bf16[2,2,64,384]{3,2,1,0:T(8,128)(2,1)S(1)}, u32[]{:S(2)}, u32[]{:S(2)}) collective-permute-start(bf16[2,2,64,384]{3,2,1,0:T(8,128)(2,1)S(1)} %get-tuple-element.76), channel_id=1, source_target_pairs={{0,128},{64,192},{128,0},{192,64},{1,129},{65,193},{129,1},{193,65... | collective-permute-start | bytes 589832 | tf_op jit(solution)/shard_map/ppermute | solution.py:27
  28.4 20.6 %collective-permute-start.3 = (bf16[4,64,1536]{2,1,0:T(8,128)(2,1)S(1)}, bf16[4,64,1536]{2,1,0:T(8,128)(2,1)}, u32[]{:S(2)}, u32[]{:S(2)}) collective-permute-start(bf16[4,64,1536]{2,1,0:T(8,128)(2,1)S(1)} %pad_maximum_fusion.4), channel_id=1, source_target_pairs={{0,1},{1,0},{2,3},{3,2},{4,5},{5,4},{6,7},{7,6},{8,9},{9,8},{10,11... | collective-permute-start | bytes 2359304 | tf_op jit(solution)/shard_map/ppermute | solution.py:27
  33.3 10.0 %collective-permute-start.13 = (bf16[64,1536]{1,0:T(8,128)(2,1)S(1)}, bf16[64,1536]{1,0:T(8,128)(2,1)S(1)}, u32[]{:S(2)}, u32[]{:S(2)}) collective-permute-start(bf16[64,1536]{1,0:T(8,128)(2,1)S(1)} %collective-permute-done.12), channel_id=1, source_target_pairs={{6,0},{24,26},{7,1},{25,27},{38,32},{56,58},{39,33},{57,59},{70,64... | collective-permute-start | bytes 589832 | tf_op jit(solution)/shard_map/ppermute | solution.py:110
  45.9 20.4 %collective-permute-start.9 = (bf16[2,4,64,384]{3,2,1,0:T(8,128)(2,1)S(1)}, bf16[2,4,64,384]{3,2,1,0:T(8,128)(2,1)S(1)}, u32[]{:S(2)}, u32[]{:S(2)}) collective-permute-start(bf16[2,4,64,384]{3,2,1,0:T(8,128)(2,1)S(1)} %get-tuple-element.74), channel_id=1, source_target_pairs={{0,8},{8,16},{16,24},{24,32},{32,40},{40,48},{48,56},{56,0},{1,9},... | collective-permute-start | bytes 1179656 | tf_op jit(solution)/shard_map/ppermute | solution.py:32
  46.0 20.4 %collective-permute-start.10 = (bf16[2,4,64,384]{3,2,1,0:T(8,128)(2,1)S(1)}, bf16[2,4,64,384]{3,2,1,0:T(8,128)(2,1)S(1)}, u32[]{:S(2)}, u32[]{:S(2)}) collective-permute-start(bf16[2,4,64,384]{3,2,1,0:T(8,128)(2,1)S(1)} %get-tuple-element.73), channel_id=1, source_target_pairs={{0,56},{8,0},{16,8},{24,16},{32,24},{40,32},{48,40},{56,48},{1,57}... | collective-permute-start | bytes 1179656 | tf_op jit(solution)/shard_map/ppermute | solution.py:32
  48.8 25.0 %collective-permute-start.11 = (bf16[2,4,64,384]{3,2,1,0:T(8,128)(2,1)S(1)}, bf16[2,4,64,384]{3,2,1,0:T(8,128)(2,1)S(1)}, u32[]{:S(2)}, u32[]{:S(2)}) collective-permute-start(bf16[2,4,64,384]{3,2,1,0:T(8,128)(2,1)S(1)} %pad_maximum_fusion.8), channel_id=1, source_target_pairs={{0,48},{8,56},{16,32},{24,40},{32,16},{40,24},{48,0},{56,8},{1,49}... | collective-permute-start | bytes 1179656 | tf_op jit(solution)/shard_map/ppermute | solution.py:37
  57.8 28.5 %collective-permute-start.7 = (f16[128,3200]{0,1:T(8,128)(2,1)S(1)}, f16[128,3200]{0,1:T(8,128)(2,1)S(1)}, u32[]{:S(2)}, u32[]{:S(2)}) collective-permute-start(f16[128,3200]{0,1:T(8,128)(2,1)S(1)} %pad_maximum_fusion.1), channel_id=1, source_target_pairs={{0,8},{8,16},{32,40},{40,48},{1,9},{9,17},{33,41},{41,49},{2,10},{... | collective-permute-start | bytes 2457608 | tf_op jit(solution)/shard_map/ppermute | solution.py:32
  60.9 25.4 %collective-permute-start.8 = (f16[128,3200]{0,1:T(8,128)(2,1)S(1)}, f16[128,3200]{0,1:T(8,128)(2,1)S(1)}, u32[]{:S(2)}, u32[]{:S(2)}) collective-permute-start(f16[128,3200]{0,1:T(8,128)(2,1)S(1)} %pad_maximum_fusion.1), channel_id=1, source_target_pairs={{16,8},{24,16},{48,40},{56,48},{17,9},{25,17},{49,41},{57,49},{18,... | collective-permute-start | bytes 2457608 | tf_op jit(solution)/shard_map/ppermute | solution.py:32
  86.3 22.4 %collective-permute-start.20 = (bf16[2,4,64,384]{3,2,1,0:T(8,128)(2,1)S(1)}, bf16[2,4,64,384]{3,2,1,0:T(8,128)(2,1)}, u32[]{:S(2)}, u32[]{:S(2)}) collective-permute-start(bf16[2,4,64,384]{3,2,1,0:T(8,128)(2,1)S(1)} %collective-permute-done.11), channel_id=1, source_target_pairs={{8,16},{16,8},{40,48},{48,40},{9,17},{17,9},{41,49},{49,41},{10,18... | collective-permute-start | bytes 1179656 | tf_op jit(solution)/shard_map/ppermute | solution.py:37
  87.8 16.3 %collective-permute-start.18 = (bf16[2,4,64,384]{3,2,1,0:T(8,128)(2,1)S(1)}, bf16[2,4,64,384]{3,2,1,0:T(8,128)(2,1)}, u32[]{:S(2)}, u32[]{:S(2)}) collective-permute-start(bf16[2,4,64,384]{3,2,1,0:T(8,128)(2,1)S(1)} %get-tuple-element.96), channel_id=1, source_target_pairs={{0,8},{8,16},{16,24},{32,40},{40,48},{48,56},{1,9},{9,17},{17,25},... | collective-permute-start | bytes 1179656 | tf_op jit(solution)/shard_map/ppermute | solution.py:32
  98.2 10.6 %collective-permute-start.19 = (bf16[2,4,64,384]{3,2,1,0:T(8,128)(2,1)S(1)}, bf16[2,4,64,384]{3,2,1,0:T(8,128)(2,1)S(1)}, u32[]{:S(2)}, u32[]{:S(2)}) collective-permute-start(bf16[2,4,64,384]{3,2,1,0:T(8,128)(2,1)S(1)} %get-tuple-element.95), channel_id=1, source_target_pairs={{24,16},{16,8},{8,0},{56,48},{48,40},{40,32},{25,17},{17,9},{9,1},... | collective-permute-start | bytes 1179656 | tf_op jit(solution)/shard_map/ppermute | solution.py:32
  111.4 10.4 %collective-permute-start.21 = (bf16[2,4,64,384]{3,2,1,0:T(8,128)(2,1)}, bf16[2,4,64,384]{3,2,1,0:T(8,128)(2,1)}, u32[]{:S(2)}, u32[]{:S(2)}) collective-permute-start(bf16[2,4,64,384]{3,2,1,0:T(8,128)(2,1)} %get-tuple-element.72), channel_id=1, source_target_pairs={{8,16},{16,8},{40,48},{48,40},{9,17},{17,9},{41,49},{49,41},{10,18... | collective-permute-start | bytes 1179656 | tf_op jit(solution)/shard_map/ppermute | solution.py:37
  112.9 13.4 %collective-permute-start.22 = (bf16[2,4,64,384]{3,2,1,0:T(8,128)(2,1)}, bf16[2,4,64,384]{3,2,1,0:T(8,128)(2,1)}, u32[]{:S(2)}, u32[]{:S(2)}) collective-permute-start(bf16[2,4,64,384]{3,2,1,0:T(8,128)(2,1)} %get-tuple-element.71), channel_id=1, source_target_pairs={{8,0},{16,24},{40,32},{48,56},{9,1},{17,25},{41,33},{49,57},{10,2}... | collective-permute-start | bytes 1179656 | tf_op jit(solution)/shard_map/ppermute | solution.py:37
  114.1 20.5 %collective-permute-start.23 = (bf16[2,4,64,384]{3,2,1,0:T(8,128)(2,1)}, bf16[2,4,64,384]{3,2,1,0:T(8,128)(2,1)}, u32[]{:S(2)}, u32[]{:S(2)}) collective-permute-start(bf16[2,4,64,384]{3,2,1,0:T(8,128)(2,1)} %collective-permute-done.20), channel_id=1, source_target_pairs={{8,0},{16,24},{40,32},{48,56},{9,1},{17,25},{41,33},{49,57},{10,2}... | collective-permute-start | bytes 1179656 | tf_op jit(solution)/shard_map/ppermute | solution.py:37
  115.5 51.1 %collective-permute-start.24 = (f16[128,3200]{0,1:T(8,128)(2,1)}, f16[128,3200]{0,1:T(8,128)(2,1)}, u32[]{:S(2)}, u32[]{:S(2)}) collective-permute-start(f16[128,3200]{0,1:T(8,128)(2,1)} %pad_maximum_fusion.3), channel_id=1, source_target_pairs={{0,56},{8,0},{16,8},{24,16},{32,24},{40,32},{48,40},{56,48},{1,57}... | collective-permute-start | bytes 2457608 | tf_op jit(solution)/shard_map/ppermute | solution.py:32
  115.6 51.0 %collective-permute-start.17 = (f16[128,3200]{0,1:T(8,128)(2,1)}, f16[128,3200]{0,1:T(8,128)(2,1)}, u32[]{:S(2)}, u32[]{:S(2)}) collective-permute-start(f16[128,3200]{0,1:T(8,128)(2,1)} %pad_maximum_fusion.2), channel_id=1, source_target_pairs={{0,8},{8,16},{16,24},{24,32},{32,40},{40,48},{48,56},{56,0},{1,9},... | collective-permute-start | bytes 2457608 | tf_op jit(solution)/shard_map/ppermute | solution.py:32
  134.7 25.9 %collective-permute-start.25 = (bf16[2,4,64,384]{3,2,1,0:T(8,128)(2,1)}, bf16[2,4,64,384]{3,2,1,0:T(8,128)(2,1)S(1)}, u32[]{:S(2)}, u32[]{:S(2)}) collective-permute-start(bf16[2,4,64,384]{3,2,1,0:T(8,128)(2,1)} %collective-permute-done.21), channel_id=1, source_target_pairs={{8,0},{16,24},{40,32},{48,56},{9,1},{17,25},{41,33},{49,57},{10,2}... | collective-permute-start | bytes 1179656 | tf_op jit(solution)/shard_map/ppermute | solution.py:37
  136.0 40.8 %collective-permute-start.26 = (bf16[4,4,2,64,1536]{4,3,2,1,0:T(8,128)(2,1)}, bf16[4,4,2,64,1536]{4,3,2,1,0:T(8,128)(2,1)}, u32[]{:S(2)}, u32[]{:S(2)}) collective-permute-start(bf16[4,4,2,64,1536]{4,3,2,1,0:T(8,128)(2,1)} %bitcast.214), channel_id=1, source_target_pairs={{0,1},{1,0},{2,3},{3,2},{4,5},{5,4},{6,7},{7,6},{8,9},{9,8},{10,11... | collective-permute-start | bytes 18874376 | tf_op jit(solution)/shard_map/ppermute | solution.py:27
  (28 other events, 203.2 us)
Sparse Core Ops, SparseCore 0:
  32.1 63.6 all-gather.2

commit v5 on v4

--- a/solution.py
+++ b/solution.py
@@ -66,8 +66,6 @@
     block = hidden // 8
     grad_scale = 1.0 / math.sqrt(tokens * 32)
 
-    from_x = [grad_out] + [shift(grad_out, "x", t) for t in (1, 2, 3)]
-    p = shift(grad_out, "zh", 1)
     gelu_value, gelu_slope = gelu_parts(pre_act.astype(jnp.float32))
     act, gelu_slope = lax.optimization_barrier((gelu_value.astype(jnp.bfloat16), gelu_slope))
     act = act.reshape(tokens, 4, 2, block).transpose(1, 2, 0, 3)
@@ -76,15 +74,18 @@
     act = jnp.where(c == 1, halves[:, :, ::-1], halves)
     pieces_out = [at(act, (y + s) % 4) for s in range(4)]
     pieces = [shift(v, "y", s) if s else v for s, v in enumerate(pieces_out)]
+    grad_out = after(grad_out, *pieces_out)
+    p = shift(grad_out, "zh", 1)
+    from_x = [grad_out] + [shift(grad_out, "x", t) for t in (1, 2, 3)]
     own, cross = (
         jnp.stack([lax.select_n((y - k) % 4, *[v[i] for v in pieces]) for k in range(4)], axis=1)
         for i in range(2)
     )
 
-    both = after(jnp.stack([grad_out, p]), *pieces_out)
+    both = jnp.stack([grad_out, p])
     all_rows = lax.all_gather(both, ("x", "y")).reshape(4, 4, 2, half, feats)
 
-    mine = after(jnp.stack(from_x), *pieces_out)
+    mine = jnp.stack(from_x)
     mine = jnp.stack([mine, shift(mine, "core", 1)], axis=1)
 
     def partial(*blocks):
@@ -135,6 +136,7 @@
     def choose(*units):
         return lax.select_n(zl, *units)
 
+    none = jnp.zeros_like(own)
     in_group = (
         choose(own, a_up, c_up, f),
         choose(a_down, own, a_up, c_up),
@@ -143,25 +145,30 @@
     )
     from_group = (
         choose(g, d, b, a_down),
-        choose(h, e, c_down, b),
-        choose(b, c_up, e, h),
+        choose(none, e, c_down, b),
+        choose(b, c_up, e, none),
         choose(a_up, b, d, g),
     )
-    none = jnp.zeros_like(own)
-    early = (from_group[0], choose(none, e, c_down, b), choose(b, c_up, e, none), from_group[3])
-    last = choose(h, none, none, h)
+    units = lax.optimization_barrier(
+        [
+            jnp.stack([jnp.stack([i[core], k[core]], axis=1) for i, k in zip(in_group, from_group)])
+            for core in range(2)
+        ]
+    )
 
-    def product(core, first, second, rows):
-        unit = jnp.stack([jnp.stack([i[core], j[core]], axis=1) for i, j in zip(first, second)])
+    def product(unit, rows):
         return lax.dot_general(
             unit.reshape(-1, block), rows.reshape(-1, feats), (((0,), (0,)), ((), ())),
             preferred_element_type=jnp.float32,
         )
 
-    summed = product(0, in_group, early, all_rows)
+    late = jnp.where(zl < 2, 1, 2)
+    summed = product(units[0], all_rows)
+    other_rows = after(other_rows, summed)
+    late_rows = jnp.stack([at(all_rows, late)[:, 1], at(other_rows, late)[:, 1]])
+    summed += product(units[1], other_rows)
     from_below, from_above = after(from_below, summed), after(from_above, summed)
-    summed += product(0, (none,), (last,), at(all_rows, jnp.where(zl < 2, 1, 2)))
-    summed += product(1, in_group, from_group, other_rows)
+    summed += product(h, late_rows)
 
     grad_act = part_own + unpack(from_below) + unpack(from_above)
     grad_pre = (grad_act * gelu_slope).astype(jnp.bfloat16)

time: 194 us -> 182 us (0.938)
  other arithmetic: 23 us -> 17.4 us
  starting transfers between devices: 61.4 us -> 56.1 us
  local copies, waits for them, and re-layouts: 9.46 us -> 14 us
  waiting for transfers between devices: 59.5 us -> 55 us
    ppermute x10, starting transfers between devices: 27.2 us -> 22.6 us  [shift(): return lax.ppermute(v, axis, [(i, (i + step) % n) for i in range(n)])]
    unnamed x50 -> x54, local copies, waits for them, and re-layouts: 5.64 us -> 9.02 us
    ppermute x6, waiting for transfers between devices: 30.9 us -> 27.6 us  [pairs_z(): return lax.ppermute(v, Z, pairs)]
    ppermute x8, waiting for transfers between devices: 20.1 us -> 17.4 us  [along_z(): return lax.ppermute(v, Z, pairs)]
    squeeze x1 -> x3, local copies, waits for them, and re-layouts: 0.75 us -> 3.03 us  [at(): return lax.dynamic_index_in_dim(v, i, 0, keepdims=False)]
    ppermute x3, waiting for transfers between devices: 7.96 us -> 9.93 us  [on_device(): q = q + lax.ppermute(p, ('zl', 'x'), [(3, (3 + t) % 4), (12, 12 + t)])]
    another operation x10 -> x12, other arithmetic: 4.66 us -> 3.59 us  [the longest x1 1.93 us: on_device(): mine = jnp.stack(from_x)]
  transfers between devices with their start and end apart: 28 -> 28, of which waited for: 10 -> 8; matrix products, arithmetic and copies ran while one was open for 24% -> 22% of each run, Pallas kernels for 0% -> 0%
where the time goes in v5:
time: 182 us; the launch traced here: 180 us
  starting transfers between devices  56.1 us (31%)
  waiting for transfers between devices  55 us (30%)
  matrix products  22.5 us (12%)
  other arithmetic  17.4 us (10%)
  between operations  14.9 us (8%)
  local copies, waits for them, and re-layouts  14 us (8%)
    ppermute x6, waiting for transfers between devices, pairs_z(): return lax.ppermute(v, Z, pairs)  27.6 us
    ppermute x8, starting transfers between devices, along_z(): return lax.ppermute(v, Z, pairs)  23.3 us
    ppermute x10, starting transfers between devices, shift(): return lax.ppermute(v, axis, [(i, (i + step) % n) for i in range(n)])  22.6 us
    ppermute x8, waiting for transfers between devices, along_z(): return lax.ppermute(v, Z, pairs)  17.4 us
    dot_general x3, matrix products, product(): lax.dot_general(unit.reshape(-1, block), rows.reshape(-1, feats), (((0,),...  13.6 us
    ppermute x3, waiting for transfers between devices, on_device(): q = q + lax.ppermute(p, ('zl', 'x'), [(3, (3 + t) % 4), (12, 12 + t)])  9.93 us
    unnamed x54, local copies, waits for them, and re-layouts  9.02 us
    dot_general x2, matrix products, partial(): lax.dot_general(rows, down_weight, (((1,), (1,)), ((), ())), preferred_el...  8.94 us
  transfers between devices with their start and end apart: 28, of which 8 were waited for; matrix products, arithmetic and copies ran while one was open for 22% of the time, Pallas kernels for 0%

profile of v5, /device:TPU:1, one launch (start us, length us, event | category | flops | bytes accessed | tf_op | source)
XLA Modules:
  0.0 179.9 jit_solution(13630956620514526271)
XLA Ops:
  8.8 2.2 %fusion.8 = (f32[128,3072]{0,1:T(8,128)}, bf16[128,3072]{0,1:T(8,128)(2,1)S(1)}) fusion(bf16[128,3072]{0,1:T(8,128)(2,1)S(1)} %copy.52), kind=kLoop, calls=%fused_computation.26 | loop fusion | flops 7864320 | bytes 3145728 | tf_op jit(solution)/shard_map/add | solution.py:19
  12.4 3.3 %collective-permute-start.2 = (bf16[64,1536]{1,0:T(8,128)(2,1)S(1)}, bf16[64,1536]{1,0:T(8,128)(2,1)S(1)}, u32[]{:S(2)}, u32[]{:S(2)}) collective-permute-start(bf16[64,1536]{1,0:T(8,128)(2,1)S(1)} %copy-done.18), channel_id=1, source_target_pairs={{0,6},{2,0},{4,2},{6,4},{1,7},{3,1},{5,3},{7,5},{8,14},{10,8},{12,... | collective-permute-start | bytes 589832 | tf_op jit(solution)/shard_map/ppermute | solution.py:27
  16.9 6.9 %collective-permute-start.12 = (bf16[64,1536]{1,0:T(8,128)(2,1)S(1)}, bf16[64,1536]{1,0:T(8,128)(2,1)S(1)}, u32[]{:S(2)}, u32[]{:S(2)}) collective-permute-start(bf16[64,1536]{1,0:T(8,128)(2,1)S(1)} %copy-done.18), channel_id=1, source_target_pairs={{0,32},{32,0},{1,33},{33,1},{2,34},{34,2},{3,35},{35,3},{4,36},{36... | collective-permute-start | bytes 589832 | tf_op jit(solution)/shard_map/ppermute | solution.py:27
  29.0 1.9 %pad_maximum_fusion.5 = (bf16[4,64,1536]{2,1,0:T(8,128)(2,1)}, bf16[4,1,64,1536]{3,2,1,0:T(8,128)(2,1)S(1)}) fusion(bf16[1,64,1536]{2,1,0:T(8,128)(2,1)S(1)} %bitcast.218, bf16[1,64,1536]{2,1,0:T(8,128)(2,1)S(1)} %bitcast.219, bf16[1,64,1536]{2,1,0:T(8,128)(2,1)} %bitcast.220, bf16[1,64,1536]{2,1,0:T(8,128)(2,1)S(1)} %bitcast.212), kind=kLoop, calls=%fused_computation.60 | loop fusion | flops 1179648 | bytes 2359296 | tf_op jit(solution)/shard_map/stack | solution.py:88
  30.9 2.5 %collective-permute-start.3 = (bf16[4,64,1536]{2,1,0:T(8,128)(2,1)}, bf16[4,64,1536]{2,1,0:T(8,128)(2,1)}, u32[]{:S(2)}, u32[]{:S(2)}) collective-permute-start(bf16[4,64,1536]{2,1,0:T(8,128)(2,1)} %get-tuple-element.75), channel_id=1, source_target_pairs={{0,1},{1,0},{2,3},{3,2},{4,5},{5,4},{6,7},{7,6},{8,9},{9,8},{10,11... | collective-permute-start | bytes 2359304 | tf_op jit(solution)/shard_map/ppermute | solution.py:27
  37.2 9.9 %collective-permute-done.13 = bf16[64,1536]{1,0:T(8,128)(2,1)S(1)} collective-permute-done((bf16[64,1536]{1,0:T(8,128)(2,1)S(1)}, bf16[64,1536]{1,0:T(8,128)(2,1)S(1)}, u32[]{:S(2)}, u32[]{:S(2)}) %collective-permute-start.13) | collective-permute-done | bytes 196640 | tf_op jit(solution)/shard_map/ppermute | solution.py:111
  48.3 7.6 %collective-permute-start.10 = (bf16[2,4,64,384]{3,2,1,0:T(8,128)(2,1)S(1)}, bf16[2,4,64,384]{3,2,1,0:T(8,128)(2,1)S(1)}, u32[]{:S(2)}, u32[]{:S(2)}) collective-permute-start(bf16[2,4,64,384]{3,2,1,0:T(8,128)(2,1)S(1)} %get-tuple-element.73), channel_id=1, source_target_pairs={{0,56},{8,0},{16,8},{24,16},{32,24},{40,32},{48,40},{56,48},{1,57}... | collective-permute-start | bytes 1179656 | tf_op jit(solution)/shard_map/ppermute | solution.py:32
  59.3 6.3 %fusion.39 = f32[256,3072]{0,1:T(8,128)S(1)} fusion(bf16[256,1536]{1,0:T(8,128)(2,1)S(1)} %bitcast.216, bf16[3072,1536]{1,0:T(8,128)(2,1)} %param.5), kind=kOutput, calls=%fused_computation.152 | convolution fusion | flops 2415919104 | bytes 13369344 | tf_op jit(solution)/shard_map/dot_general | solution.py:94
  66.2 3.4 %collective-permute-start.7 = (f16[128,3200]{0,1:T(8,128)(2,1)S(1)}, f16[128,3200]{0,1:T(8,128)(2,1)S(1)}, u32[]{:S(2)}, u32[]{:S(2)}) collective-permute-start(f16[128,3200]{0,1:T(8,128)(2,1)S(1)} %pad_maximum_fusion.2), channel_id=1, source_target_pairs={{0,8},{8,16},{32,40},{40,48},{1,9},{9,17},{33,41},{41,49},{2,10},{... | collective-permute-start | bytes 2457608 | tf_op jit(solution)/shard_map/ppermute | solution.py:32
  70.4 2.6 %fusion.40 = f32[256,3072]{0,1:T(8,128)S(1)} fusion(bf16[256,1536]{1,0:T(8,128)(2,1)S(1)} %bitcast.215, bf16[3072,1536]{1,0:T(8,128)(2,1)S(1)} %bitcast.222), kind=kOutput, calls=%fused_computation.153 | convolution fusion | flops 2415919104 | bytes 13369344 | tf_op jit(solution)/shard_map/dot_general | solution.py:94
  73.3 8.1 %collective-permute-done.11 = bf16[2,4,64,384]{3,2,1,0:T(8,128)(2,1)S(1)} collective-permute-done((bf16[2,4,64,384]{3,2,1,0:T(8,128)(2,1)S(1)}, bf16[2,4,64,384]{3,2,1,0:T(8,128)(2,1)S(1)}, u32[]{:S(2)}, u32[]{:S(2)}) %collective-permute-start.11) | collective-permute-done | bytes 393248 | tf_op jit(solution)/shard_map/ppermute | solution.py:37
  81.4 12.0 %collective-permute-done.7 = f16[128,3200]{0,1:T(8,128)(2,1)S(1)} collective-permute-done((f16[128,3200]{0,1:T(8,128)(2,1)S(1)}, f16[128,3200]{0,1:T(8,128)(2,1)S(1)}, u32[]{:S(2)}, u32[]{:S(2)}) %collective-permute-start.7) | collective-permute-done | bytes 819232 | tf_op jit(solution)/shard_map/ppermute | solution.py:32
  94.1 5.8 %collective-permute-start.18 = (bf16[2,4,64,384]{3,2,1,0:T(8,128)(2,1)S(1)}, bf16[2,4,64,384]{3,2,1,0:T(8,128)(2,1)S(1)}, u32[]{:S(2)}, u32[]{:S(2)}) collective-permute-start(bf16[2,4,64,384]{3,2,1,0:T(8,128)(2,1)S(1)} %get-tuple-element.100), channel_id=1, source_target_pairs={{0,8},{8,16},{16,24},{32,40},{40,48},{48,56},{1,9},{9,17},{17,25},... | collective-permute-start | bytes 1179656 | tf_op jit(solution)/shard_map/ppermute | solution.py:32
  106.4 3.9 %collective-permute-done.19 = bf16[2,4,64,384]{3,2,1,0:T(8,128)(2,1)S(1)} collective-permute-done((bf16[2,4,64,384]{3,2,1,0:T(8,128)(2,1)S(1)}, bf16[2,4,64,384]{3,2,1,0:T(8,128)(2,1)S(1)}, u32[]{:S(2)}, u32[]{:S(2)}) %collective-permute-start.19) | collective-permute-done | bytes 393248 | tf_op jit(solution)/shard_map/ppermute | solution.py:32
  115.0 11.0 %collective-permute-done.22 = bf16[2,4,64,384]{3,2,1,0:T(8,128)(2,1)} collective-permute-done((bf16[2,4,64,384]{3,2,1,0:T(8,128)(2,1)S(1)}, bf16[2,4,64,384]{3,2,1,0:T(8,128)(2,1)}, u32[]{:S(2)}, u32[]{:S(2)}) %collective-permute-start.22) | collective-permute-done | bytes 393248 | tf_op jit(solution)/shard_map/ppermute | solution.py:37
  126.0 8.4 %collective-permute-done.23 = bf16[2,4,64,384]{3,2,1,0:T(8,128)(2,1)} collective-permute-done((bf16[2,4,64,384]{3,2,1,0:T(8,128)(2,1)S(1)}, bf16[2,4,64,384]{3,2,1,0:T(8,128)(2,1)}, u32[]{:S(2)}, u32[]{:S(2)}) %collective-permute-start.23) | collective-permute-done | bytes 393248 | tf_op jit(solution)/shard_map/ppermute | solution.py:37
  134.4 3.5 %collective-permute-start.24 = (bf16[4,4,2,64,1536]{4,3,2,1,0:T(8,128)(2,1)}, bf16[4,4,2,64,1536]{4,3,2,1,0:T(8,128)(2,1)}, u32[]{:S(2)}, u32[]{:S(2)}) collective-permute-start(bf16[4,4,2,64,1536]{4,3,2,1,0:T(8,128)(2,1)} %bitcast.204), channel_id=1, source_target_pairs={{0,1},{1,0},{2,3},{3,2},{4,5},{5,4},{6,7},{7,6},{8,9},{9,8},{10,11... | collective-permute-start | bytes 18874376 | tf_op jit(solution)/shard_map/ppermute | solution.py:27
  137.9 4.3 %collective-permute-start.25 = (f16[128,3200]{0,1:T(8,128)(2,1)}, f16[128,3200]{0,1:T(8,128)(2,1)S(1)}, u32[]{:S(2)}, u32[]{:S(2)}) collective-permute-start(f16[128,3200]{0,1:T(8,128)(2,1)} %pad_maximum_fusion.4), channel_id=1, source_target_pairs={{0,56},{8,0},{16,8},{24,16},{32,24},{40,32},{48,40},{56,48},{1,57}... | collective-permute-start | bytes 2457608 | tf_op jit(solution)/shard_map/ppermute | solution.py:32
  143.8 2.1 %select_select_fusion.3 = (bf16[2,4,64,384]{3,2,1,0:T(8,128)(2,1)S(1)}, bf16[2,4,64,384]{3,2,1,0:T(8,128)(2,1)S(1)}, bf16[2,4,64,384]{3,2,1,0:T(8,128)(2,1)S(1)}...) fusion(bf16[2,4,64,384]{3,2,1,0:T(8,128)(2,1)S(1)} %collective-permute-done.9, ...), kind=kLoop, calls=%fused_computation.84 | loop fusion | flops 3538944 | bytes 5505027 | tf_op jit(solution)/shard_map/select_n | solution.py:137
  152.7 2.6 %convolution_bitcast_fusion.1 = f32[384,1536]{1,0:T(8,128)S(1)} fusion(bf16[4,4,2,64,1536]{4,3,2,1,0:T(8,128)(2,1)S(1)} %bitcast.208, bf16[4,4,2,64,384]{4,3,1,2,0:T(8,128)(2,1)S(1)} %pad_maximum_fusion), kind=kOutput, calls=%fused_computation.8 | convolution fusion | flops 2415919104 | bytes 10223616 | tf_op jit(solution)/shard_map/dot_general | solution.py:160
  155.4 6.9 %fusion.2 = f32[384,1536]{1,0:T(8,128)} fusion(f32[384,1536]{1,0:T(8,128)S(1)} %convolution_bitcast_fusion.1, bf16[4,4,2,64,1536]{4,3,2,1,0:T(8,128)(2,1)} %collective-permute-done.24, bf16[4,4,2,64,384]{4,3,1,2,0:T(8,128)(2,1)S(1)} %pad_maximum_fusion.1), kind=kOutput, calls=%fused_computation.12 | convolution fusion | flops 2416508928 | bytes 12582912 | tf_op jit(solution)/shard_map/dot_general | solution.py:160
  162.3 2.8 %copy_bitcast_fusion = bf16[4,2,64,1536]{3,2,0,1:T(8,128)(2,1)} fusion(bf16[4,4,2,64,1536]{4,3,2,1,0:T(8,128)(2,1)} %collective-permute-done.24, s32[]{:T(128)S(6)} %select_n.801), kind=kLoop, calls=%fused_computation.39 | loop fusion | bytes 3145732 | tf_op jit(solution)/shard_map/jit(dynamic_index_in_dim)/squeeze | solution.py:41
  166.5 2.4 %copy.73 = bf16[128,3072]{1,0:T(8,128)(2,1)} copy(bf16[128,3072]{0,1:T(8,128)(2,1)} %fusion.14) | data formatting | bytes 1572864
  169.1 4.0 %fusion.1 = f32[384,1536]{1,0:T(8,128)} fusion(f32[384,1536]{1,0:T(8,128)} %fusion.2, bf16[2,4,64,384]{3,2,1,0:T(8,128)(2,1)} %collective-permute-done.26, bf16[1,4,64,1536]{3,2,1,0:T(8,128)(2,1)S(1)} %slice_bitcast_fusion, bf16[1,4,64,1536]{3,2,1,0:T(8,128)(2,1)S(1)} %copy-done.17), kind=kOutput, calls=%fused_computation.11 | convolution fusion | flops 605945856 | bytes 6684672 | tf_op jit(solution)/shard_map/dot_general | solution.py:160
  (159 shorter events, 40.3 us)
Async XLA Ops:
  7.2 127.3 %all-gather.3.cloned.1.call-start = ((), (), s32[]{:S(2)}) async-start(), calls=%async_computation | async-start | bytes 6684672 | tf_op jit(solution)/shard_map/all_gather | solution.py:86
  12.4 12.6 %collective-permute-start.2 = (bf16[64,1536]{1,0:T(8,128)(2,1)S(1)}, bf16[64,1536]{1,0:T(8,128)(2,1)S(1)}, u32[]{:S(2)}, u32[]{:S(2)}) collective-permute-start(bf16[64,1536]{1,0:T(8,128)(2,1)S(1)} %copy-done.18), channel_id=1, source_target_pairs={{0,6},{2,0},{4,2},{6,4},{1,7},{3,1},{5,3},{7,5},{8,14},{10,8},{12,... | collective-permute-start | bytes 589832 | tf_op jit(solution)/shard_map/ppermute | solution.py:27
  15.7 10.8 %collective-permute-start.1 = (bf16[64,1536]{1,0:T(8,128)(2,1)S(1)}, bf16[64,1536]{1,0:T(8,128)(2,1)S(1)}, u32[]{:S(2)}, u32[]{:S(2)}) collective-permute-start(bf16[64,1536]{1,0:T(8,128)(2,1)S(1)} %copy-done.18), channel_id=1, source_target_pairs={{0,4},{2,6},{4,0},{6,2},{1,5},{3,7},{5,1},{7,3},{8,12},{10,14},{12... | collective-permute-start | bytes 589832 | tf_op jit(solution)/shard_map/ppermute | solution.py:27
  16.3 12.0 %collective-permute-start = (bf16[64,1536]{1,0:T(8,128)(2,1)S(1)}, bf16[64,1536]{1,0:T(8,128)(2,1)S(1)}, u32[]{:S(2)}, u32[]{:S(2)}) collective-permute-start(bf16[64,1536]{1,0:T(8,128)(2,1)S(1)} %copy-done.18), channel_id=1, source_target_pairs={{0,2},{2,4},{4,6},{6,0},{1,3},{3,5},{5,7},{7,1},{8,10},{10,12},{12... | collective-permute-start | bytes 589832 | tf_op jit(solution)/shard_map/ppermute | solution.py:27
  16.9 16.6 %collective-permute-start.12 = (bf16[64,1536]{1,0:T(8,128)(2,1)S(1)}, bf16[64,1536]{1,0:T(8,128)(2,1)S(1)}, u32[]{:S(2)}, u32[]{:S(2)}) collective-permute-start(bf16[64,1536]{1,0:T(8,128)(2,1)S(1)} %copy-done.18), channel_id=1, source_target_pairs={{0,32},{32,0},{1,33},{33,1},{2,34},{34,2},{3,35},{35,3},{4,36},{36... | collective-permute-start | bytes 589832 | tf_op jit(solution)/shard_map/ppermute | solution.py:27
  23.8 11.1 %collective-permute-start.4 = (bf16[2,2,64,384]{3,2,1,0:T(8,128)(2,1)S(1)}, bf16[2,2,64,384]{3,2,1,0:T(8,128)(2,1)S(1)}, u32[]{:S(2)}, u32[]{:S(2)}) collective-permute-start(bf16[2,2,64,384]{3,2,1,0:T(8,128)(2,1)S(1)} %get-tuple-element.79), channel_id=1, source_target_pairs={{0,64},{64,128},{128,192},{192,0},{1,65},{65,129},{129,193},{193,1... | collective-permute-start | bytes 589832 | tf_op jit(solution)/shard_map/ppermute | solution.py:27
  25.1 10.5 %collective-permute-start.6 = (bf16[2,2,64,384]{3,2,1,0:T(8,128)(2,1)S(1)}, bf16[2,2,64,384]{3,2,1,0:T(8,128)(2,1)S(1)}, u32[]{:S(2)}, u32[]{:S(2)}) collective-permute-start(bf16[2,2,64,384]{3,2,1,0:T(8,128)(2,1)S(1)} %get-tuple-element.77), channel_id=1, source_target_pairs={{0,192},{64,0},{128,64},{192,128},{1,193},{65,1},{129,65},{193,129... | collective-permute-start | bytes 589832 | tf_op jit(solution)/shard_map/ppermute | solution.py:27
  26.5 10.4 %collective-permute-start.5 = (bf16[2,2,64,384]{3,2,1,0:T(8,128)(2,1)S(1)}, bf16[2,2,64,384]{3,2,1,0:T(8,128)(2,1)S(1)}, u32[]{:S(2)}, u32[]{:S(2)}) collective-permute-start(bf16[2,2,64,384]{3,2,1,0:T(8,128)(2,1)S(1)} %get-tuple-element.78), channel_id=1, source_target_pairs={{0,128},{64,192},{128,0},{192,64},{1,129},{65,193},{129,1},{193,65... | collective-permute-start | bytes 589832 | tf_op jit(solution)/shard_map/ppermute | solution.py:27
  30.9 26.5 %collective-permute-start.3 = (bf16[4,64,1536]{2,1,0:T(8,128)(2,1)}, bf16[4,64,1536]{2,1,0:T(8,128)(2,1)}, u32[]{:S(2)}, u32[]{:S(2)}) collective-permute-start(bf16[4,64,1536]{2,1,0:T(8,128)(2,1)} %get-tuple-element.75), channel_id=1, source_target_pairs={{0,1},{1,0},{2,3},{3,2},{4,5},{5,4},{6,7},{7,6},{8,9},{9,8},{10,11... | collective-permute-start | bytes 2359304 | tf_op jit(solution)/shard_map/ppermute | solution.py:27
  35.6 11.5 %collective-permute-start.13 = (bf16[64,1536]{1,0:T(8,128)(2,1)S(1)}, bf16[64,1536]{1,0:T(8,128)(2,1)S(1)}, u32[]{:S(2)}, u32[]{:S(2)}) collective-permute-start(bf16[64,1536]{1,0:T(8,128)(2,1)S(1)} %collective-permute-done.12), channel_id=1, source_target_pairs={{6,0},{24,26},{7,1},{25,27},{38,32},{56,58},{39,33},{57,59},{70,64... | collective-permute-start | bytes 589832 | tf_op jit(solution)/shard_map/ppermute | solution.py:111
  48.2 25.0 %collective-permute-start.9 = (bf16[2,4,64,384]{3,2,1,0:T(8,128)(2,1)S(1)}, bf16[2,4,64,384]{3,2,1,0:T(8,128)(2,1)S(1)}, u32[]{:S(2)}, u32[]{:S(2)}) collective-permute-start(bf16[2,4,64,384]{3,2,1,0:T(8,128)(2,1)S(1)} %get-tuple-element.74), channel_id=1, source_target_pairs={{0,8},{8,16},{16,24},{24,32},{32,40},{40,48},{48,56},{56,0},{1,9},... | collective-permute-start | bytes 1179656 | tf_op jit(solution)/shard_map/ppermute | solution.py:32
  48.3 24.9 %collective-permute-start.10 = (bf16[2,4,64,384]{3,2,1,0:T(8,128)(2,1)S(1)}, bf16[2,4,64,384]{3,2,1,0:T(8,128)(2,1)S(1)}, u32[]{:S(2)}, u32[]{:S(2)}) collective-permute-start(bf16[2,4,64,384]{3,2,1,0:T(8,128)(2,1)S(1)} %get-tuple-element.73), channel_id=1, source_target_pairs={{0,56},{8,0},{16,8},{24,16},{32,24},{40,32},{48,40},{56,48},{1,57}... | collective-permute-start | bytes 1179656 | tf_op jit(solution)/shard_map/ppermute | solution.py:32
  56.0 25.3 %collective-permute-start.11 = (bf16[2,4,64,384]{3,2,1,0:T(8,128)(2,1)S(1)}, bf16[2,4,64,384]{3,2,1,0:T(8,128)(2,1)S(1)}, u32[]{:S(2)}, u32[]{:S(2)}) collective-permute-start(bf16[2,4,64,384]{3,2,1,0:T(8,128)(2,1)S(1)} %pad_maximum_fusion.9), channel_id=1, source_target_pairs={{0,48},{8,56},{16,32},{24,40},{32,16},{40,24},{48,0},{56,8},{1,49}... | collective-permute-start | bytes 1179656 | tf_op jit(solution)/shard_map/ppermute | solution.py:37
  66.2 27.2 %collective-permute-start.7 = (f16[128,3200]{0,1:T(8,128)(2,1)S(1)}, f16[128,3200]{0,1:T(8,128)(2,1)S(1)}, u32[]{:S(2)}, u32[]{:S(2)}) collective-permute-start(f16[128,3200]{0,1:T(8,128)(2,1)S(1)} %pad_maximum_fusion.2), channel_id=1, source_target_pairs={{0,8},{8,16},{32,40},{40,48},{1,9},{9,17},{33,41},{41,49},{2,10},{... | collective-permute-start | bytes 2457608 | tf_op jit(solution)/shard_map/ppermute | solution.py:32
  69.6 23.8 %collective-permute-start.8 = (f16[128,3200]{0,1:T(8,128)(2,1)S(1)}, f16[128,3200]{0,1:T(8,128)(2,1)S(1)}, u32[]{:S(2)}, u32[]{:S(2)}) collective-permute-start(f16[128,3200]{0,1:T(8,128)(2,1)S(1)} %pad_maximum_fusion.2), channel_id=1, source_target_pairs={{16,8},{24,16},{48,40},{56,48},{17,9},{25,17},{49,41},{57,49},{18,... | collective-permute-start | bytes 2457608 | tf_op jit(solution)/shard_map/ppermute | solution.py:32
  93.4 16.9 %collective-permute-start.20 = (bf16[2,4,64,384]{3,2,1,0:T(8,128)(2,1)S(1)}, bf16[2,4,64,384]{3,2,1,0:T(8,128)(2,1)S(1)}, u32[]{:S(2)}, u32[]{:S(2)}) collective-permute-start(bf16[2,4,64,384]{3,2,1,0:T(8,128)(2,1)S(1)} %collective-permute-done.11), channel_id=1, source_target_pairs={{8,16},{16,8},{40,48},{48,40},{9,17},{17,9},{41,49},{49,41},{10,18... | collective-permute-start | bytes 1179656 | tf_op jit(solution)/shard_map/ppermute | solution.py:37
  94.1 12.2 %collective-permute-start.18 = (bf16[2,4,64,384]{3,2,1,0:T(8,128)(2,1)S(1)}, bf16[2,4,64,384]{3,2,1,0:T(8,128)(2,1)S(1)}, u32[]{:S(2)}, u32[]{:S(2)}) collective-permute-start(bf16[2,4,64,384]{3,2,1,0:T(8,128)(2,1)S(1)} %get-tuple-element.100), channel_id=1, source_target_pairs={{0,8},{8,16},{16,24},{32,40},{40,48},{48,56},{1,9},{9,17},{17,25},... | collective-permute-start | bytes 1179656 | tf_op jit(solution)/shard_map/ppermute | solution.py:32
  100.0 10.3 %collective-permute-start.19 = (bf16[2,4,64,384]{3,2,1,0:T(8,128)(2,1)S(1)}, bf16[2,4,64,384]{3,2,1,0:T(8,128)(2,1)S(1)}, u32[]{:S(2)}, u32[]{:S(2)}) collective-permute-start(bf16[2,4,64,384]{3,2,1,0:T(8,128)(2,1)S(1)} %get-tuple-element.99), channel_id=1, source_target_pairs={{24,16},{16,8},{8,0},{56,48},{48,40},{40,32},{25,17},{17,9},{9,1},... | collective-permute-start | bytes 1179656 | tf_op jit(solution)/shard_map/ppermute | solution.py:32
  112.4 13.6 %collective-permute-start.22 = (bf16[2,4,64,384]{3,2,1,0:T(8,128)(2,1)S(1)}, bf16[2,4,64,384]{3,2,1,0:T(8,128)(2,1)}, u32[]{:S(2)}, u32[]{:S(2)}) collective-permute-start(bf16[2,4,64,384]{3,2,1,0:T(8,128)(2,1)S(1)} %get-tuple-element.71), channel_id=1, source_target_pairs={{8,0},{16,24},{40,32},{48,56},{9,1},{17,25},{41,33},{49,57},{10,2}... | collective-permute-start | bytes 1179656 | tf_op jit(solution)/shard_map/ppermute | solution.py:37
  113.7 20.7 %collective-permute-start.23 = (bf16[2,4,64,384]{3,2,1,0:T(8,128)(2,1)S(1)}, bf16[2,4,64,384]{3,2,1,0:T(8,128)(2,1)}, u32[]{:S(2)}, u32[]{:S(2)}) collective-permute-start(bf16[2,4,64,384]{3,2,1,0:T(8,128)(2,1)S(1)} %collective-permute-done.20), channel_id=1, source_target_pairs={{8,0},{16,24},{40,32},{48,56},{9,1},{17,25},{41,33},{49,57},{10,2}... | collective-permute-start | bytes 1179656 | tf_op jit(solution)/shard_map/ppermute | solution.py:37
  134.4 20.9 %collective-permute-start.24 = (bf16[4,4,2,64,1536]{4,3,2,1,0:T(8,128)(2,1)}, bf16[4,4,2,64,1536]{4,3,2,1,0:T(8,128)(2,1)}, u32[]{:S(2)}, u32[]{:S(2)}) collective-permute-start(bf16[4,4,2,64,1536]{4,3,2,1,0:T(8,128)(2,1)} %bitcast.204), channel_id=1, source_target_pairs={{0,1},{1,0},{2,3},{3,2},{4,5},{5,4},{6,7},{7,6},{8,9},{9,8},{10,11... | collective-permute-start | bytes 18874376 | tf_op jit(solution)/shard_map/ppermute | solution.py:27
  137.9 24.3 %collective-permute-start.25 = (f16[128,3200]{0,1:T(8,128)(2,1)}, f16[128,3200]{0,1:T(8,128)(2,1)S(1)}, u32[]{:S(2)}, u32[]{:S(2)}) collective-permute-start(f16[128,3200]{0,1:T(8,128)(2,1)} %pad_maximum_fusion.4), channel_id=1, source_target_pairs={{0,56},{8,0},{16,8},{24,16},{32,24},{40,32},{48,40},{56,48},{1,57}... | collective-permute-start | bytes 2457608 | tf_op jit(solution)/shard_map/ppermute | solution.py:32
  142.3 22.8 %collective-permute-start.17 = (f16[128,3200]{0,1:T(8,128)(2,1)}, f16[128,3200]{0,1:T(8,128)(2,1)S(1)}, u32[]{:S(2)}, u32[]{:S(2)}) collective-permute-start(f16[128,3200]{0,1:T(8,128)(2,1)} %pad_maximum_fusion.3), channel_id=1, source_target_pairs={{0,8},{8,16},{16,24},{24,32},{32,40},{40,48},{48,56},{56,0},{1,9},... | collective-permute-start | bytes 2457608 | tf_op jit(solution)/shard_map/ppermute | solution.py:32
  142.3 26.8 %collective-permute-start.26 = (bf16[2,4,64,384]{3,2,1,0:T(8,128)(2,1)}, bf16[2,4,64,384]{3,2,1,0:T(8,128)(2,1)}, u32[]{:S(2)}, u32[]{:S(2)}) collective-permute-start(bf16[2,4,64,384]{3,2,1,0:T(8,128)(2,1)} %collective-permute-done.21), channel_id=1, source_target_pairs={{8,0},{16,24},{40,32},{48,56},{9,1},{17,25},{41,33},{49,57},{10,2}... | collective-permute-start | bytes 1179656 | tf_op jit(solution)/shard_map/ppermute | solution.py:37
  (30 other events, 191.9 us)
Sparse Core Ops, SparseCore 0:
  34.4 67.0 all-gather.2

commit v6 on v3

--- a/solution.py
+++ b/solution.py
@@ -66,7 +66,9 @@
     block = hidden // 8
     grad_scale = 1.0 / math.sqrt(tokens * 32)
 
+    e0, e3 = zl == 0, zl == 3
     p = shift(grad_out, "zh", 1)
+
     gelu_value, gelu_slope = gelu_parts(pre_act.astype(jnp.float32))
     act, gelu_slope = lax.optimization_barrier((gelu_value.astype(jnp.bfloat16), gelu_slope))
     act = act.reshape(tokens, 4, 2, block).transpose(1, 2, 0, 3)
@@ -80,18 +82,25 @@
         for i in range(2)
     )
 
-    both = after(jnp.stack([grad_out, p]), *pieces_out)
+    both = after(jnp.stack([grad_out, p]), own, cross)
     all_rows = lax.all_gather(both, ("x", "y")).reshape(4, 4, 2, half, feats)
 
-    from_x = jnp.stack([both] + [shift(both, "x", t) for t in (1, 2, 3)])
-    beyond = at(from_x[:, 1], jnp.where(zl == 0, x - 3, x) % 4)
-    mine = jnp.concatenate([from_x[:, 0], beyond[None]])
+    a_up = along_z(jnp.where(e3, cross, own), 1, range(4))
+    a_down = along_z(jnp.where(e0, cross, own), -1, range(4))
+    b = pairs_z(cross, {0: -2, 1: -2, 2: 2, 3: 2})
+
+    near_g = after(grad_out, own, cross)
+    from_x = [near_g] + [shift(near_g, "x", t) for t in (1, 2, 3)]
+    p, *from_x = lax.optimization_barrier((p, *from_x, a_up, a_down))[:5]
+    beyond = jnp.where(jnp.where(e0, x == 3, x == 0), p, jnp.zeros_like(p))
+    for t in (1, 2, 3):
+        beyond = beyond + lax.ppermute(p, ("zl", "x"), [(3, (3 + t) % 4), (12, 12 + t)])
+    mine = jnp.stack(from_x + [beyond])
     mine = jnp.stack([mine, shift(mine, "core", 1)], axis=1)
-    mine = after(mine, own, cross)
 
     place = [(x - zl - k) % 4 for k in (2, 1, -1, 0)]
-    place[1] = jnp.where(zl == 3, 4, place[1])
-    place[2] = jnp.where(zl == 0, 4, place[2])
+    place[1] = jnp.where(e3, 4, place[1])
+    place[2] = jnp.where(e0, 4, place[2])
     rows = jnp.stack([at(mine, k) for k in place])
     rows = jnp.where(c == 1, rows[:, ::-1], rows).reshape(4 * tokens, feats)
     parts = lax.dot_general(
@@ -102,29 +111,23 @@
     )
     far = pack(part_far)
 
-    e0, e3 = zl == 0, zl == 3
-    a_up = along_z(jnp.where(e3, cross, own), 1, range(4))
-    a_down = along_z(jnp.where(e0, cross, own), -1, range(4))
-    b = pairs_z(cross, {0: -2, 1: -2, 2: 2, 3: 2})
     far_up = along_z(far, 1, (0, 1))
     far_down = along_z(far, -1, (2, 3))
-    c_up = along_z(after(jnp.where(e0, b, a_up), far), 1, (0, 1, 2))
-    c_down = along_z(after(jnp.where(e3, b, a_down), far), -1, (3, 2, 1))
-    d = pairs_z(after(b, far), {1: 1, 2: -1})
-    near_up = pack(part_up + unpack(after(far_up, a_up, a_down, b)))
-    near_down = pack(part_down + unpack(after(far_down, a_up, a_down, b)))
-    from_below = along_z(near_up, 1, range(4))
-    from_above = along_z(near_down, -1, range(4))
+    c_up = along_z(jnp.where(e0, b, a_up), 1, (0, 1, 2))
+    c_down = along_z(jnp.where(e3, b, a_down), -1, (3, 2, 1))
+    d = pairs_z(b, {1: 1, 2: -1})
+    c_up, c_down, d = lax.optimization_barrier((c_up, c_down, d))
     e = pairs_z(jnp.where(zl == 1, c_up, c_down), {1: 1, 2: -1})
     f = pairs_z(jnp.where(zl == 2, c_up, c_down), {1: -1, 2: 1})
     g = pairs_z(d, {1: -1, 2: 1})
+    e, f, g, far = lax.optimization_barrier((e, f, g, far))
     h = pairs_z(e, {1: -1, 2: 1})
-
-    all_rows = after(all_rows, e, f, g)
-    other_rows = shift(all_rows, "core", 1)
-    own, a_up, a_down, b, c_up, c_down, d, e, f, g = lax.optimization_barrier(
-        (own, a_up, a_down, b, c_up, c_down, d, e, f, g)
-    )
+    far_up, far_down = lax.optimization_barrier((far_up, far_down, e, f, g))[:2]
+    near_up = pack(part_up + unpack(far_up))
+    near_down = pack(part_down + unpack(far_down))
+    from_below = along_z(near_up, 1, range(4))
+    from_above = along_z(near_down, -1, range(4))
+    other_rows = shift(after(all_rows, e, f, g), "core", 1)
 
     def choose(*units):
         return lax.select_n(zl, *units)
@@ -141,21 +144,22 @@
         choose(b, c_up, e, h),
         choose(a_up, b, d, g),
     )
-    none = jnp.zeros_like(own)
-    early = (from_group[0], choose(none, e, c_down, b), choose(b, c_up, e, none), from_group[3])
-    last = choose(h, none, none, h)
+    units = lax.optimization_barrier(
+        [
+            jnp.stack([jnp.stack([i[core], k[core]], axis=1) for i, k in zip(in_group, from_group)])
+            for core in range(2)
+        ]
+    )
 
-    def product(core, first, second, rows):
-        unit = jnp.stack([jnp.stack([i[core], j[core]], axis=1) for i, j in zip(first, second)])
+    def product(unit, rows):
         return lax.dot_general(
             unit.reshape(-1, block), rows.reshape(-1, feats), (((0,), (0,)), ((), ())),
             preferred_element_type=jnp.float32,
         )
 
-    summed = product(0, in_group, early, all_rows)
-    from_below, from_above = after(from_below, summed), after(from_above, summed)
-    summed += product(0, (none,), (last,), at(all_rows, jnp.where(zl < 2, 1, 2)))
-    summed += product(1, in_group, from_group, other_rows)
+    summed = product(units[0], all_rows)
+    summed += product(units[1], after(other_rows, summed))
+    from_below, from_above = lax.optimization_barrier((from_below, from_above, summed))[:2]
 
     grad_act = part_own + unpack(from_below) + unpack(from_above)
     grad_pre = (grad_act * gelu_slope).astype(jnp.bfloat16)

time: 215 us -> 175 us (0.81)
  waiting for transfers between devices: 70.7 us -> 50.7 us
  other arithmetic: 31.1 us -> 20.4 us
  starting transfers between devices: 67.4 us -> 58.9 us
  matrix products: 19.8 us -> 14.8 us
  local copies, waits for them, and re-layouts: 10.6 us -> 13.7 us
    ppermute x8, starting transfers between devices: 38.4 us -> 24.5 us  [along_z(): return lax.ppermute(v, Z, pairs)]
    ppermute x8, waiting for transfers between devices: 33.6 us -> 23 us  [along_z(): return lax.ppermute(v, Z, pairs)]
    unnamed x58 -> x46, local copies, waits for them, and re-layouts: 6.35 us -> 12.1 us
    ppermute x6, waiting for transfers between devices: 12.5 us -> 6.87 us  [pairs_z(): return lax.ppermute(v, Z, pairs)]
    ppermute x9, waiting for transfers between devices: 24.6 us -> 19.5 us  [shift(): return lax.ppermute(v, axis, [(i, (i + step) % n) for i in range(n)])]
    another operation x10 -> x11, other arithmetic: 7.45 us -> 2.37 us  [the longest x1 0.83 us: on_device(): both = after(jnp.stack([grad_out, p]), own, cross)]
    dot_general x3 -> x2, matrix products: 11.8 us -> 6.71 us  [product(): lax.dot_general(unit.reshape(-1, block), rows.reshape(-1, feats), (((0,),...]
    ppermute x9, starting transfers between devices: 20 us -> 25 us  [shift(): return lax.ppermute(v, axis, [(i, (i + step) % n) for i in range(n)])]
  transfers between devices with their start and end apart: 24 -> 27, of which waited for: 12 -> 12; matrix products, arithmetic and copies ran while one was open for 23% -> 24% of each run, Pallas kernels for 0% -> 0%
where the time goes in v6:
time: 175 us; the launch traced here: 173 us
  starting transfers between devices  58.9 us (34%)
  waiting for transfers between devices  50.7 us (29%)
  other arithmetic  20.4 us (12%)
  matrix products  14.8 us (8%)
  between operations  14.8 us (8%)
  local copies, waits for them, and re-layouts  13.7 us (8%)
    ppermute x9, starting transfers between devices, shift(): return lax.ppermute(v, axis, [(i, (i + step) % n) for i in range(n)])  25 us
    ppermute x8, starting transfers between devices, along_z(): return lax.ppermute(v, Z, pairs)  24.5 us
    ppermute x8, waiting for transfers between devices, along_z(): return lax.ppermute(v, Z, pairs)  23 us
    ppermute x9, waiting for transfers between devices, shift(): return lax.ppermute(v, axis, [(i, (i + step) % n) for i in range(n)])  19.5 us
    unnamed x46, local copies, waits for them, and re-layouts  12.1 us
    dot_general x1, matrix products, on_device(): lax.dot_general(rows, down_weight, (((1,), (1,)), ((), ())), preferred_el...  8.06 us
    ppermute x6, waiting for transfers between devices, pairs_z(): return lax.ppermute(v, Z, pairs)  6.87 us
    ppermute x6, starting transfers between devices, pairs_z(): return lax.ppermute(v, Z, pairs)  6.74 us
  transfers between devices with their start and end apart: 27, of which 12 were waited for; matrix products, arithmetic and copies ran while one was open for 24% of the time, Pallas kernels for 0%

profile of v6, /device:TPU:1, one launch (start us, length us, event | category | flops | bytes accessed | tf_op | source)
XLA Modules:
  0.0 173.2 jit_solution(14802007470579433098)
XLA Ops:
  7.2 7.8 %collective-permute-start = (bf16[64,1536]{1,0:T(8,128)(2,1)}, bf16[64,1536]{1,0:T(8,128)(2,1)S(1)}, u32[]{:S(2)}, u32[]{:S(2)}) collective-permute-start(bf16[64,1536]{1,0:T(8,128)(2,1)} %param.4), channel_id=1, source_target_pairs={{0,32},{32,0},{1,33},{33,1},{2,34},{34,2},{3,35},{35,3},{4,36},{36... | collective-permute-start | bytes 589832 | tf_op jit(solution)/shard_map/ppermute | solution.py:27
  19.2 2.9 %collective-permute-start.2 = (bf16[2,2,64,384]{3,2,1,0:T(8,128)(2,1)}, bf16[2,2,64,384]{3,2,1,0:T(8,128)(2,1)S(1)}, u32[]{:S(2)}, u32[]{:S(2)}) collective-permute-start(bf16[2,2,64,384]{3,2,1,0:T(8,128)(2,1)} %get-tuple-element.78), channel_id=1, source_target_pairs={{0,128},{64,192},{128,0},{192,64},{1,129},{65,193},{129,1},{193,65... | collective-permute-start | bytes 589832 | tf_op jit(solution)/shard_map/ppermute | solution.py:27
  24.4 1.9 %collective-permute-done.2 = bf16[2,2,64,384]{3,2,1,0:T(8,128)(2,1)S(1)} collective-permute-done((bf16[2,2,64,384]{3,2,1,0:T(8,128)(2,1)}, bf16[2,2,64,384]{3,2,1,0:T(8,128)(2,1)S(1)}, u32[]{:S(2)}, u32[]{:S(2)}) %collective-permute-start.2) | collective-permute-done | bytes 196640 | tf_op jit(solution)/shard_map/ppermute | solution.py:27
  26.4 5.0 %collective-permute-done.3 = bf16[2,2,64,384]{3,2,1,0:T(8,128)(2,1)S(1)} collective-permute-done((bf16[2,2,64,384]{3,2,1,0:T(8,128)(2,1)}, bf16[2,2,64,384]{3,2,1,0:T(8,128)(2,1)S(1)}, u32[]{:S(2)}, u32[]{:S(2)}) %collective-permute-start.3) | collective-permute-done | bytes 196640 | tf_op jit(solution)/shard_map/ppermute | solution.py:27
  33.2 2.0 %broadcast_select_fusion.3 = (bf16[2,4,64,384]{3,2,1,0:T(8,128)(2,1)}, bf16[2,4,64,384]{3,2,1,0:T(8,128)(2,1)}) fusion(pred[]{:T(512)S(6)} %eq.45, bf16[2,1,64,384]{3,2,1,0:T(8,128)(2,1)} %copy-done.10, bf16[2,1,64,384]{3,2,1,0:T(8,128)(2,1)S(1)} %get-tuple-element.61, bf16[2,1,64,384]{3,2,1,0:T(8,128)(2,1)} %copy-done.9, ...), kind=kLoop, calls=%fused_computation.75 | loop fusion | flops 1572864 | bytes 1572866 | tf_op jit(solution)/shard_map/jit(_where)/select_n | solution.py:89
  36.8 2.5 %collective-permute-start.6 = (bf16[64,1536]{1,0:T(8,128)(2,1)}, bf16[64,1536]{1,0:T(8,128)(2,1)S(1)}, u32[]{:S(2)}, u32[]{:S(2)}) collective-permute-start(bf16[64,1536]{1,0:T(8,128)(2,1)} %param.4), channel_id=1, source_target_pairs={{0,6},{2,0},{4,2},{6,4},{1,7},{3,1},{5,3},{7,5},{8,14},{10,8},{12,... | collective-permute-start | bytes 589832 | tf_op jit(solution)/shard_map/ppermute | solution.py:27
  40.4 4.0 %collective-permute-done.6 = bf16[64,1536]{1,0:T(8,128)(2,1)S(1)} collective-permute-done((bf16[64,1536]{1,0:T(8,128)(2,1)}, bf16[64,1536]{1,0:T(8,128)(2,1)S(1)}, u32[]{:S(2)}, u32[]{:S(2)}) %collective-permute-start.6) | collective-permute-done | bytes 196640 | tf_op jit(solution)/shard_map/ppermute | solution.py:27
  45.6 7.3 %collective-permute-done.4 = bf16[64,1536]{1,0:T(8,128)(2,1)} collective-permute-done((bf16[64,1536]{1,0:T(8,128)(2,1)}, bf16[64,1536]{1,0:T(8,128)(2,1)}, u32[]{:S(2)}, u32[]{:S(2)}) %collective-permute-start.4) | collective-permute-done | bytes 196640 | tf_op jit(solution)/shard_map/ppermute | solution.py:27
  63.1 7.9 %collective-permute-start.12 = (bf16[5,64,1536]{2,1,0:T(8,128)(2,1)}, bf16[5,64,1536]{2,1,0:T(8,128)(2,1)}, u32[]{:S(2)}, u32[]{:S(2)}) collective-permute-start(bf16[5,64,1536]{2,1,0:T(8,128)(2,1)} %bitcast_dynamic-update-slice_fusion), channel_id=1, source_target_pairs={{0,1},{1,0},{2,3},{3,2},{4,5},{5,4},{6,7},{7,6},{8,9},{9,8},{10,11... | collective-permute-start | bytes 2949128 | tf_op jit(solution)/shard_map/ppermute | solution.py:27
  74.7 4.5 %collective-permute-start.16 = (bf16[2,4,64,384]{3,2,1,0:T(8,128)(2,1)}, bf16[2,4,64,384]{3,2,1,0:T(8,128)(2,1)S(1)}, u32[]{:S(2)}, u32[]{:S(2)}) collective-permute-start(bf16[2,4,64,384]{3,2,1,0:T(8,128)(2,1)} %get-tuple-element.102), channel_id=1, source_target_pairs={{0,8},{8,16},{16,24},{32,40},{40,48},{48,56},{1,9},{9,17},{17,25},... | collective-permute-start | bytes 1179656 | tf_op jit(solution)/shard_map/ppermute | solution.py:32
  79.3 5.6 %collective-permute-done.17 = bf16[2,4,64,384]{3,2,1,0:T(8,128)(2,1)S(1)} collective-permute-done((bf16[2,4,64,384]{3,2,1,0:T(8,128)(2,1)}, bf16[2,4,64,384]{3,2,1,0:T(8,128)(2,1)S(1)}, u32[]{:S(2)}, u32[]{:S(2)}) %collective-permute-start.17) | collective-permute-done | bytes 393248 | tf_op jit(solution)/shard_map/ppermute | solution.py:32
  84.9 2.8 %collective-permute-done.16 = bf16[2,4,64,384]{3,2,1,0:T(8,128)(2,1)S(1)} collective-permute-done((bf16[2,4,64,384]{3,2,1,0:T(8,128)(2,1)}, bf16[2,4,64,384]{3,2,1,0:T(8,128)(2,1)S(1)}, u32[]{:S(2)}, u32[]{:S(2)}) %collective-permute-start.16) | collective-permute-done | bytes 393248 | tf_op jit(solution)/shard_map/ppermute | solution.py:32
  94.0 8.1 %fusion.28 = f32[512,3072]{0,1:T(8,128)S(1)} fusion(bf16[512,1536]{1,0:T(8,128)(2,1)S(1)} %bitcast.198, bf16[3072,1536]{1,0:T(8,128)(2,1)} %param.5), kind=kOutput, calls=%fused_computation.134 | convolution fusion | flops 4831838208 | bytes 17301504 | tf_op jit(solution)/shard_map/dot_general | solution.py:106
  102.3 2.4 %copy-done = f32[512,3072]{0,1:T(8,128)} copy-done((f32[512,3072]{0,1:T(8,128)}, f32[512,3072]{0,1:T(8,128)S(1)}, u32[]{:S(2)}) %copy-start) | copy-done | bytes 6291480
  107.6 12.7 %collective-permute-start.13 = (f16[128,3200]{0,1:T(8,128)(2,1)}, f16[128,3200]{0,1:T(8,128)(2,1)}, u32[]{:S(2)}, u32[]{:S(2)}) collective-permute-start(f16[128,3200]{0,1:T(8,128)(2,1)} %pad_maximum_fusion.3), channel_id=1, source_target_pairs={{0,8},{8,16},{32,40},{40,48},{1,9},{9,17},{33,41},{41,49},{2,10},{... | collective-permute-start | bytes 2457608 | tf_op jit(solution)/shard_map/ppermute | solution.py:32
  123.8 1.7 select_select_fusion.3
  125.9 6.9 %collective-permute-done.24 = bf16[2,4,64,384]{3,2,1,0:T(8,128)(2,1)} collective-permute-done((bf16[2,4,64,384]{3,2,1,0:T(8,128)(2,1)}, bf16[2,4,64,384]{3,2,1,0:T(8,128)(2,1)}, u32[]{:S(2)}, u32[]{:S(2)}) %collective-permute-start.24) | collective-permute-done | bytes 393248 | tf_op jit(solution)/shard_map/ppermute | solution.py:37
  137.1 1.9 %abs_reduce_fusion = (f32[128]{0:T(128)S(1)}, f32[128]{0:T(128)S(1)}) fusion(f32[512,3072]{0,1:T(8,128)S(1)} %bitcast.190, f32[128]{0:T(128)S(1)} %get-tuple-element.111, f16[128,3200]{0,1:T(8,128)(2,1)} %collective-permute-done.14, f32[128]{0:T(128)S(1)} %get-tuple-element.112, f16[128,3200]{0,1:T(8,128)(2,1)} %collective-permute-done.13), kind=kLoop, calls=%fused_computation.38 | loop fusion | flops 3931904 | bytes 4720640 | tf_op jit(solution)/shard_map/reduce_max | solution.py:49
  139.0 2.1 %multiply_convert_fusion = (f16[128,3072]{0,1:T(8,128)(2,1)S(1)}, f16[128,3072]{0,1:T(8,128)(2,1)S(1)}) fusion(f32[512,3072]{0,1:T(8,128)S(1)} %bitcast.190, f32[128]{0:T(128)S(1)} %get-tuple-element.103, f32[128]{0:T(128)S(1)} %get-tuple-element.111, f16[128,3200]{0,1:T(8,128)(2,1)} %collective-permute-done.14, f32[128]{0:T(128)S(1)} %get-tuple-element.105, ...), kind=kLoop, calls=%fused_computation.37 | loop fusion | flops 3932160 | bytes 6293504 | tf_op jit(solution)/shard_map/convert_element_type | solution.py:51
  141.4 2.6 %collective-permute-start.23 = (f16[128,3200]{0,1:T(8,128)(2,1)S(1)}, f16[128,3200]{0,1:T(8,128)(2,1)S(1)}, u32[]{:S(2)}, u32[]{:S(2)}) collective-permute-start(f16[128,3200]{0,1:T(8,128)(2,1)S(1)} %pad_maximum_fusion.5), channel_id=1, source_target_pairs={{0,56},{8,0},{16,8},{24,16},{32,24},{40,32},{48,40},{56,48},{1,57}... | collective-permute-start | bytes 2457608 | tf_op jit(solution)/shard_map/ppermute | solution.py:32
  144.6 2.7 %fusion.29 = f32[384,1536]{1,0:T(8,128)S(1)} fusion(bf16[2048,384]{1,0:T(8,128)(2,1)S(1)} %bitcast.195, bf16[2048,1536]{1,0:T(8,128)(2,1)S(1)} %bitcast.194), kind=kOutput, calls=%fused_computation.135 | convolution fusion | flops 2415919104 | bytes 10223616 | tf_op jit(solution)/shard_map/dot_general | solution.py:155
  147.2 4.0 %broadcast_multiply_fusion = f32[384,1536]{1,0:T(8,128)} fusion(f32[384,1536]{1,0:T(8,128)S(1)} %fusion.29, bf16[4,4,2,64,1536]{4,3,2,1,0:T(8,128)(2,1)S(1)} %collective-permute-done.25, bf16[4,4,2,64,384]{4,3,1,2,0:T(8,128)(2,1)S(1)} %pad_maximum_fusion.2), kind=kOutput, calls=%fused_computation.45 | convolution fusion | flops 2417098752 | bytes 12582912 | tf_op jit(solution)/shard_map/dot_general | solution.py:155
  151.3 9.1 %collective-permute-done.23 = f16[128,3200]{0,1:T(8,128)(2,1)S(1)} collective-permute-done((f16[128,3200]{0,1:T(8,128)(2,1)S(1)}, f16[128,3200]{0,1:T(8,128)(2,1)S(1)}, u32[]{:S(2)}, u32[]{:S(2)}) %collective-permute-start.23) | collective-permute-done | bytes 819232 | tf_op jit(solution)/shard_map/ppermute | solution.py:32
  160.4 4.4 %collective-permute-done.22 = f16[128,3200]{0,1:T(8,128)(2,1)S(1)} collective-permute-done((f16[128,3200]{0,1:T(8,128)(2,1)S(1)}, f16[128,3200]{0,1:T(8,128)(2,1)S(1)}, u32[]{:S(2)}, u32[]{:S(2)}) %collective-permute-start.22) | collective-permute-done | bytes 819232 | tf_op jit(solution)/shard_map/ppermute | solution.py:32
  (132 shorter events, 45.6 us)
Async XLA Ops:
  7.2 115.3 %all-gather.3.cloned.1.call-start = ((), (), s32[]{:S(2)}) async-start(), calls=%async_computation | async-start | bytes 6684672 | tf_op jit(solution)/shard_map/all_gather | solution.py:86
  7.2 16.4 %collective-permute-start = (bf16[64,1536]{1,0:T(8,128)(2,1)}, bf16[64,1536]{1,0:T(8,128)(2,1)S(1)}, u32[]{:S(2)}, u32[]{:S(2)}) collective-permute-start(bf16[64,1536]{1,0:T(8,128)(2,1)} %param.4), channel_id=1, source_target_pairs={{0,32},{32,0},{1,33},{33,1},{2,34},{34,2},{3,35},{35,3},{4,36},{36... | collective-permute-start | bytes 589832 | tf_op jit(solution)/shard_map/ppermute | solution.py:27
  22.1 9.3 %collective-permute-start.3 = (bf16[2,2,64,384]{3,2,1,0:T(8,128)(2,1)}, bf16[2,2,64,384]{3,2,1,0:T(8,128)(2,1)S(1)}, u32[]{:S(2)}, u32[]{:S(2)}) collective-permute-start(bf16[2,2,64,384]{3,2,1,0:T(8,128)(2,1)} %get-tuple-element.79), channel_id=1, source_target_pairs={{0,192},{64,0},{128,64},{192,128},{1,193},{65,1},{129,65},{193,129... | collective-permute-start | bytes 589832 | tf_op jit(solution)/shard_map/ppermute | solution.py:27
  22.9 8.5 %collective-permute-start.1 = (bf16[2,2,64,384]{3,2,1,0:T(8,128)(2,1)S(1)}, bf16[2,2,64,384]{3,2,1,0:T(8,128)(2,1)S(1)}, u32[]{:S(2)}, u32[]{:S(2)}) collective-permute-start(bf16[2,2,64,384]{3,2,1,0:T(8,128)(2,1)S(1)} %get-tuple-element.80), channel_id=1, source_target_pairs={{0,64},{64,128},{128,192},{192,0},{1,65},{65,129},{129,193},{193,1... | collective-permute-start | bytes 589832 | tf_op jit(solution)/shard_map/ppermute | solution.py:27
  35.2 17.7 %collective-permute-start.8 = (bf16[2,4,64,384]{3,2,1,0:T(8,128)(2,1)}, bf16[2,4,64,384]{3,2,1,0:T(8,128)(2,1)S(1)}, u32[]{:S(2)}, u32[]{:S(2)}) collective-permute-start(bf16[2,4,64,384]{3,2,1,0:T(8,128)(2,1)} %get-tuple-element.76), channel_id=1, source_target_pairs={{0,56},{8,0},{16,8},{24,16},{32,24},{40,32},{48,40},{56,48},{1,57}... | collective-permute-start | bytes 1179656 | tf_op jit(solution)/shard_map/ppermute | solution.py:32
  35.3 17.6 %collective-permute-start.7 = (bf16[2,4,64,384]{3,2,1,0:T(8,128)(2,1)}, bf16[2,4,64,384]{3,2,1,0:T(8,128)(2,1)S(1)}, u32[]{:S(2)}, u32[]{:S(2)}) collective-permute-start(bf16[2,4,64,384]{3,2,1,0:T(8,128)(2,1)} %get-tuple-element.77), channel_id=1, source_target_pairs={{0,8},{8,16},{16,24},{24,32},{32,40},{40,48},{48,56},{56,0},{1,9},... | collective-permute-start | bytes 1179656 | tf_op jit(solution)/shard_map/ppermute | solution.py:32
  36.8 7.6 %collective-permute-start.6 = (bf16[64,1536]{1,0:T(8,128)(2,1)}, bf16[64,1536]{1,0:T(8,128)(2,1)S(1)}, u32[]{:S(2)}, u32[]{:S(2)}) collective-permute-start(bf16[64,1536]{1,0:T(8,128)(2,1)} %param.4), channel_id=1, source_target_pairs={{0,6},{2,0},{4,2},{6,4},{1,7},{3,1},{5,3},{7,5},{8,14},{10,8},{12,... | collective-permute-start | bytes 589832 | tf_op jit(solution)/shard_map/ppermute | solution.py:27
  39.8 13.1 %collective-permute-start.4 = (bf16[64,1536]{1,0:T(8,128)(2,1)}, bf16[64,1536]{1,0:T(8,128)(2,1)}, u32[]{:S(2)}, u32[]{:S(2)}) collective-permute-start(bf16[64,1536]{1,0:T(8,128)(2,1)} %param.4), channel_id=1, source_target_pairs={{0,2},{2,4},{4,6},{6,0},{1,3},{3,5},{5,7},{7,1},{8,10},{10,12},{12... | collective-permute-start | bytes 589832 | tf_op jit(solution)/shard_map/ppermute | solution.py:27
  44.4 26.6 %collective-permute-start.15 = (bf16[2,4,64,384]{3,2,1,0:T(8,128)(2,1)}, bf16[2,4,64,384]{3,2,1,0:T(8,128)(2,1)S(1)}, u32[]{:S(2)}, u32[]{:S(2)}) collective-permute-start(bf16[2,4,64,384]{3,2,1,0:T(8,128)(2,1)} %pad_maximum_fusion.7), channel_id=1, source_target_pairs={{0,48},{8,56},{16,32},{24,40},{32,16},{40,24},{48,0},{56,8},{1,49}... | collective-permute-start | bytes 1179656 | tf_op jit(solution)/shard_map/ppermute | solution.py:37
  52.9 8.2 %collective-permute-start.11 = (bf16[64,1536]{1,0:T(8,128)(2,1)}, bf16[64,1536]{1,0:T(8,128)(2,1)S(1)}, u32[]{:S(2)}, u32[]{:S(2)}) collective-permute-start(bf16[64,1536]{1,0:T(8,128)(2,1)} %copy-done.11), channel_id=1, source_target_pairs={{6,4},{24,30},{7,5},{25,31},{38,36},{56,62},{39,37},{57,63},{70,68... | collective-permute-start | bytes 589832 | tf_op jit(solution)/shard_map/ppermute | solution.py:97
  53.6 7.5 %collective-permute-start.10 = (bf16[64,1536]{1,0:T(8,128)(2,1)}, bf16[64,1536]{1,0:T(8,128)(2,1)S(1)}, u32[]{:S(2)}, u32[]{:S(2)}) collective-permute-start(bf16[64,1536]{1,0:T(8,128)(2,1)} %copy-done.11), channel_id=1, source_target_pairs={{6,2},{24,28},{7,3},{25,29},{38,34},{56,60},{39,35},{57,61},{70,66... | collective-permute-start | bytes 589832 | tf_op jit(solution)/shard_map/ppermute | solution.py:97
  54.3 8.1 %collective-permute-start.9 = (bf16[64,1536]{1,0:T(8,128)(2,1)}, bf16[64,1536]{1,0:T(8,128)(2,1)S(1)}, u32[]{:S(2)}, u32[]{:S(2)}) collective-permute-start(bf16[64,1536]{1,0:T(8,128)(2,1)} %copy-done.11), channel_id=1, source_target_pairs={{6,0},{24,26},{7,1},{25,27},{38,32},{56,58},{39,33},{57,59},{70,64... | collective-permute-start | bytes 589832 | tf_op jit(solution)/shard_map/ppermute | solution.py:97
  63.1 28.7 %collective-permute-start.12 = (bf16[5,64,1536]{2,1,0:T(8,128)(2,1)}, bf16[5,64,1536]{2,1,0:T(8,128)(2,1)}, u32[]{:S(2)}, u32[]{:S(2)}) collective-permute-start(bf16[5,64,1536]{2,1,0:T(8,128)(2,1)} %bitcast_dynamic-update-slice_fusion), channel_id=1, source_target_pairs={{0,1},{1,0},{2,3},{3,2},{4,5},{5,4},{6,7},{7,6},{8,9},{9,8},{10,11... | collective-permute-start | bytes 2949128 | tf_op jit(solution)/shard_map/ppermute | solution.py:27
  72.0 12.9 %collective-permute-start.17 = (bf16[2,4,64,384]{3,2,1,0:T(8,128)(2,1)}, bf16[2,4,64,384]{3,2,1,0:T(8,128)(2,1)S(1)}, u32[]{:S(2)}, u32[]{:S(2)}) collective-permute-start(bf16[2,4,64,384]{3,2,1,0:T(8,128)(2,1)} %get-tuple-element.101), channel_id=1, source_target_pairs={{24,16},{16,8},{8,0},{56,48},{48,40},{40,32},{25,17},{17,9},{9,1},... | collective-permute-start | bytes 1179656 | tf_op jit(solution)/shard_map/ppermute | solution.py:32
  74.7 13.0 %collective-permute-start.16 = (bf16[2,4,64,384]{3,2,1,0:T(8,128)(2,1)}, bf16[2,4,64,384]{3,2,1,0:T(8,128)(2,1)S(1)}, u32[]{:S(2)}, u32[]{:S(2)}) collective-permute-start(bf16[2,4,64,384]{3,2,1,0:T(8,128)(2,1)} %get-tuple-element.102), channel_id=1, source_target_pairs={{0,8},{8,16},{16,24},{32,40},{40,48},{48,56},{1,9},{9,17},{17,25},... | collective-permute-start | bytes 1179656 | tf_op jit(solution)/shard_map/ppermute | solution.py:32
  87.7 32.7 %collective-permute-start.21 = (bf16[2,4,64,384]{3,2,1,0:T(8,128)(2,1)}, bf16[2,4,64,384]{3,2,1,0:T(8,128)(2,1)S(1)}, u32[]{:S(2)}, u32[]{:S(2)}) collective-permute-start(bf16[2,4,64,384]{3,2,1,0:T(8,128)(2,1)} %collective-permute-done.18), channel_id=1, source_target_pairs={{8,0},{16,24},{40,32},{48,56},{9,1},{17,25},{41,33},{49,57},{10,2}... | collective-permute-start | bytes 1179656 | tf_op jit(solution)/shard_map/ppermute | solution.py:37
  89.1 31.3 %collective-permute-start.20 = (bf16[2,4,64,384]{3,2,1,0:T(8,128)(2,1)S(1)}, bf16[2,4,64,384]{3,2,1,0:T(8,128)(2,1)}, u32[]{:S(2)}, u32[]{:S(2)}) collective-permute-start(bf16[2,4,64,384]{3,2,1,0:T(8,128)(2,1)S(1)} %get-tuple-element.74), channel_id=1, source_target_pairs={{8,0},{16,24},{40,32},{48,56},{9,1},{17,25},{41,33},{49,57},{10,2}... | collective-permute-start | bytes 1179656 | tf_op jit(solution)/shard_map/ppermute | solution.py:37
  90.4 30.0 %collective-permute-start.19 = (bf16[2,4,64,384]{3,2,1,0:T(8,128)(2,1)S(1)}, bf16[2,4,64,384]{3,2,1,0:T(8,128)(2,1)}, u32[]{:S(2)}, u32[]{:S(2)}) collective-permute-start(bf16[2,4,64,384]{3,2,1,0:T(8,128)(2,1)S(1)} %get-tuple-element.75), channel_id=1, source_target_pairs={{8,16},{16,8},{40,48},{48,40},{9,17},{17,9},{41,49},{49,41},{10,18... | collective-permute-start | bytes 1179656 | tf_op jit(solution)/shard_map/ppermute | solution.py:37
  106.1 29.1 %collective-permute-start.14 = (f16[128,3200]{0,1:T(8,128)(2,1)}, f16[128,3200]{0,1:T(8,128)(2,1)}, u32[]{:S(2)}, u32[]{:S(2)}) collective-permute-start(f16[128,3200]{0,1:T(8,128)(2,1)} %pad_maximum_fusion.3), channel_id=1, source_target_pairs={{16,8},{24,16},{48,40},{56,48},{17,9},{25,17},{49,41},{57,49},{18,... | collective-permute-start | bytes 2457608 | tf_op jit(solution)/shard_map/ppermute | solution.py:32
  107.6 28.7 %collective-permute-start.13 = (f16[128,3200]{0,1:T(8,128)(2,1)}, f16[128,3200]{0,1:T(8,128)(2,1)}, u32[]{:S(2)}, u32[]{:S(2)}) collective-permute-start(f16[128,3200]{0,1:T(8,128)(2,1)} %pad_maximum_fusion.3), channel_id=1, source_target_pairs={{0,8},{8,16},{32,40},{40,48},{1,9},{9,17},{33,41},{41,49},{2,10},{... | collective-permute-start | bytes 2457608 | tf_op jit(solution)/shard_map/ppermute | solution.py:32
  121.1 11.6 %collective-permute-start.24 = (bf16[2,4,64,384]{3,2,1,0:T(8,128)(2,1)}, bf16[2,4,64,384]{3,2,1,0:T(8,128)(2,1)}, u32[]{:S(2)}, u32[]{:S(2)}) collective-permute-start(bf16[2,4,64,384]{3,2,1,0:T(8,128)(2,1)} %collective-permute-done.19), channel_id=1, source_target_pairs={{8,0},{16,24},{40,32},{48,56},{9,1},{17,25},{41,33},{49,57},{10,2}... | collective-permute-start | bytes 1179656 | tf_op jit(solution)/shard_map/ppermute | solution.py:37
  122.5 24.8 %collective-permute-start.25 = (bf16[4,4,2,64,1536]{4,3,2,1,0:T(8,128)(2,1)}, bf16[4,4,2,64,1536]{4,3,2,1,0:T(8,128)(2,1)S(1)}, u32[]{:S(2)}, u32[]{:S(2)}) collective-permute-start(bf16[4,4,2,64,1536]{4,3,2,1,0:T(8,128)(2,1)} %bitcast.191), channel_id=1, source_target_pairs={{0,1},{1,0},{2,3},{3,2},{4,5},{5,4},{6,7},{7,6},{8,9},{9,8},{10,11... | collective-permute-start | bytes 18874376 | tf_op jit(solution)/shard_map/ppermute | solution.py:27
  141.4 19.0 %collective-permute-start.23 = (f16[128,3200]{0,1:T(8,128)(2,1)S(1)}, f16[128,3200]{0,1:T(8,128)(2,1)S(1)}, u32[]{:S(2)}, u32[]{:S(2)}) collective-permute-start(f16[128,3200]{0,1:T(8,128)(2,1)S(1)} %pad_maximum_fusion.5), channel_id=1, source_target_pairs={{0,56},{8,0},{16,8},{24,16},{32,24},{40,32},{48,40},{56,48},{1,57}... | collective-permute-start | bytes 2457608 | tf_op jit(solution)/shard_map/ppermute | solution.py:32
  144.2 20.6 %collective-permute-start.22 = (f16[128,3200]{0,1:T(8,128)(2,1)S(1)}, f16[128,3200]{0,1:T(8,128)(2,1)S(1)}, u32[]{:S(2)}, u32[]{:S(2)}) collective-permute-start(f16[128,3200]{0,1:T(8,128)(2,1)S(1)} %pad_maximum_fusion.4), channel_id=1, source_target_pairs={{0,8},{8,16},{16,24},{24,32},{32,40},{40,48},{48,56},{56,0},{1,9},... | collective-permute-start | bytes 2457608 | tf_op jit(solution)/shard_map/ppermute | solution.py:32
  (23 other events, 161.6 us)
Sparse Core Ops, SparseCore 0:
  33.3 66.2 all-gather.2

commit v7 on v6

--- a/solution.py
+++ b/solution.py
@@ -91,42 +91,45 @@
 
     near_g = after(grad_out, own, cross)
     from_x = [near_g] + [shift(near_g, "x", t) for t in (1, 2, 3)]
-    p, *from_x = lax.optimization_barrier((p, *from_x, a_up, a_down))[:5]
+    from_x = lax.optimization_barrier((*from_x, a_up, a_down, b))[:4]
+    mine = jnp.stack(from_x)
+    mine = jnp.stack([mine, shift(mine, "core", 1)], axis=1)
+
+    def partial(*blocks):
+        rows = jnp.stack(blocks)
+        rows = jnp.where(c == 1, rows[:, ::-1], rows).reshape(-1, feats)
+        sums = lax.dot_general(
+            rows, down_weight, (((1,), (1,)), ((), ())), preferred_element_type=jnp.float32
+        )
+        return [sums[k * tokens : (k + 1) * tokens] for k in range(len(blocks))]
+
+    part_far, part_own = partial(*(at(mine, (x - zl - k) % 4) for k in (2, 0)))
+    far = pack(part_far)
+    p = after(p, far)
     beyond = jnp.where(jnp.where(e0, x == 3, x == 0), p, jnp.zeros_like(p))
     for t in (1, 2, 3):
         beyond = beyond + lax.ppermute(p, ("zl", "x"), [(3, (3 + t) % 4), (12, 12 + t)])
-    mine = jnp.stack(from_x + [beyond])
-    mine = jnp.stack([mine, shift(mine, "core", 1)], axis=1)
-
-    place = [(x - zl - k) % 4 for k in (2, 1, -1, 0)]
-    place[1] = jnp.where(e3, 4, place[1])
-    place[2] = jnp.where(e0, 4, place[2])
-    rows = jnp.stack([at(mine, k) for k in place])
-    rows = jnp.where(c == 1, rows[:, ::-1], rows).reshape(4 * tokens, feats)
-    parts = lax.dot_general(
-        rows, down_weight, (((1,), (1,)), ((), ())), preferred_element_type=jnp.float32
-    )
-    part_far, part_up, part_down, part_own = (
-        parts[k * tokens : (k + 1) * tokens] for k in range(4)
-    )
-    far = pack(part_far)
+    beyond = jnp.stack([beyond, shift(beyond, "core", 1)])
+    up, down = (at(mine, (x - zl - k) % 4) for k in (1, -1))
+    part_up, part_down = partial(jnp.where(e3, beyond, up), jnp.where(e0, beyond, down))
 
     far_up = along_z(far, 1, (0, 1))
     far_down = along_z(far, -1, (2, 3))
     c_up = along_z(jnp.where(e0, b, a_up), 1, (0, 1, 2))
     c_down = along_z(jnp.where(e3, b, a_down), -1, (3, 2, 1))
     d = pairs_z(b, {1: 1, 2: -1})
-    c_up, c_down, d = lax.optimization_barrier((c_up, c_down, d))
+    c_up, c_down, d = lax.optimization_barrier((c_up, c_down, d, far))[:3]
     e = pairs_z(jnp.where(zl == 1, c_up, c_down), {1: 1, 2: -1})
     f = pairs_z(jnp.where(zl == 2, c_up, c_down), {1: -1, 2: 1})
     g = pairs_z(d, {1: -1, 2: 1})
-    e, f, g, far = lax.optimization_barrier((e, f, g, far))
+    e, f, g = lax.optimization_barrier((e, f, g))
     h = pairs_z(e, {1: -1, 2: 1})
-    far_up, far_down = lax.optimization_barrier((far_up, far_down, e, f, g))[:2]
+    far_up, far_down = lax.optimization_barrier((far_up, far_down, g))[:2]
     near_up = pack(part_up + unpack(far_up))
     near_down = pack(part_down + unpack(far_down))
     from_below = along_z(near_up, 1, range(4))
     from_above = along_z(near_down, -1, range(4))
+    h = after(h, near_up, near_down)
     other_rows = shift(after(all_rows, e, f, g), "core", 1)
 
     def choose(*units):

time: 175 us -> 162 us (0.926)
  starting transfers between devices: 58.9 us -> 51.5 us
  local copies, waits for them, and re-layouts: 13.7 us -> 6.93 us
  matrix products: 14.8 us -> 17.3 us
    ppermute x8, waiting for transfers between devices: 23 us -> 11.5 us  [along_z(): return lax.ppermute(v, Z, pairs)]
    ppermute x6, waiting for transfers between devices: 6.87 us -> 16.8 us  [pairs_z(): return lax.ppermute(v, Z, pairs)]
    unnamed x46 -> x70, local copies, waits for them, and re-layouts: 12.1 us -> 5.28 us
    ppermute x3, waiting for transfers between devices: 1.25 us -> 7.85 us  [on_device(): lax.ppermute(p, ('zl', 'x'), [(3, (3 + t) % 4), (12, 12 + t)])]
    ppermute x9 -> x10, waiting for transfers between devices: 19.5 us -> 15 us  [shift(): return lax.ppermute(v, axis, [(i, (i + step) % n) for i in range(n)])]
    ppermute x8, starting transfers between devices: 24.5 us -> 20.4 us  [along_z(): return lax.ppermute(v, Z, pairs)]
    ppermute x9 -> x10, starting transfers between devices: 25 us -> 21.7 us  [shift(): return lax.ppermute(v, axis, [(i, (i + step) % n) for i in range(n)])]
    dot_general x1 -> x2, matrix products: 8.06 us -> 10.6 us  [partial(): lax.dot_general(rows, down_weight, (((1,), (1,)), ((), ())), preferred_el...]
  transfers between devices with their start and end apart: 27 -> 28, of which waited for: 12 -> 12; matrix products, arithmetic and copies ran while one was open for 24% -> 24% of each run, Pallas kernels for 0% -> 0%
where the time goes in v7:
time: 162 us
  starting transfers between devices  51.5 us (32%)
  waiting for transfers between devices  51.2 us (32%)
  other arithmetic  19.7 us (12%)
  matrix products  17.3 us (11%)
  between operations  15 us (9%)
  local copies, waits for them, and re-layouts  6.93 us (4%)
    ppermute x10, starting transfers between devices, shift(): return lax.ppermute(v, axis, [(i, (i + step) % n) for i in range(n)])  21.7 us
    ppermute x8, starting transfers between devices, along_z(): return lax.ppermute(v, Z, pairs)  20.4 us
    ppermute x6, waiting for transfers between devices, pairs_z(): return lax.ppermute(v, Z, pairs)  16.8 us
    ppermute x10, waiting for transfers between devices, shift(): return lax.ppermute(v, axis, [(i, (i + step) % n) for i in range(n)])  15 us
    ppermute x8, waiting for transfers between devices, along_z(): return lax.ppermute(v, Z, pairs)  11.5 us
    dot_general x2, matrix products, partial(): lax.dot_general(rows, down_weight, (((1,), (1,)), ((), ())), preferred_el...  10.6 us
    ppermute x3, waiting for transfers between devices, on_device(): lax.ppermute(p, ('zl', 'x'), [(3, (3 + t) % 4), (12, 12 + t)])  7.85 us
    ppermute x6, starting transfers between devices, pairs_z(): return lax.ppermute(v, Z, pairs)  6.7 us
  transfers between devices with their start and end apart: 28, of which 12 were waited for; matrix products, arithmetic and copies ran while one was open for 24% of the time, Pallas kernels for 0%

profile of v7, /device:TPU:1, one launch (start us, length us, event | category | flops | bytes accessed | tf_op | source)
XLA Modules:
  0.0 161.6 jit_solution(18445302768202770670)
XLA Ops:
  7.2 7.8 %collective-permute-start.10 = (bf16[64,1536]{1,0:T(8,128)(2,1)}, bf16[64,1536]{1,0:T(8,128)(2,1)S(1)}, u32[]{:S(2)}, u32[]{:S(2)}) collective-permute-start(bf16[64,1536]{1,0:T(8,128)(2,1)} %param.4), channel_id=1, source_target_pairs={{0,32},{32,0},{1,33},{33,1},{2,34},{34,2},{3,35},{35,3},{4,36},{36... | collective-permute-start | bytes 589832 | tf_op jit(solution)/shard_map/ppermute | solution.py:27
  16.5 2.2 %fusion.6 = (f32[128,3072]{0,1:T(8,128)}, bf16[128,3072]{0,1:T(8,128)(2,1)S(1)}) fusion(bf16[128,3072]{0,1:T(8,128)(2,1)S(1)} %copy.52), kind=kLoop, calls=%fused_computation.22 | loop fusion | flops 7864320 | bytes 3145728 | tf_op jit(solution)/shard_map/add | solution.py:19
  19.6 3.0 %collective-permute-start.1 = (bf16[2,2,64,384]{3,2,1,0:T(8,128)(2,1)S(1)}, bf16[2,2,64,384]{3,2,1,0:T(8,128)(2,1)S(1)}, u32[]{:S(2)}, u32[]{:S(2)}) collective-permute-start(bf16[2,2,64,384]{3,2,1,0:T(8,128)(2,1)S(1)} %get-tuple-element.82), channel_id=1, source_target_pairs={{0,128},{64,192},{128,0},{192,64},{1,129},{65,193},{129,1},{193,65... | collective-permute-start | bytes 589832 | tf_op jit(solution)/shard_map/ppermute | solution.py:27
  24.9 1.8 %collective-permute-done.1 = bf16[2,2,64,384]{3,2,1,0:T(8,128)(2,1)S(1)} collective-permute-done((bf16[2,2,64,384]{3,2,1,0:T(8,128)(2,1)S(1)}, bf16[2,2,64,384]{3,2,1,0:T(8,128)(2,1)S(1)}, u32[]{:S(2)}, u32[]{:S(2)}) %collective-permute-start.1) | collective-permute-done | bytes 196640 | tf_op jit(solution)/shard_map/ppermute | solution.py:27
  26.7 4.9 %collective-permute-done.2 = bf16[2,2,64,384]{3,2,1,0:T(8,128)(2,1)S(1)} collective-permute-done((bf16[2,2,64,384]{3,2,1,0:T(8,128)(2,1)S(1)}, bf16[2,2,64,384]{3,2,1,0:T(8,128)(2,1)S(1)}, u32[]{:S(2)}, u32[]{:S(2)}) %collective-permute-start.2) | collective-permute-done | bytes 196640 | tf_op jit(solution)/shard_map/ppermute | solution.py:27
  32.0 2.6 %collective-permute-start.5 = (bf16[64,1536]{1,0:T(8,128)(2,1)S(1)}, bf16[64,1536]{1,0:T(8,128)(2,1)S(1)}, u32[]{:S(2)}, u32[]{:S(2)}) collective-permute-start(bf16[64,1536]{1,0:T(8,128)(2,1)S(1)} %copy-done.31), channel_id=1, source_target_pairs={{0,6},{2,0},{4,2},{6,4},{1,7},{3,1},{5,3},{7,5},{8,14},{10,8},{12,... | collective-permute-start | bytes 589832 | tf_op jit(solution)/shard_map/ppermute | solution.py:27
  38.1 4.2 %collective-permute-done.4 = bf16[64,1536]{1,0:T(8,128)(2,1)S(1)} collective-permute-done((bf16[64,1536]{1,0:T(8,128)(2,1)S(1)}, bf16[64,1536]{1,0:T(8,128)(2,1)S(1)}, u32[]{:S(2)}, u32[]{:S(2)}) %collective-permute-start.4) | collective-permute-done | bytes 196640 | tf_op jit(solution)/shard_map/ppermute | solution.py:27
  42.3 3.7 %collective-permute-done.3 = bf16[64,1536]{1,0:T(8,128)(2,1)S(1)} collective-permute-done((bf16[64,1536]{1,0:T(8,128)(2,1)S(1)}, bf16[64,1536]{1,0:T(8,128)(2,1)S(1)}, u32[]{:S(2)}, u32[]{:S(2)}) %collective-permute-start.3) | collective-permute-done | bytes 196640 | tf_op jit(solution)/shard_map/ppermute | solution.py:27
  46.5 11.9 %collective-permute-done.8 = bf16[2,4,64,384]{3,2,1,0:T(8,128)(2,1)S(1)} collective-permute-done((bf16[2,4,64,384]{3,2,1,0:T(8,128)(2,1)S(1)}, bf16[2,4,64,384]{3,2,1,0:T(8,128)(2,1)S(1)}, u32[]{:S(2)}, u32[]{:S(2)}) %collective-permute-start.8) | collective-permute-done | bytes 393248 | tf_op jit(solution)/shard_map/ppermute | solution.py:37
  59.4 2.5 %collective-permute-start.9 = (bf16[4,64,1536]{2,1,0:T(8,128)(2,1)}, bf16[4,64,1536]{2,1,0:T(8,128)(2,1)S(1)}, u32[]{:S(2)}, u32[]{:S(2)}) collective-permute-start(bf16[4,64,1536]{2,1,0:T(8,128)(2,1)} %get-tuple-element.78), channel_id=1, source_target_pairs={{0,1},{1,0},{2,3},{3,2},{4,5},{5,4},{6,7},{7,6},{8,9},{9,8},{10,11... | collective-permute-start | bytes 2359304 | tf_op jit(solution)/shard_map/ppermute | solution.py:27
  63.4 7.2 %collective-permute-start.17 = (bf16[2,4,64,384]{3,2,1,0:T(8,128)(2,1)S(1)}, bf16[2,4,64,384]{3,2,1,0:T(8,128)(2,1)S(1)}, u32[]{:S(2)}, u32[]{:S(2)}) collective-permute-start(bf16[2,4,64,384]{3,2,1,0:T(8,128)(2,1)S(1)} %get-tuple-element.106), channel_id=1, source_target_pairs={{0,8},{8,16},{16,24},{32,40},{40,48},{48,56},{1,9},{9,17},{17,25},... | collective-permute-start | bytes 1179656 | tf_op jit(solution)/shard_map/ppermute | solution.py:32
  72.3 5.3 %fusion.31 = f32[256,3072]{0,1:T(8,128)S(1)} fusion(bf16[256,1536]{1,0:T(8,128)(2,1)S(1)} %bitcast.200, bf16[3072,1536]{1,0:T(8,128)(2,1)} %param.5), kind=kOutput, calls=%fused_computation.137 | convolution fusion | flops 2415919104 | bytes 13369344 | tf_op jit(solution)/shard_map/dot_general | solution.py:101
  88.1 7.8 %collective-permute-done.11 = bf16[64,1536]{1,0:T(8,128)(2,1)S(1)} collective-permute-done((bf16[64,1536]{1,0:T(8,128)(2,1)S(1)}, bf16[64,1536]{1,0:T(8,128)(2,1)S(1)}, u32[]{:S(2)}, u32[]{:S(2)}) %collective-permute-start.11) | collective-permute-done | bytes 196640 | tf_op jit(solution)/shard_map/ppermute | solution.py:111
  99.3 4.2 %collective-permute-start.15 = (f16[128,3200]{0,1:T(8,128)(2,1)}, f16[128,3200]{0,1:T(8,128)(2,1)}, u32[]{:S(2)}, u32[]{:S(2)}) collective-permute-start(f16[128,3200]{0,1:T(8,128)(2,1)} %pad_maximum_fusion.2), channel_id=1, source_target_pairs={{0,8},{8,16},{32,40},{40,48},{1,9},{9,17},{33,41},{41,49},{2,10},{... | collective-permute-start | bytes 2457608 | tf_op jit(solution)/shard_map/ppermute | solution.py:32
  103.5 4.1 %collective-permute-done.21 = bf16[2,4,64,384]{3,2,1,0:T(8,128)(2,1)S(1)} collective-permute-done((bf16[2,4,64,384]{3,2,1,0:T(8,128)(2,1)}, bf16[2,4,64,384]{3,2,1,0:T(8,128)(2,1)S(1)}, u32[]{:S(2)}, u32[]{:S(2)}) %collective-permute-start.21) | collective-permute-done | bytes 393248 | tf_op jit(solution)/shard_map/ppermute | solution.py:37
  109.4 5.4 %fusion.32 = f32[256,3072]{0,1:T(8,128)S(1)} fusion(bf16[256,1536]{1,0:T(8,128)(2,1)S(1)} %bitcast.199, bf16[3072,1536]{1,0:T(8,128)(2,1)} %param.5), kind=kOutput, calls=%fused_computation.138 | convolution fusion | flops 2415919104 | bytes 13369344 | tf_op jit(solution)/shard_map/dot_general | solution.py:101
  114.8 2.3 %select_select_fusion.3 = (bf16[2,4,64,384]{3,2,1,0:T(8,128)(2,1)}, bf16[2,4,64,384]{3,2,1,0:T(8,128)(2,1)S(1)}, bf16[2,4,64,384]{3,2,1,0:T(8,128)(2,1)S(1)}, bf16[2,4,64,384]{3,2,1,0:T(8,128)(2,1)}) fusion(bf16[2,4,64,384]{3,2,1,0:T(8,128)(2,1)S(1)} %copy-done.4, bf16[2,4,64,384]{3,2,1,0:T(8,128)(2,1)S(1)} %copy-done.10, ...), kind=kLoop, calls=%fused_computation.73 | loop fusion | flops 2949120 | bytes 4718595 | tf_op jit(solution)/shard_map/select_n | solution.py:136
  118.0 1.8 %collective-permute-start.26 = (bf16[4,4,2,64,1536]{4,3,2,1,0:T(8,128)(2,1)}, bf16[4,4,2,64,1536]{4,3,2,1,0:T(8,128)(2,1)S(1)}, u32[]{:S(2)}, u32[]{:S(2)}) collective-permute-start(bf16[4,4,2,64,1536]{4,3,2,1,0:T(8,128)(2,1)} %bitcast.189), channel_id=1, source_target_pairs={{0,1},{1,0},{2,3},{3,2},{4,5},{5,4},{6,7},{7,6},{8,9},{9,8},{10,11... | collective-permute-start | bytes 18874376 | tf_op jit(solution)/shard_map/ppermute | solution.py:27
  124.6 2.0 %multiply_convert_fusion = (f16[128,3072]{0,1:T(8,128)(2,1)S(1)}, f16[128,3072]{0,1:T(8,128)(2,1)S(1)}) fusion(f32[256,3072]{0,1:T(8,128)S(1)} %fusion.32, f32[128]{0:T(128)S(1)} %get-tuple-element.107, f32[128]{0:T(128)S(1)} %get-tuple-element.115, f16[128,3200]{0,1:T(8,128)(2,1)} %collective-permute-done.16, f32[128]{0:T(128)S(1)} %get-tuple-element.109, ...), kind=kLoop, calls=%fused_computation.35 | loop fusion | flops 3932160 | bytes 6293504 | tf_op jit(solution)/shard_map/convert_element_type | solution.py:51
  126.9 4.2 %collective-permute-start.24 = (f16[128,3200]{0,1:T(8,128)(2,1)S(1)}, f16[128,3200]{0,1:T(8,128)(2,1)S(1)}, u32[]{:S(2)}, u32[]{:S(2)}) collective-permute-start(f16[128,3200]{0,1:T(8,128)(2,1)S(1)} %pad_maximum_fusion.4), channel_id=1, source_target_pairs={{0,56},{8,0},{16,8},{24,16},{32,24},{40,32},{48,40},{56,48},{1,57}... | collective-permute-start | bytes 2457608 | tf_op jit(solution)/shard_map/ppermute | solution.py:32
  135.4 2.6 %fusion.33 = f32[384,1536]{1,0:T(8,128)S(1)} fusion(bf16[2048,384]{1,0:T(8,128)(2,1)S(1)} %bitcast.193, bf16[2048,1536]{1,0:T(8,128)(2,1)S(1)} %bitcast.192), kind=kOutput, calls=%fused_computation.139 | convolution fusion | flops 2415919104 | bytes 10223616 | tf_op jit(solution)/shard_map/dot_general | solution.py:158
  138.1 4.0 %broadcast_multiply_fusion = f32[384,1536]{1,0:T(8,128)} fusion(f32[384,1536]{1,0:T(8,128)S(1)} %fusion.33, bf16[4,4,2,64,1536]{4,3,2,1,0:T(8,128)(2,1)S(1)} %collective-permute-done.26, bf16[4,4,2,64,384]{4,3,1,2,0:T(8,128)(2,1)S(1)} %pad_maximum_fusion.1), kind=kOutput, calls=%fused_computation.45 | convolution fusion | flops 2417098752 | bytes 12582912 | tf_op jit(solution)/shard_map/dot_general | solution.py:158
  142.1 6.6 %collective-permute-done.24 = f16[128,3200]{0,1:T(8,128)(2,1)S(1)} collective-permute-done((f16[128,3200]{0,1:T(8,128)(2,1)S(1)}, f16[128,3200]{0,1:T(8,128)(2,1)S(1)}, u32[]{:S(2)}, u32[]{:S(2)}) %collective-permute-start.24) | collective-permute-done | bytes 819232 | tf_op jit(solution)/shard_map/ppermute | solution.py:32
  148.7 4.4 %collective-permute-done.23 = f16[128,3200]{0,1:T(8,128)(2,1)S(1)} collective-permute-done((f16[128,3200]{0,1:T(8,128)(2,1)S(1)}, f16[128,3200]{0,1:T(8,128)(2,1)S(1)}, u32[]{:S(2)}, u32[]{:S(2)}) %collective-permute-start.23) | collective-permute-done | bytes 819232 | tf_op jit(solution)/shard_map/ppermute | solution.py:32
  (164 shorter events, 39.9 us)
Async XLA Ops:
  7.2 110.9 %all-gather.3.cloned.1.call-start = ((), (), s32[]{:S(2)}) async-start(), calls=%async_computation | async-start | bytes 6684672 | tf_op jit(solution)/shard_map/all_gather | solution.py:86
  7.2 16.9 %collective-permute-start.10 = (bf16[64,1536]{1,0:T(8,128)(2,1)}, bf16[64,1536]{1,0:T(8,128)(2,1)S(1)}, u32[]{:S(2)}, u32[]{:S(2)}) collective-permute-start(bf16[64,1536]{1,0:T(8,128)(2,1)} %param.4), channel_id=1, source_target_pairs={{0,32},{32,0},{1,33},{33,1},{2,34},{34,2},{3,35},{35,3},{4,36},{36... | collective-permute-start | bytes 589832 | tf_op jit(solution)/shard_map/ppermute | solution.py:27
  19.6 7.0 %collective-permute-start.1 = (bf16[2,2,64,384]{3,2,1,0:T(8,128)(2,1)S(1)}, bf16[2,2,64,384]{3,2,1,0:T(8,128)(2,1)S(1)}, u32[]{:S(2)}, u32[]{:S(2)}) collective-permute-start(bf16[2,2,64,384]{3,2,1,0:T(8,128)(2,1)S(1)} %get-tuple-element.82), channel_id=1, source_target_pairs={{0,128},{64,192},{128,0},{192,64},{1,129},{65,193},{129,1},{193,65... | collective-permute-start | bytes 589832 | tf_op jit(solution)/shard_map/ppermute | solution.py:27
  22.6 8.9 %collective-permute-start.2 = (bf16[2,2,64,384]{3,2,1,0:T(8,128)(2,1)S(1)}, bf16[2,2,64,384]{3,2,1,0:T(8,128)(2,1)S(1)}, u32[]{:S(2)}, u32[]{:S(2)}) collective-permute-start(bf16[2,2,64,384]{3,2,1,0:T(8,128)(2,1)S(1)} %get-tuple-element.83), channel_id=1, source_target_pairs={{0,192},{64,0},{128,64},{192,128},{1,193},{65,1},{129,65},{193,129... | collective-permute-start | bytes 589832 | tf_op jit(solution)/shard_map/ppermute | solution.py:27
  23.4 8.2 %collective-permute-start = (bf16[2,2,64,384]{3,2,1,0:T(8,128)(2,1)S(1)}, bf16[2,2,64,384]{3,2,1,0:T(8,128)(2,1)S(1)}, u32[]{:S(2)}, u32[]{:S(2)}) collective-permute-start(bf16[2,2,64,384]{3,2,1,0:T(8,128)(2,1)S(1)} %get-tuple-element.84), channel_id=1, source_target_pairs={{0,64},{64,128},{128,192},{192,0},{1,65},{65,129},{129,193},{193,1... | collective-permute-start | bytes 589832 | tf_op jit(solution)/shard_map/ppermute | solution.py:27
  34.7 11.4 %collective-permute-start.7 = (bf16[2,4,64,384]{3,2,1,0:T(8,128)(2,1)S(1)}, bf16[2,4,64,384]{3,2,1,0:T(8,128)(2,1)S(1)}, u32[]{:S(2)}, u32[]{:S(2)}) collective-permute-start(bf16[2,4,64,384]{3,2,1,0:T(8,128)(2,1)S(1)} %get-tuple-element.80), channel_id=1, source_target_pairs={{0,56},{8,0},{16,8},{24,16},{32,24},{40,32},{48,40},{56,48},{1,57}... | collective-permute-start | bytes 1179656 | tf_op jit(solution)/shard_map/ppermute | solution.py:32
  34.8 11.7 %collective-permute-start.6 = (bf16[2,4,64,384]{3,2,1,0:T(8,128)(2,1)S(1)}, bf16[2,4,64,384]{3,2,1,0:T(8,128)(2,1)S(1)}, u32[]{:S(2)}, u32[]{:S(2)}) collective-permute-start(bf16[2,4,64,384]{3,2,1,0:T(8,128)(2,1)S(1)} %get-tuple-element.81), channel_id=1, source_target_pairs={{0,8},{8,16},{16,24},{24,32},{32,40},{40,48},{48,56},{56,0},{1,9},... | collective-permute-start | bytes 1179656 | tf_op jit(solution)/shard_map/ppermute | solution.py:32
  36.2 22.2 %collective-permute-start.8 = (bf16[2,4,64,384]{3,2,1,0:T(8,128)(2,1)S(1)}, bf16[2,4,64,384]{3,2,1,0:T(8,128)(2,1)S(1)}, u32[]{:S(2)}, u32[]{:S(2)}) collective-permute-start(bf16[2,4,64,384]{3,2,1,0:T(8,128)(2,1)S(1)} %pad_maximum_fusion.9), channel_id=1, source_target_pairs={{0,48},{8,56},{16,32},{24,40},{32,16},{40,24},{48,0},{56,8},{1,49}... | collective-permute-start | bytes 1179656 | tf_op jit(solution)/shard_map/ppermute | solution.py:37
  37.1 8.9 %collective-permute-start.3 = (bf16[64,1536]{1,0:T(8,128)(2,1)S(1)}, bf16[64,1536]{1,0:T(8,128)(2,1)S(1)}, u32[]{:S(2)}, u32[]{:S(2)}) collective-permute-start(bf16[64,1536]{1,0:T(8,128)(2,1)S(1)} %copy-done.31), channel_id=1, source_target_pairs={{0,2},{2,4},{4,6},{6,0},{1,3},{3,5},{5,7},{7,1},{8,10},{10,12},{12... | collective-permute-start | bytes 589832 | tf_op jit(solution)/shard_map/ppermute | solution.py:27
  59.4 12.6 %collective-permute-start.9 = (bf16[4,64,1536]{2,1,0:T(8,128)(2,1)}, bf16[4,64,1536]{2,1,0:T(8,128)(2,1)S(1)}, u32[]{:S(2)}, u32[]{:S(2)}) collective-permute-start(bf16[4,64,1536]{2,1,0:T(8,128)(2,1)} %get-tuple-element.78), channel_id=1, source_target_pairs={{0,1},{1,0},{2,3},{3,2},{4,5},{5,4},{6,7},{7,6},{8,9},{9,8},{10,11... | collective-permute-start | bytes 2359304 | tf_op jit(solution)/shard_map/ppermute | solution.py:27
  62.1 21.1 %collective-permute-start.18 = (bf16[2,4,64,384]{3,2,1,0:T(8,128)(2,1)S(1)}, bf16[2,4,64,384]{3,2,1,0:T(8,128)(2,1)S(1)}, u32[]{:S(2)}, u32[]{:S(2)}) collective-permute-start(bf16[2,4,64,384]{3,2,1,0:T(8,128)(2,1)S(1)} %get-tuple-element.105), channel_id=1, source_target_pairs={{24,16},{16,8},{8,0},{56,48},{48,40},{40,32},{25,17},{17,9},{9,1},... | collective-permute-start | bytes 1179656 | tf_op jit(solution)/shard_map/ppermute | solution.py:32
  63.4 19.8 %collective-permute-start.17 = (bf16[2,4,64,384]{3,2,1,0:T(8,128)(2,1)S(1)}, bf16[2,4,64,384]{3,2,1,0:T(8,128)(2,1)S(1)}, u32[]{:S(2)}, u32[]{:S(2)}) collective-permute-start(bf16[2,4,64,384]{3,2,1,0:T(8,128)(2,1)S(1)} %get-tuple-element.106), channel_id=1, source_target_pairs={{0,8},{8,16},{16,24},{32,40},{40,48},{48,56},{1,9},{9,17},{17,25},... | collective-permute-start | bytes 1179656 | tf_op jit(solution)/shard_map/ppermute | solution.py:32
  70.6 11.2 %collective-permute-start.19 = (bf16[2,4,64,384]{3,2,1,0:T(8,128)(2,1)S(1)}, bf16[2,4,64,384]{3,2,1,0:T(8,128)(2,1)}, u32[]{:S(2)}, u32[]{:S(2)}) collective-permute-start(bf16[2,4,64,384]{3,2,1,0:T(8,128)(2,1)S(1)} %collective-permute-done.8), channel_id=1, source_target_pairs={{8,16},{16,8},{40,48},{48,40},{9,17},{17,9},{41,49},{49,41},{10,18... | collective-permute-start | bytes 1179656 | tf_op jit(solution)/shard_map/ppermute | solution.py:37
  81.8 14.1 %collective-permute-start.11 = (bf16[64,1536]{1,0:T(8,128)(2,1)S(1)}, bf16[64,1536]{1,0:T(8,128)(2,1)S(1)}, u32[]{:S(2)}, u32[]{:S(2)}) collective-permute-start(bf16[64,1536]{1,0:T(8,128)(2,1)S(1)} %collective-permute-done.10), channel_id=1, source_target_pairs={{6,0},{24,26},{7,1},{25,27},{38,32},{56,58},{39,33},{57,59},{70,64... | collective-permute-start | bytes 589832 | tf_op jit(solution)/shard_map/ppermute | solution.py:111
  83.2 16.2 %collective-permute-start.22 = (bf16[2,4,64,384]{3,2,1,0:T(8,128)(2,1)}, bf16[2,4,64,384]{3,2,1,0:T(8,128)(2,1)}, u32[]{:S(2)}, u32[]{:S(2)}) collective-permute-start(bf16[2,4,64,384]{3,2,1,0:T(8,128)(2,1)} %collective-permute-done.19), channel_id=1, source_target_pairs={{8,0},{16,24},{40,32},{48,56},{9,1},{17,25},{41,33},{49,57},{10,2}... | collective-permute-start | bytes 1179656 | tf_op jit(solution)/shard_map/ppermute | solution.py:37
  85.3 22.3 %collective-permute-start.21 = (bf16[2,4,64,384]{3,2,1,0:T(8,128)(2,1)}, bf16[2,4,64,384]{3,2,1,0:T(8,128)(2,1)S(1)}, u32[]{:S(2)}, u32[]{:S(2)}) collective-permute-start(bf16[2,4,64,384]{3,2,1,0:T(8,128)(2,1)} %get-tuple-element.76), channel_id=1, source_target_pairs={{8,0},{16,24},{40,32},{48,56},{9,1},{17,25},{41,33},{49,57},{10,2}... | collective-permute-start | bytes 1179656 | tf_op jit(solution)/shard_map/ppermute | solution.py:37
  86.6 21.0 %collective-permute-start.20 = (bf16[2,4,64,384]{3,2,1,0:T(8,128)(2,1)S(1)}, bf16[2,4,64,384]{3,2,1,0:T(8,128)(2,1)}, u32[]{:S(2)}, u32[]{:S(2)}) collective-permute-start(bf16[2,4,64,384]{3,2,1,0:T(8,128)(2,1)S(1)} %get-tuple-element.77), channel_id=1, source_target_pairs={{8,16},{16,8},{40,48},{48,40},{9,17},{17,9},{41,49},{49,41},{10,18... | collective-permute-start | bytes 1179656 | tf_op jit(solution)/shard_map/ppermute | solution.py:37
  95.9 13.0 %collective-permute-start.14 = (bf16[64,1536]{1,0:T(8,128)(2,1)S(1)}, bf16[64,1536]{1,0:T(8,128)(2,1)S(1)}, u32[]{:S(2)}, u32[]{:S(2)}) collective-permute-start(bf16[64,1536]{1,0:T(8,128)(2,1)S(1)} %add_add_fusion), channel_id=1, source_target_pairs={{0,1},{1,0},{2,3},{3,2},{4,5},{5,4},{6,7},{7,6},{8,9},{9,8},{10,11... | collective-permute-start | bytes 589832 | tf_op jit(solution)/shard_map/ppermute | solution.py:27
  97.0 25.1 %collective-permute-start.16 = (f16[128,3200]{0,1:T(8,128)(2,1)}, f16[128,3200]{0,1:T(8,128)(2,1)}, u32[]{:S(2)}, u32[]{:S(2)}) collective-permute-start(f16[128,3200]{0,1:T(8,128)(2,1)} %pad_maximum_fusion.2), channel_id=1, source_target_pairs={{16,8},{24,16},{48,40},{56,48},{17,9},{25,17},{49,41},{57,49},{18,... | collective-permute-start | bytes 2457608 | tf_op jit(solution)/shard_map/ppermute | solution.py:32
  99.3 22.8 %collective-permute-start.15 = (f16[128,3200]{0,1:T(8,128)(2,1)}, f16[128,3200]{0,1:T(8,128)(2,1)}, u32[]{:S(2)}, u32[]{:S(2)}) collective-permute-start(f16[128,3200]{0,1:T(8,128)(2,1)} %pad_maximum_fusion.2), channel_id=1, source_target_pairs={{0,8},{8,16},{32,40},{40,48},{1,9},{9,17},{33,41},{41,49},{2,10},{... | collective-permute-start | bytes 2457608 | tf_op jit(solution)/shard_map/ppermute | solution.py:32
  107.7 24.0 %collective-permute-start.25 = (bf16[2,4,64,384]{3,2,1,0:T(8,128)(2,1)}, bf16[2,4,64,384]{3,2,1,0:T(8,128)(2,1)}, u32[]{:S(2)}, u32[]{:S(2)}) collective-permute-start(bf16[2,4,64,384]{3,2,1,0:T(8,128)(2,1)} %collective-permute-done.20), channel_id=1, source_target_pairs={{8,0},{16,24},{40,32},{48,56},{9,1},{17,25},{41,33},{49,57},{10,2}... | collective-permute-start | bytes 1179656 | tf_op jit(solution)/shard_map/ppermute | solution.py:37
  118.0 20.0 %collective-permute-start.26 = (bf16[4,4,2,64,1536]{4,3,2,1,0:T(8,128)(2,1)}, bf16[4,4,2,64,1536]{4,3,2,1,0:T(8,128)(2,1)S(1)}, u32[]{:S(2)}, u32[]{:S(2)}) collective-permute-start(bf16[4,4,2,64,1536]{4,3,2,1,0:T(8,128)(2,1)} %bitcast.189), channel_id=1, source_target_pairs={{0,1},{1,0},{2,3},{3,2},{4,5},{5,4},{6,7},{7,6},{8,9},{9,8},{10,11... | collective-permute-start | bytes 18874376 | tf_op jit(solution)/shard_map/ppermute | solution.py:27
  126.9 21.8 %collective-permute-start.24 = (f16[128,3200]{0,1:T(8,128)(2,1)S(1)}, f16[128,3200]{0,1:T(8,128)(2,1)S(1)}, u32[]{:S(2)}, u32[]{:S(2)}) collective-permute-start(f16[128,3200]{0,1:T(8,128)(2,1)S(1)} %pad_maximum_fusion.4), channel_id=1, source_target_pairs={{0,56},{8,0},{16,8},{24,16},{32,24},{40,32},{48,40},{56,48},{1,57}... | collective-permute-start | bytes 2457608 | tf_op jit(solution)/shard_map/ppermute | solution.py:32
  131.4 21.7 %collective-permute-start.23 = (f16[128,3200]{0,1:T(8,128)(2,1)S(1)}, f16[128,3200]{0,1:T(8,128)(2,1)S(1)}, u32[]{:S(2)}, u32[]{:S(2)}) collective-permute-start(f16[128,3200]{0,1:T(8,128)(2,1)S(1)} %pad_maximum_fusion.3), channel_id=1, source_target_pairs={{0,8},{8,16},{16,24},{24,32},{32,40},{40,48},{48,56},{56,0},{1,9},... | collective-permute-start | bytes 2457608 | tf_op jit(solution)/shard_map/ppermute | solution.py:32
  (38 other events, 255.4 us)
Sparse Core Ops, SparseCore 0:
  32.1 70.1 all-gather.2

commit v8 on v7

--- a/solution.py
+++ b/solution.py
@@ -122,7 +122,7 @@
     e = pairs_z(jnp.where(zl == 1, c_up, c_down), {1: 1, 2: -1})
     f = pairs_z(jnp.where(zl == 2, c_up, c_down), {1: -1, 2: 1})
     g = pairs_z(d, {1: -1, 2: 1})
-    e, f, g = lax.optimization_barrier((e, f, g))
+    e, f, g, part_up, part_down = lax.optimization_barrier((e, f, g, part_up, part_down))
     h = pairs_z(e, {1: -1, 2: 1})
     far_up, far_down = lax.optimization_barrier((far_up, far_down, g))[:2]
     near_up = pack(part_up + unpack(far_up))
@@ -130,6 +130,7 @@
     from_below = along_z(near_up, 1, range(4))
     from_above = along_z(near_down, -1, range(4))
     h = after(h, near_up, near_down)
+    own = after(own, near_up, near_down)
     other_rows = shift(after(all_rows, e, f, g), "core", 1)
 
     def choose(*units):

time: 162 us -> 164 us (1.012)
  starting transfers between devices: 51.5 us -> 59.3 us
  waiting for transfers between devices: 51.2 us -> 44.6 us
  local copies, waits for them, and re-layouts: 6.93 us -> 8.71 us
    ppermute x8, starting transfers between devices: 20.4 us -> 27.2 us  [along_z(): return lax.ppermute(v, Z, pairs)]
    ppermute x3, waiting for transfers between devices: 7.85 us -> 2.42 us  [on_device(): lax.ppermute(p, ('zl', 'x'), [(3, (3 + t) % 4), (12, 12 + t)])]
    ppermute x8, waiting for transfers between devices: 11.5 us -> 8.75 us  [along_z(): return lax.ppermute(v, Z, pairs)]
    unnamed x70 -> x44, local copies, waits for them, and re-layouts: 5.28 us -> 7.69 us
    select_n x2 -> x1, other arithmetic: 3.87 us -> 1.76 us  [choose(): return lax.select_n(zl, *units)]
    another operation x9, other arithmetic: 2.8 us -> 0.76 us  [on_device(): jnp.stack([jnp.stack([i[core], k[core]], axis=1) for i, k in zip(in_group...]
  transfers between devices with their start and end apart: 28 -> 28, of which waited for: 12 -> 11; matrix products, arithmetic and copies ran while one was open for 24% -> 22% of each run, Pallas kernels for 0% -> 0%
where the time goes in v8:
time: 164 us
  starting transfers between devices  59.3 us (36%)
  waiting for transfers between devices  44.6 us (27%)
  other arithmetic  18.9 us (12%)
  matrix products  17.3 us (11%)
  between operations  14.8 us (9%)
  local copies, waits for them, and re-layouts  8.71 us (5%)
    ppermute x8, starting transfers between devices, along_z(): return lax.ppermute(v, Z, pairs)  27.2 us
    ppermute x10, starting transfers between devices, shift(): return lax.ppermute(v, axis, [(i, (i + step) % n) for i in range(n)])  22.1 us
    ppermute x6, waiting for transfers between devices, pairs_z(): return lax.ppermute(v, Z, pairs)  18.3 us
    ppermute x10, waiting for transfers between devices, shift(): return lax.ppermute(v, axis, [(i, (i + step) % n) for i in range(n)])  15.1 us
    dot_general x2, matrix products, partial(): lax.dot_general(rows, down_weight, (((1,), (1,)), ((), ())), preferred_el...  10.6 us
    ppermute x8, waiting for transfers between devices, along_z(): return lax.ppermute(v, Z, pairs)  8.75 us
    unnamed x44, local copies, waits for them, and re-layouts  7.69 us
    ppermute x6, starting transfers between devices, pairs_z(): return lax.ppermute(v, Z, pairs)  6.75 us
  transfers between devices with their start and end apart: 28, of which 11 were waited for; matrix products, arithmetic and copies ran while one was open for 22% of the time, Pallas kernels for 0%

profile of v8, /device:TPU:1, one launch (start us, length us, event | category | flops | bytes accessed | tf_op | source)
XLA Modules:
  0.0 163.7 jit_solution(17741366827538759181)
XLA Ops:
  7.2 7.8 %collective-permute-start.16 = (bf16[64,1536]{1,0:T(8,128)(2,1)}, bf16[64,1536]{1,0:T(8,128)(2,1)S(1)}, u32[]{:S(2)}, u32[]{:S(2)}) collective-permute-start(bf16[64,1536]{1,0:T(8,128)(2,1)} %param.4), channel_id=1, source_target_pairs={{0,32},{32,0},{1,33},{33,1},{2,34},{34,2},{3,35},{35,3},{4,36},{36... | collective-permute-start | bytes 589832 | tf_op jit(solution)/shard_map/ppermute | solution.py:27
  16.5 2.2 %fusion.6 = (f32[128,3072]{0,1:T(8,128)}, bf16[128,3072]{0,1:T(8,128)(2,1)S(1)}) fusion(bf16[128,3072]{0,1:T(8,128)(2,1)S(1)} %copy.52), kind=kLoop, calls=%fused_computation.22 | loop fusion | flops 7864320 | bytes 3145728 | tf_op jit(solution)/shard_map/add | solution.py:19
  19.6 3.0 %collective-permute-start.1 = (bf16[2,2,64,384]{3,2,1,0:T(8,128)(2,1)S(1)}, bf16[2,2,64,384]{3,2,1,0:T(8,128)(2,1)S(1)}, u32[]{:S(2)}, u32[]{:S(2)}) collective-permute-start(bf16[2,2,64,384]{3,2,1,0:T(8,128)(2,1)S(1)} %get-tuple-element.90), channel_id=1, source_target_pairs={{0,128},{64,192},{128,0},{192,64},{1,129},{65,193},{129,1},{193,65... | collective-permute-start | bytes 589832 | tf_op jit(solution)/shard_map/ppermute | solution.py:27
  24.9 1.8 %collective-permute-done.1 = bf16[2,2,64,384]{3,2,1,0:T(8,128)(2,1)S(1)} collective-permute-done((bf16[2,2,64,384]{3,2,1,0:T(8,128)(2,1)S(1)}, bf16[2,2,64,384]{3,2,1,0:T(8,128)(2,1)S(1)}, u32[]{:S(2)}, u32[]{:S(2)}) %collective-permute-start.1) | collective-permute-done | bytes 196640 | tf_op jit(solution)/shard_map/ppermute | solution.py:27
  26.7 4.9 %collective-permute-done.2 = bf16[2,2,64,384]{3,2,1,0:T(8,128)(2,1)S(1)} collective-permute-done((bf16[2,2,64,384]{3,2,1,0:T(8,128)(2,1)S(1)}, bf16[2,2,64,384]{3,2,1,0:T(8,128)(2,1)S(1)}, u32[]{:S(2)}, u32[]{:S(2)}) %collective-permute-start.2) | collective-permute-done | bytes 196640 | tf_op jit(solution)/shard_map/ppermute | solution.py:27
  33.5 2.6 %collective-permute-start.5 = (bf16[64,1536]{1,0:T(8,128)(2,1)S(1)}, bf16[64,1536]{1,0:T(8,128)(2,1)S(1)}, u32[]{:S(2)}, u32[]{:S(2)}) collective-permute-start(bf16[64,1536]{1,0:T(8,128)(2,1)S(1)} %copy-done.13), channel_id=1, source_target_pairs={{0,6},{2,0},{4,2},{6,4},{1,7},{3,1},{5,3},{7,5},{8,14},{10,8},{12,... | collective-permute-start | bytes 589832 | tf_op jit(solution)/shard_map/ppermute | solution.py:27
  39.7 4.2 %collective-permute-done.4 = bf16[64,1536]{1,0:T(8,128)(2,1)S(1)} collective-permute-done((bf16[64,1536]{1,0:T(8,128)(2,1)S(1)}, bf16[64,1536]{1,0:T(8,128)(2,1)S(1)}, u32[]{:S(2)}, u32[]{:S(2)}) %collective-permute-start.4) | collective-permute-done | bytes 196640 | tf_op jit(solution)/shard_map/ppermute | solution.py:27
  43.8 3.7 %collective-permute-done.3 = bf16[64,1536]{1,0:T(8,128)(2,1)S(1)} collective-permute-done((bf16[64,1536]{1,0:T(8,128)(2,1)S(1)}, bf16[64,1536]{1,0:T(8,128)(2,1)S(1)}, u32[]{:S(2)}, u32[]{:S(2)}) %collective-permute-start.3) | collective-permute-done | bytes 196640 | tf_op jit(solution)/shard_map/ppermute | solution.py:27
  48.0 11.9 %collective-permute-done.8 = bf16[2,4,64,384]{3,2,1,0:T(8,128)(2,1)S(1)} collective-permute-done((bf16[2,4,64,384]{3,2,1,0:T(8,128)(2,1)S(1)}, bf16[2,4,64,384]{3,2,1,0:T(8,128)(2,1)S(1)}, u32[]{:S(2)}, u32[]{:S(2)}) %collective-permute-start.8) | collective-permute-done | bytes 393248 | tf_op jit(solution)/shard_map/ppermute | solution.py:37
  60.9 2.5 %collective-permute-start.9 = (bf16[4,64,1536]{2,1,0:T(8,128)(2,1)}, bf16[4,64,1536]{2,1,0:T(8,128)(2,1)S(1)}, u32[]{:S(2)}, u32[]{:S(2)}) collective-permute-start(bf16[4,64,1536]{2,1,0:T(8,128)(2,1)} %get-tuple-element.86), channel_id=1, source_target_pairs={{0,1},{1,0},{2,3},{3,2},{4,5},{5,4},{6,7},{7,6},{8,9},{9,8},{10,11... | collective-permute-start | bytes 2359304 | tf_op jit(solution)/shard_map/ppermute | solution.py:27
  65.8 7.2 %collective-permute-start.10 = (bf16[2,4,64,384]{3,2,1,0:T(8,128)(2,1)}, bf16[2,4,64,384]{3,2,1,0:T(8,128)(2,1)S(1)}, u32[]{:S(2)}, u32[]{:S(2)}) collective-permute-start(bf16[2,4,64,384]{3,2,1,0:T(8,128)(2,1)} %get-tuple-element.112), channel_id=1, source_target_pairs={{0,8},{8,16},{16,24},{32,40},{40,48},{48,56},{1,9},{9,17},{17,25},... | collective-permute-start | bytes 1179656 | tf_op jit(solution)/shard_map/ppermute | solution.py:32
  74.7 5.4 %fusion.32 = f32[256,3072]{0,1:T(8,128)S(1)} fusion(bf16[256,1536]{1,0:T(8,128)(2,1)S(1)} %bitcast.200, bf16[3072,1536]{1,0:T(8,128)(2,1)} %param.5), kind=kOutput, calls=%fused_computation.138 | convolution fusion | flops 2415919104 | bytes 13369344 | tf_op jit(solution)/shard_map/dot_general | solution.py:101
  86.4 1.6 collective-permute-start.22
  88.0 7.4 %collective-permute-start.21 = (f16[128,3200]{0,1:T(8,128)(2,1)}, f16[128,3200]{0,1:T(8,128)(2,1)S(1)}, u32[]{:S(2)}, u32[]{:S(2)}) collective-permute-start(f16[128,3200]{0,1:T(8,128)(2,1)} %pad_maximum_fusion.2), channel_id=1, source_target_pairs={{0,8},{8,16},{32,40},{40,48},{1,9},{9,17},{33,41},{41,49},{2,10},{... | collective-permute-start | bytes 2457608 | tf_op jit(solution)/shard_map/ppermute | solution.py:32
  96.6 2.4 %collective-permute-done.17 = bf16[64,1536]{1,0:T(8,128)(2,1)S(1)} collective-permute-done((bf16[64,1536]{1,0:T(8,128)(2,1)S(1)}, bf16[64,1536]{1,0:T(8,128)(2,1)S(1)}, u32[]{:S(2)}, u32[]{:S(2)}) %collective-permute-start.17) | collective-permute-done | bytes 196640 | tf_op jit(solution)/shard_map/ppermute | solution.py:111
  104.3 5.2 %fusion.33 = f32[256,3072]{0,1:T(8,128)S(1)} fusion(bf16[256,1536]{1,0:T(8,128)(2,1)S(1)} %bitcast.199, bf16[3072,1536]{1,0:T(8,128)(2,1)} %param.5), kind=kOutput, calls=%fused_computation.139 | convolution fusion | flops 2415919104 | bytes 13369344 | tf_op jit(solution)/shard_map/dot_general | solution.py:101
  109.7 6.4 %collective-permute-done.14 = bf16[2,4,64,384]{3,2,1,0:T(8,128)(2,1)S(1)} collective-permute-done((bf16[2,4,64,384]{3,2,1,0:T(8,128)(2,1)S(1)}, bf16[2,4,64,384]{3,2,1,0:T(8,128)(2,1)S(1)}, u32[]{:S(2)}, u32[]{:S(2)}) %collective-permute-start.14) | collective-permute-done | bytes 393248 | tf_op jit(solution)/shard_map/ppermute | solution.py:37
  118.6 2.1 %collective-permute-start.26 = (bf16[4,4,2,64,1536]{4,3,2,1,0:T(8,128)(2,1)}, bf16[4,4,2,64,1536]{4,3,2,1,0:T(8,128)(2,1)S(1)}, u32[]{:S(2)}, u32[]{:S(2)}) collective-permute-start(bf16[4,4,2,64,1536]{4,3,2,1,0:T(8,128)(2,1)} %bitcast.189), channel_id=1, source_target_pairs={{0,1},{1,0},{2,3},{3,2},{4,5},{5,4},{6,7},{7,6},{8,9},{9,8},{10,11... | collective-permute-start | bytes 18874376 | tf_op jit(solution)/shard_map/ppermute | solution.py:27
  122.4 7.9 %collective-permute-start.23 = (f16[128,3200]{0,1:T(8,128)(2,1)S(1)}, f16[128,3200]{0,1:T(8,128)(2,1)S(1)}, u32[]{:S(2)}, u32[]{:S(2)}) collective-permute-start(f16[128,3200]{0,1:T(8,128)(2,1)S(1)} %pad_maximum_fusion.3), channel_id=1, source_target_pairs={{0,8},{8,16},{16,24},{24,32},{32,40},{40,48},{48,56},{56,0},{1,9},... | collective-permute-start | bytes 2457608 | tf_op jit(solution)/shard_map/ppermute | solution.py:32
  132.4 1.5 multiply_convert_fusion
  135.3 1.8 %select_select_fusion.4 = (bf16[2,4,64,384]{3,2,1,0:T(8,128)(2,1)S(1)}, bf16[2,4,64,384]{3,2,1,0:T(8,128)(2,1)S(1)}, bf16[2,4,64,384]{3,2,1,0:T(8,128)(2,1)S(1)}...) fusion(bf16[2,4,64,384]{3,2,1,0:T(8,128)(2,1)S(1)} %copy-done.1, ...), kind=kLoop, calls=%fused_computation.74 | loop fusion | flops 4718592 | bytes 7471107 | tf_op jit(solution)/shard_map/select_n | solution.py:137
  140.2 2.6 %fusion.34 = f32[384,1536]{1,0:T(8,128)S(1)} fusion(bf16[2048,384]{1,0:T(8,128)(2,1)S(1)} %bitcast.193, bf16[2048,1536]{1,0:T(8,128)(2,1)S(1)} %bitcast.192), kind=kOutput, calls=%fused_computation.140 | convolution fusion | flops 2415919104 | bytes 10223616 | tf_op jit(solution)/shard_map/dot_general | solution.py:159
  142.9 4.0 %broadcast_multiply_fusion = f32[384,1536]{1,0:T(8,128)} fusion(f32[384,1536]{1,0:T(8,128)S(1)} %fusion.34, bf16[4,4,2,64,1536]{4,3,2,1,0:T(8,128)(2,1)S(1)} %collective-permute-done.26, bf16[4,4,2,64,384]{4,3,1,2,0:T(8,128)(2,1)S(1)} %pad_maximum_fusion.1), kind=kOutput, calls=%fused_computation.45 | convolution fusion | flops 2417098752 | bytes 12582912 | tf_op jit(solution)/shard_map/dot_general | solution.py:159
  148.0 7.2 %collective-permute-done.24 = f16[128,3200]{0,1:T(8,128)(2,1)S(1)} collective-permute-done((f16[128,3200]{0,1:T(8,128)(2,1)S(1)}, f16[128,3200]{0,1:T(8,128)(2,1)S(1)}, u32[]{:S(2)}, u32[]{:S(2)}) %collective-permute-start.24) | collective-permute-done | bytes 819232 | tf_op jit(solution)/shard_map/ppermute | solution.py:32
  (140 shorter events, 41.4 us)
Async XLA Ops:
  7.2 111.5 %all-gather.3.cloned.1.call-start = ((), (), s32[]{:S(2)}) async-start(), calls=%async_computation | async-start | bytes 6684672 | tf_op jit(solution)/shard_map/all_gather | solution.py:86
  7.2 16.9 %collective-permute-start.16 = (bf16[64,1536]{1,0:T(8,128)(2,1)}, bf16[64,1536]{1,0:T(8,128)(2,1)S(1)}, u32[]{:S(2)}, u32[]{:S(2)}) collective-permute-start(bf16[64,1536]{1,0:T(8,128)(2,1)} %param.4), channel_id=1, source_target_pairs={{0,32},{32,0},{1,33},{33,1},{2,34},{34,2},{3,35},{35,3},{4,36},{36... | collective-permute-start | bytes 589832 | tf_op jit(solution)/shard_map/ppermute | solution.py:27
  22.6 8.9 %collective-permute-start.2 = (bf16[2,2,64,384]{3,2,1,0:T(8,128)(2,1)S(1)}, bf16[2,2,64,384]{3,2,1,0:T(8,128)(2,1)S(1)}, u32[]{:S(2)}, u32[]{:S(2)}) collective-permute-start(bf16[2,2,64,384]{3,2,1,0:T(8,128)(2,1)S(1)} %get-tuple-element.91), channel_id=1, source_target_pairs={{0,192},{64,0},{128,64},{192,128},{1,193},{65,1},{129,65},{193,129... | collective-permute-start | bytes 589832 | tf_op jit(solution)/shard_map/ppermute | solution.py:27
  23.4 8.2 %collective-permute-start = (bf16[2,2,64,384]{3,2,1,0:T(8,128)(2,1)S(1)}, bf16[2,2,64,384]{3,2,1,0:T(8,128)(2,1)S(1)}, u32[]{:S(2)}, u32[]{:S(2)}) collective-permute-start(bf16[2,2,64,384]{3,2,1,0:T(8,128)(2,1)S(1)} %get-tuple-element.92), channel_id=1, source_target_pairs={{0,64},{64,128},{128,192},{192,0},{1,65},{65,129},{129,193},{193,1... | collective-permute-start | bytes 589832 | tf_op jit(solution)/shard_map/ppermute | solution.py:27
  36.2 11.4 %collective-permute-start.7 = (bf16[2,4,64,384]{3,2,1,0:T(8,128)(2,1)S(1)}, bf16[2,4,64,384]{3,2,1,0:T(8,128)(2,1)S(1)}, u32[]{:S(2)}, u32[]{:S(2)}) collective-permute-start(bf16[2,4,64,384]{3,2,1,0:T(8,128)(2,1)S(1)} %get-tuple-element.88), channel_id=1, source_target_pairs={{0,56},{8,0},{16,8},{24,16},{32,24},{40,32},{48,40},{56,48},{1,57}... | collective-permute-start | bytes 1179656 | tf_op jit(solution)/shard_map/ppermute | solution.py:32
  36.3 11.7 %collective-permute-start.6 = (bf16[2,4,64,384]{3,2,1,0:T(8,128)(2,1)S(1)}, bf16[2,4,64,384]{3,2,1,0:T(8,128)(2,1)S(1)}, u32[]{:S(2)}, u32[]{:S(2)}) collective-permute-start(bf16[2,4,64,384]{3,2,1,0:T(8,128)(2,1)S(1)} %get-tuple-element.89), channel_id=1, source_target_pairs={{0,8},{8,16},{16,24},{24,32},{32,40},{40,48},{48,56},{56,0},{1,9},... | collective-permute-start | bytes 1179656 | tf_op jit(solution)/shard_map/ppermute | solution.py:32
  37.7 22.2 %collective-permute-start.8 = (bf16[2,4,64,384]{3,2,1,0:T(8,128)(2,1)S(1)}, bf16[2,4,64,384]{3,2,1,0:T(8,128)(2,1)S(1)}, u32[]{:S(2)}, u32[]{:S(2)}) collective-permute-start(bf16[2,4,64,384]{3,2,1,0:T(8,128)(2,1)S(1)} %copy-done.18), channel_id=1, source_target_pairs={{0,48},{8,56},{16,32},{24,40},{32,16},{40,24},{48,0},{56,8},{1,49}... | collective-permute-start | bytes 1179656 | tf_op jit(solution)/shard_map/ppermute | solution.py:37
  38.7 8.9 %collective-permute-start.3 = (bf16[64,1536]{1,0:T(8,128)(2,1)S(1)}, bf16[64,1536]{1,0:T(8,128)(2,1)S(1)}, u32[]{:S(2)}, u32[]{:S(2)}) collective-permute-start(bf16[64,1536]{1,0:T(8,128)(2,1)S(1)} %copy-done.13), channel_id=1, source_target_pairs={{0,2},{2,4},{4,6},{6,0},{1,3},{3,5},{5,7},{7,1},{8,10},{10,12},{12... | collective-permute-start | bytes 589832 | tf_op jit(solution)/shard_map/ppermute | solution.py:27
  60.9 13.5 %collective-permute-start.9 = (bf16[4,64,1536]{2,1,0:T(8,128)(2,1)}, bf16[4,64,1536]{2,1,0:T(8,128)(2,1)S(1)}, u32[]{:S(2)}, u32[]{:S(2)}) collective-permute-start(bf16[4,64,1536]{2,1,0:T(8,128)(2,1)} %get-tuple-element.86), channel_id=1, source_target_pairs={{0,1},{1,0},{2,3},{3,2},{4,5},{5,4},{6,7},{7,6},{8,9},{9,8},{10,11... | collective-permute-start | bytes 2359304 | tf_op jit(solution)/shard_map/ppermute | solution.py:27
  64.5 21.9 %collective-permute-start.11 = (bf16[2,4,64,384]{3,2,1,0:T(8,128)(2,1)}, bf16[2,4,64,384]{3,2,1,0:T(8,128)(2,1)S(1)}, u32[]{:S(2)}, u32[]{:S(2)}) collective-permute-start(bf16[2,4,64,384]{3,2,1,0:T(8,128)(2,1)} %get-tuple-element.111), channel_id=1, source_target_pairs={{24,16},{16,8},{8,0},{56,48},{48,40},{40,32},{25,17},{17,9},{9,1},... | collective-permute-start | bytes 1179656 | tf_op jit(solution)/shard_map/ppermute | solution.py:32
  65.8 22.2 %collective-permute-start.10 = (bf16[2,4,64,384]{3,2,1,0:T(8,128)(2,1)}, bf16[2,4,64,384]{3,2,1,0:T(8,128)(2,1)S(1)}, u32[]{:S(2)}, u32[]{:S(2)}) collective-permute-start(bf16[2,4,64,384]{3,2,1,0:T(8,128)(2,1)} %get-tuple-element.112), channel_id=1, source_target_pairs={{0,8},{8,16},{16,24},{32,40},{40,48},{48,56},{1,9},{9,17},{17,25},... | collective-permute-start | bytes 1179656 | tf_op jit(solution)/shard_map/ppermute | solution.py:32
  73.0 12.0 %collective-permute-start.12 = (bf16[2,4,64,384]{3,2,1,0:T(8,128)(2,1)S(1)}, bf16[2,4,64,384]{3,2,1,0:T(8,128)(2,1)}, u32[]{:S(2)}, u32[]{:S(2)}) collective-permute-start(bf16[2,4,64,384]{3,2,1,0:T(8,128)(2,1)S(1)} %collective-permute-done.8), channel_id=1, source_target_pairs={{8,16},{16,8},{40,48},{48,40},{9,17},{17,9},{41,49},{49,41},{10,18... | collective-permute-start | bytes 1179656 | tf_op jit(solution)/shard_map/ppermute | solution.py:37
  83.0 12.4 %collective-permute-start.19 = (bf16[64,1536]{1,0:T(8,128)(2,1)S(1)}, bf16[64,1536]{1,0:T(8,128)(2,1)S(1)}, u32[]{:S(2)}, u32[]{:S(2)}) collective-permute-start(bf16[64,1536]{1,0:T(8,128)(2,1)S(1)} %collective-permute-done.16), channel_id=1, source_target_pairs={{6,4},{24,30},{7,5},{25,31},{38,36},{56,62},{39,37},{57,63},{70,68... | collective-permute-start | bytes 589832 | tf_op jit(solution)/shard_map/ppermute | solution.py:111
  83.6 13.0 %collective-permute-start.18 = (bf16[64,1536]{1,0:T(8,128)(2,1)S(1)}, bf16[64,1536]{1,0:T(8,128)(2,1)}, u32[]{:S(2)}, u32[]{:S(2)}) collective-permute-start(bf16[64,1536]{1,0:T(8,128)(2,1)S(1)} %collective-permute-done.16), channel_id=1, source_target_pairs={{6,2},{24,28},{7,3},{25,29},{38,34},{56,60},{39,35},{57,61},{70,66... | collective-permute-start | bytes 589832 | tf_op jit(solution)/shard_map/ppermute | solution.py:111
  85.0 14.1 %collective-permute-start.17 = (bf16[64,1536]{1,0:T(8,128)(2,1)S(1)}, bf16[64,1536]{1,0:T(8,128)(2,1)S(1)}, u32[]{:S(2)}, u32[]{:S(2)}) collective-permute-start(bf16[64,1536]{1,0:T(8,128)(2,1)S(1)} %collective-permute-done.16), channel_id=1, source_target_pairs={{6,0},{24,26},{7,1},{25,27},{38,32},{56,58},{39,33},{57,59},{70,64... | collective-permute-start | bytes 589832 | tf_op jit(solution)/shard_map/ppermute | solution.py:111
  86.4 31.1 %collective-permute-start.22 = (f16[128,3200]{0,1:T(8,128)(2,1)}, f16[128,3200]{0,1:T(8,128)(2,1)}, u32[]{:S(2)}, u32[]{:S(2)}) collective-permute-start(f16[128,3200]{0,1:T(8,128)(2,1)} %pad_maximum_fusion.2), channel_id=1, source_target_pairs={{16,8},{24,16},{48,40},{56,48},{17,9},{25,17},{49,41},{57,49},{18,... | collective-permute-start | bytes 2457608 | tf_op jit(solution)/shard_map/ppermute | solution.py:32
  88.0 29.5 %collective-permute-start.21 = (f16[128,3200]{0,1:T(8,128)(2,1)}, f16[128,3200]{0,1:T(8,128)(2,1)S(1)}, u32[]{:S(2)}, u32[]{:S(2)}) collective-permute-start(f16[128,3200]{0,1:T(8,128)(2,1)} %pad_maximum_fusion.2), channel_id=1, source_target_pairs={{0,8},{8,16},{32,40},{40,48},{1,9},{9,17},{33,41},{41,49},{2,10},{... | collective-permute-start | bytes 2457608 | tf_op jit(solution)/shard_map/ppermute | solution.py:32
  95.3 14.4 %collective-permute-start.15 = (bf16[2,4,64,384]{3,2,1,0:T(8,128)(2,1)}, bf16[2,4,64,384]{3,2,1,0:T(8,128)(2,1)S(1)}, u32[]{:S(2)}, u32[]{:S(2)}) collective-permute-start(bf16[2,4,64,384]{3,2,1,0:T(8,128)(2,1)} %collective-permute-done.12), channel_id=1, source_target_pairs={{8,0},{16,24},{40,32},{48,56},{9,1},{17,25},{41,33},{49,57},{10,2}... | collective-permute-start | bytes 1179656 | tf_op jit(solution)/shard_map/ppermute | solution.py:37
  101.2 15.0 %collective-permute-start.14 = (bf16[2,4,64,384]{3,2,1,0:T(8,128)(2,1)S(1)}, bf16[2,4,64,384]{3,2,1,0:T(8,128)(2,1)S(1)}, u32[]{:S(2)}, u32[]{:S(2)}) collective-permute-start(bf16[2,4,64,384]{3,2,1,0:T(8,128)(2,1)S(1)} %get-tuple-element.84), channel_id=1, source_target_pairs={{8,0},{16,24},{40,32},{48,56},{9,1},{17,25},{41,33},{49,57},{10,2}... | collective-permute-start | bytes 1179656 | tf_op jit(solution)/shard_map/ppermute | solution.py:37
  102.5 13.7 %collective-permute-start.13 = (bf16[2,4,64,384]{3,2,1,0:T(8,128)(2,1)S(1)}, bf16[2,4,64,384]{3,2,1,0:T(8,128)(2,1)}, u32[]{:S(2)}, u32[]{:S(2)}) collective-permute-start(bf16[2,4,64,384]{3,2,1,0:T(8,128)(2,1)S(1)} %get-tuple-element.85), channel_id=1, source_target_pairs={{8,16},{16,8},{40,48},{48,40},{9,17},{17,9},{41,49},{49,41},{10,18... | collective-permute-start | bytes 1179656 | tf_op jit(solution)/shard_map/ppermute | solution.py:37
  116.2 18.3 %collective-permute-start.25 = (bf16[2,4,64,384]{3,2,1,0:T(8,128)(2,1)}, bf16[2,4,64,384]{3,2,1,0:T(8,128)(2,1)}, u32[]{:S(2)}, u32[]{:S(2)}) collective-permute-start(bf16[2,4,64,384]{3,2,1,0:T(8,128)(2,1)} %collective-permute-done.13), channel_id=1, source_target_pairs={{8,0},{16,24},{40,32},{48,56},{9,1},{17,25},{41,33},{49,57},{10,2}... | collective-permute-start | bytes 1179656 | tf_op jit(solution)/shard_map/ppermute | solution.py:37
  118.6 24.3 %collective-permute-start.26 = (bf16[4,4,2,64,1536]{4,3,2,1,0:T(8,128)(2,1)}, bf16[4,4,2,64,1536]{4,3,2,1,0:T(8,128)(2,1)S(1)}, u32[]{:S(2)}, u32[]{:S(2)}) collective-permute-start(bf16[4,4,2,64,1536]{4,3,2,1,0:T(8,128)(2,1)} %bitcast.189), channel_id=1, source_target_pairs={{0,1},{1,0},{2,3},{3,2},{4,5},{5,4},{6,7},{7,6},{8,9},{9,8},{10,11... | collective-permute-start | bytes 18874376 | tf_op jit(solution)/shard_map/ppermute | solution.py:27
  122.4 25.5 %collective-permute-start.23 = (f16[128,3200]{0,1:T(8,128)(2,1)S(1)}, f16[128,3200]{0,1:T(8,128)(2,1)S(1)}, u32[]{:S(2)}, u32[]{:S(2)}) collective-permute-start(f16[128,3200]{0,1:T(8,128)(2,1)S(1)} %pad_maximum_fusion.3), channel_id=1, source_target_pairs={{0,8},{8,16},{16,24},{24,32},{32,40},{40,48},{48,56},{56,0},{1,9},... | collective-permute-start | bytes 2457608 | tf_op jit(solution)/shard_map/ppermute | solution.py:32
  134.2 21.0 %collective-permute-start.24 = (f16[128,3200]{0,1:T(8,128)(2,1)S(1)}, f16[128,3200]{0,1:T(8,128)(2,1)S(1)}, u32[]{:S(2)}, u32[]{:S(2)}) collective-permute-start(f16[128,3200]{0,1:T(8,128)(2,1)S(1)} %pad_maximum_fusion.4), channel_id=1, source_target_pairs={{0,56},{8,0},{16,8},{24,16},{32,24},{40,32},{48,40},{56,48},{1,57}... | collective-permute-start | bytes 2457608 | tf_op jit(solution)/shard_map/ppermute | solution.py:32
  (25 other events, 148.5 us)
Sparse Core Ops, SparseCore 0:
  33.6 70.1 all-gather.2
